TPU v7x, 32 devices: a whole 2x2x4 slice. The times are simulated.
32 devices in a mesh: gx: 4 (over x, core), gy: 8 (over z, y).
Axes of the slice: x: 2, y: 2, z: 4, core: 2. Of those that a mesh axis runs over, the one named last changes fastest.
Arguments:
- off_state: float32 [5, 128, 128, 256], P(None, 'gx', 'gy'), may hold values from -0.9 to 3, as said below
- near_state: float32 [96, 5, 8, 64, 128], P(('gx', 'gy')), may hold values from -0.9 to 3, as said below
- near_metric: float32 [96, 3, 8, 64, 128], P(('gx', 'gy')), may hold values from 0.5 to 1.1
- slot_block: int32 [96], P(('gx', 'gy')), may hold values from -1 to 63, as said below
- block_faces: int32 [64, 2], replicated, may hold values from 0 to 63, as said below
- fringe_in: int32 [3, 256], P(None, ('gx', 'gy')), may hold values from 0 to 23, as said below
- fringe_in_maps: bfloat16 [256, 128, 128], P(('gx', 'gy')), may hold values from 0 to 1
- fringe_out: int32 [3, 256], P(None, ('gx', 'gy')), may hold values from 0 to 23, as said below
- fringe_out_maps: bfloat16 [256, 128, 128], P(('gx', 'gy')), may hold values from 0 to 1
Outputs:
- off_next: float32 [5, 128, 128, 256], P(None, 'gx', 'gy')
- near_next: float32 [96, 5, 8, 64, 128], P(('gx', 'gy'))
Inputs may be any that keep to these rules, and one draw needn't show every extreme that they name: `off_state`: component 0 (density) lies within 0.8 to 1.2, components 1 to 3 within -0.9 to 0.9, component 4 within 2 to 3. `near_state`: component 0 (density) lies within 0.8 to 1.2, components 1 to 3 within -0.9 to 0.9, component 4 within 2 to 3, in empty slots too. `slot_block`: entry 3 * d + s is the block in slot s of device d (devices in gx+gy order). A device's occupied slots come first and it holds at least one block; every block is in exactly one slot; the blocks of gx row r are numbered from r * 2 * 8 and held in that row; the devices at gy and gy + 4 of one row hold 4 blocks together. `block_faces`: row b gives the block across b's lower and upper face around the body; they agree (b is the lower neighbour of its upper neighbour) and lie in b's gx row. `fringe_in`: column 8 * d + k is row k of device d: entry 0 a near-body tile of d in an occupied slot, entry 1 the gy index of the receiving device in d's gx row, entry 2 one of its off-body tiles. Every off-body tile is replaced at most once; every device receives exactly 8 rows, and sends exactly 1 row to each of 8 devices. `fringe_out`: column 8 * d + k is row k of device d: entry 0 an off-body tile of d, entry 1 the gy index of the receiving device in d's gx row, entry 2 a near-body tile of that device in an occupied slot. Every near-body tile is replaced at most once; every device receives exactly 8 rows, and sends exactly 1 row to each of 8 devices.
All inputs are finite; a program needn't handle non-finite values.
Results may differ from a plain program's by a relative error of at most 0.0014.
The roundings to bfloat16 on the way count: a program that leaves them out, or rounds other values in their place, can miss the bound.
Values may be sent and summed in bfloat16 or wider, within the bound.
No kernel may reach another device: no remote copies, remote signals or barrier semaphores. Data moves between devices by JAX's collectives and lax.ppermute only.
A program may use at most 384 MiB of HBM per device.

v0:
```python
import jax
import jax.numpy as jnp
from jax import lax
from jax.sharding import PartitionSpec as P

TW = 8
TL = 128
BLK_DEV = 2
BCAP = 3


HEAT_RATIO = 1.4
VISCOSITY = 0.8
CONDUCTION = 1.12
TIME_STEP = 0.1
WALL_SIGN = (1.0, -1.0, -1.0, -1.0, 1.0)
QUIET_STATE = (1.0, 0.0, 0.0, 0.0, 2.5)


def extended(block, sides, width):
    for axis, dim in sides:
        count = lax.axis_size(axis)
        forward = [(i, i + 1) for i in range(count - 1)]
        forward.append((count - 1, 0))
        backward = [(target, source) for source, target in forward]
        low = lax.ppermute(
            lax.slice_in_dim(block, block.shape[dim] - width, None, axis=dim), axis, forward
        )
        high = lax.ppermute(lax.slice_in_dim(block, 0, width, axis=dim), axis, backward)
        block = jnp.concatenate([low, block, high], axis=dim)
    return block


def as_sent(shard):

    def short(part):
        return part.astype(jnp.bfloat16) if part.dtype == jnp.float32 else part

    return jax.tree.map(short, shard)


def partner(value, axis, apart):
    mask = 2**apart
    pairs = [(source, source ^ mask) for source in range(lax.axis_size(axis))]
    return lax.ppermute(value, axis, pairs)


def shifted(values, direction, offset):
    leading = values.ndim - 3
    selector = [slice(None)] * leading
    for spatial in range(3):
        extent = values.shape[leading + spatial]
        if spatial == direction:
            selector.append(slice(1 + offset, extent - 1 + offset))
        else:
            selector.append(slice(1, extent - 1))
    return values[tuple(selector)]


def member(values, number):
    return values[..., number, :, :, :]


def residual(padded, metric):
    density = member(padded, 0)
    reciprocal_mass_per_volume = 1.0 / density
    fluid_speed_vector = [
        member(padded, 1 + direction) * reciprocal_mass_per_volume for direction in range(3)
    ]
    motion_work_share = 0.5 * (
        fluid_speed_vector[0] * fluid_speed_vector[0]
        + fluid_speed_vector[1] * fluid_speed_vector[1]
        + fluid_speed_vector[2] * fluid_speed_vector[2]
    )
    energy = member(padded, 4)
    normal_stress_level = (HEAT_RATIO - 1.0) * (energy - density * motion_work_share)
    thermal_level = normal_stress_level * reciprocal_mass_per_volume
    viscous_contribution = jnp.stack(
        [
            fluid_speed_vector[0],
            fluid_speed_vector[1],
            fluid_speed_vector[2],
            motion_work_share,
            thermal_level,
        ],
        axis=-4,
    )
    middle = shifted(viscous_contribution, 0, 0)
    summed = None
    for direction in range(3):
        momentum = member(padded, 1 + direction)
        pieces = [
            momentum,
            momentum * fluid_speed_vector[0],
            momentum * fluid_speed_vector[1],
            momentum * fluid_speed_vector[2],
            (energy + normal_stress_level) * fluid_speed_vector[direction],
        ]
        pieces[1 + direction] = pieces[1 + direction] + normal_stress_level
        fluxes = jnp.stack(pieces, axis=-4)
        difference = shifted(fluxes, direction, 1) - shifted(fluxes, direction, -1)
        second = (
            shifted(viscous_contribution, direction, 1)
            + shifted(viscous_contribution, direction, -1)
            - 2.0 * middle
        )
        viscous = jnp.stack(
            [
                jnp.zeros_like(member(second, 0)),
                VISCOSITY * member(second, 0),
                VISCOSITY * member(second, 1),
                VISCOSITY * member(second, 2),
                VISCOSITY * member(second, 3) + CONDUCTION * member(second, 4),
            ],
            axis=-4,
        )
        if metric is None:
            contrib = viscous - 0.5 * difference
        else:
            spacing = jnp.expand_dims(member(metric, direction), -4)
            contrib = spacing * spacing * viscous - 0.5 * spacing * difference
        summed = contrib if summed is None else summed + contrib
    return summed


def runge_kutta(initial, rate_of):
    section_one = initial + TIME_STEP * rate_of(initial)
    section_two = 0.75 * initial + 0.25 * (section_one + TIME_STEP * rate_of(section_one))
    return 1.0 / 3.0 * initial + 2.0 / 3.0 * (section_two + TIME_STEP * rate_of(section_two))


def frame_near(current, ghost_low, upper_ghost_cells):
    joined = jnp.concatenate([ghost_low, current, upper_ghost_cells], axis=3)
    wall_sign = jnp.array(WALL_SIGN, jnp.float32).reshape(5, 1, 1, 1)
    joined = jnp.concatenate([joined[:, :, 0:1] * wall_sign, joined, joined[:, :, -1:]], axis=2)
    return jnp.concatenate([joined[..., 0:1], joined, joined[..., -1:]], axis=4)


def off_tiles(fields):
    components, width_x, width_y, width_z = fields.shape
    blocks = fields.reshape(components, width_x // TW, TW, width_y // TW, TW, width_z // TL, TL)
    return blocks.transpose(1, 3, 5, 0, 2, 4, 6).reshape(-1, components * TW * TW * TL)


def off_fields(tiles, layout):
    components, width_x, width_y, width_z = layout
    blocks = tiles.reshape(width_x // TW, width_y // TW, width_z // TL, components, TW, TW, TL)
    return blocks.transpose(3, 0, 4, 1, 5, 2, 6).reshape(layout)


def near_tiles(fields):
    slots_here, components, normal, around, span_cells = fields.shape
    blocks = fields.reshape(slots_here, components, normal, around // TW, TW, span_cells)
    return blocks.transpose(0, 3, 1, 2, 4, 5).reshape(slots_here * (around // TW), -1)


def near_fields(tiles, layout):
    slots_here, components, normal, around, span_cells = layout
    blocks = tiles.reshape(slots_here, around // TW, components, normal, TW, span_cells)
    return blocks.transpose(0, 2, 3, 1, 4, 5).reshape(layout)


def off_hold(marks, layout):
    components, width_x, width_y, width_z = layout
    tile_grid = marks.reshape(width_x // TW, 1, width_y // TW, 1, width_z // TL, 1)
    spread = jnp.broadcast_to(tile_grid, (width_x // TW, TW, width_y // TW, TW, width_z // TL, TL))
    return 1.0 - spread.reshape(width_x, width_y, width_z)


def interpolate(tiles, chosen, tile_maps):
    donors = jnp.take(tiles, chosen, axis=0).astype(jnp.bfloat16)
    tile_lines = donors.reshape(donors.shape[0], -1, tile_maps.shape[-1])
    mixed_rows = jnp.einsum(
        "rkl,rlm->rkm", tile_lines, tile_maps, preferred_element_type=jnp.float32
    )
    return mixed_rows.astype(jnp.bfloat16).reshape(donors.shape[0], -1)


def neighbours(block_ids, block_faces):
    catalogue = jnp.arange(block_faces.shape[0])
    matches = block_ids[:, None] == catalogue[None, :]
    lower_ids = jnp.sum(jnp.where(matches, block_faces[None, :, 0], 0), axis=1)
    upper_ids = jnp.sum(jnp.where(matches, block_faces[None, :, 1], 0), axis=1)
    present = block_ids >= 0
    return (jnp.where(present, lower_ids, -1), jnp.where(present, upper_ids, -1))


def off_rate(fields, hold_mask):
    framed = extended(fields.astype(jnp.bfloat16), (("gx", 1), ("gy", 2)), 1).astype(fields.dtype)
    framed = jnp.concatenate([framed[..., -1:], framed, framed[..., :1]], axis=-1)
    return residual(framed, None) * hold_mask


def near_rate(fields, metric, hold_mask, block_ids, lower_ids, upper_ids):
    slots_here = fields.shape[0]
    face_cells = fields.shape[1] * fields.shape[2] * fields.shape[4]
    face_rows = jnp.concatenate([fields[:, :, :, 0, :], fields[:, :, :, -1, :]], axis=1)
    face_rows = face_rows.reshape(slots_here, 2 * face_cells)
    zeros_init = jnp.zeros((slots_here, face_cells), jnp.float32)
    portion_faces = lax.all_gather(as_sent(face_rows), "gy", axis=0, tiled=True)
    portion_ids = lax.all_gather(as_sent(block_ids), "gy", axis=0, tiled=True)
    from_lower = (portion_ids[None, :] == lower_ids[:, None]).astype(jnp.float32)
    from_upper = (portion_ids[None, :] == upper_ids[:, None]).astype(jnp.float32)
    ghost_low = zeros_init + jnp.dot(
        from_lower, portion_faces[:, face_cells:], precision=lax.Precision.HIGHEST
    )
    upper_ghost_cells = zeros_init + jnp.dot(
        from_upper, portion_faces[:, :face_cells], precision=lax.Precision.HIGHEST
    )
    ghost_low, upper_ghost_cells = (ghost_low, upper_ghost_cells)
    face_shape = (slots_here, fields.shape[1], fields.shape[2], 1, fields.shape[4])
    framed = frame_near(
        fields, ghost_low.reshape(face_shape), upper_ghost_cells.reshape(face_shape)
    )
    return residual(framed, metric) * hold_mask


def local(
    off_state,
    near_state,
    near_metric,
    slot_block,
    block_faces,
    fringe_in,
    fringe_in_maps,
    fringe_out,
    fringe_out_maps,
):
    occupied = slot_block >= 0
    quiet_state = jnp.array(QUIET_STATE, jnp.float32).reshape(1, 5, 1, 1, 1)
    near_filled = jnp.where(occupied[:, None, None, None, None], near_state, quiet_state)
    tiles_off = off_tiles(off_state)
    tiles_near = near_tiles(near_filled)
    count_off = tiles_off.shape[0]
    count_near = tiles_near.shape[0]
    sent_in = interpolate(tiles_near, fringe_in[0], fringe_in_maps)
    sent_out = interpolate(tiles_off, fringe_out[0], fringe_out_maps)
    own_column = lax.axis_index("gy")
    values_in = lax.all_gather(sent_in, "gy", axis=0, tiled=True)
    column_in = lax.all_gather(fringe_in[1], "gy", axis=0, tiled=True)
    tile_in = lax.all_gather(fringe_in[2], "gy", axis=0, tiled=True)
    values_out = lax.all_gather(sent_out, "gy", axis=0, tiled=True)
    column_out = lax.all_gather(fringe_out[1], "gy", axis=0, tiled=True)
    tile_out = lax.all_gather(fringe_out[2], "gy", axis=0, tiled=True)
    hits_off = (column_in[None, :] == own_column) & (
        tile_in[None, :] == jnp.arange(count_off)[:, None]
    )
    hits_near = (column_out[None, :] == own_column) & (
        tile_out[None, :] == jnp.arange(count_near)[:, None]
    )
    into_off = jnp.dot(hits_off.astype(jnp.bfloat16), values_in, preferred_element_type=jnp.float32)
    into_near = jnp.dot(
        hits_near.astype(jnp.bfloat16), values_out, preferred_element_type=jnp.float32
    )
    marks_off = jnp.sum(hits_off.astype(jnp.float32), axis=1)
    marks_near = jnp.sum(hits_near.astype(jnp.float32), axis=1)
    got_off, marks_off, got_near, marks_near = (into_off, marks_off, into_near, marks_near)
    tiles_off = jnp.where(marks_off[:, None] > 0.0, got_off, tiles_off)
    tiles_near = jnp.where(marks_near[:, None] > 0.0, got_near, tiles_near)
    off_start = off_fields(tiles_off, off_state.shape)
    hold_off = off_hold(marks_off, off_state.shape)
    off_next = runge_kutta(off_start, lambda fields: off_rate(fields, hold_off))
    near_start = near_fields(tiles_near, near_filled.shape)
    tile_hold = marks_near.reshape(near_filled.shape[0], -1)
    spare_slots = BCAP - BLK_DEV
    load_here = jnp.sum(occupied.astype(jnp.int32))
    partner_bit = lax.axis_size("gy").bit_length() - 2
    partner_parcel = partner(
        (near_start[BLK_DEV:], near_metric[BLK_DEV:], tile_hold[BLK_DEV:], slot_block[BLK_DEV:]),
        "gy",
        partner_bit,
    )
    work_seats = jnp.arange(BLK_DEV)
    keep_own = work_seats < load_here
    borrowed = jnp.clip(work_seats - load_here, 0, spare_slots - 1)

    def settle_work(own_part, partner_part):
        borrowed_rows = jnp.take(partner_part, borrowed, axis=0)
        keep_shape = keep_own.reshape((-1,) + (1,) * (own_part.ndim - 1))
        return jnp.where(keep_shape, own_part[:BLK_DEV], borrowed_rows)

    work_fields = settle_work(near_start, partner_parcel[0])
    work_metric = settle_work(near_metric, partner_parcel[1])
    work_hold = settle_work(tile_hold, partner_parcel[2])
    work_ids = settle_work(slot_block, partner_parcel[3])
    lower_ids, upper_ids = neighbours(work_ids, block_faces)
    hold_near = 1.0 - jnp.repeat(work_hold, TW, axis=1)[:, None, None, :, None]
    result = runge_kutta(
        work_fields,
        lambda fields: near_rate(fields, work_metric, hold_near, work_ids, lower_ids, upper_ids),
    )
    outward = jnp.clip(load_here + jnp.arange(spare_slots), 0, BLK_DEV - 1)
    returned = partner(jnp.take(result, outward, axis=0), "gy", partner_bit)
    merged = jnp.concatenate([result, returned], axis=0)
    near_next = jnp.where(occupied[:, None, None, None, None], merged, 0.0)
    return (off_next, near_next)


def solution(mesh):
    in_specs = (
        P(None, "gx", "gy", None),
        P(("gx", "gy"), None, None, None, None),
        P(("gx", "gy"), None, None, None, None),
        P(("gx", "gy")),
        P(),
        P(None, ("gx", "gy")),
        P(("gx", "gy"), None, None),
        P(None, ("gx", "gy")),
        P(("gx", "gy"), None, None),
    )
    out_specs = (P(None, "gx", "gy", None), P(("gx", "gy"), None, None, None, None))
    return jax.shard_map(local, mesh=mesh, in_specs=in_specs, out_specs=out_specs, check_vma=False)
```

profile of v0, /device:TPU:0, one launch (start us, length us, event | category | flops | bytes accessed | tf_op | source)
XLA Modules:
  0.0 904.6 jit_solution(5485323822727170869)
XLA Ops:
  9.3 4.4 copy_select_fusion
  13.7 4.2 copy.67
  17.9 3.6 gather_fusion
  23.9 4.0 collective-permute-start.14
  58.1 30.5 %all-reduce.5 = (s32[64]{0:T(128)S(1)}, s32[64]{0:T(128)S(1)}, s32[64]{0:T(128)S(1)}, s32[64]{0:T(128)S(1)}, s32[16]{0:T(128)S(1)}) all-reduce(s32[64]{0:T(128)S(1)} %bitcast_dynamic-update-slice_fusion.2, s32[64]{0:T(128)S(1)} %bitcast_dynamic-update-slice_fusion.3, ...), channel_id=3, replica_groups=mesh['gx'=4,'gy'=8] {'gy'}, use_global_device_ids=true, to_apply=%add.1 | all-reduce | flops 272 | bytes 2176
  89.3 4.3 collective-permute-done.15
  93.8 41.5 %all-gather.10.cloned.1.call-done = bf16[64,40960]{1,0:T(8,128)(2,1)} async-done(((bf16[8,40960]{1,0:T(8,128)(2,1)}), bf16[64,40960]{1,0:T(8,128)(2,1)}) %all-gather.10.cloned.1.call-update) | async-done | bytes 5242896 | tf_op jit(solution)/shard_map/all_gather | solution.py:239
  135.3 3.3 fusion.92
  149.5 4.2 collective-permute-done.3
  172.2 6.5 fusion.91
  194.2 13.8 %fusion.236 = (bf16[5,32,16,256]{3,1,2,0:T(8,128)(2,1)S(1)}, f32[5,32,16,256]{3,1,2,0:T(8,128)}) fusion(f32[5,32,16,256]{3,1,2,0:T(8,128)S(1)} %bitcast.154, f32[32,16,256]{2,0,1:T(8,128)S(1)} %bitcast.165, f32[5,32,16,256]{3,1,2,0:T(8,128)} %fusion.179, f32[5,34,18,258]{3,1,2,0:T(8,128)} %copy-done.60, f32[5,32,16,256]{3,1,2,0:T(8,128)} %fusion.184, ...), kind=kLoop, calls=%fused_computation.653 | loop fusion | flops 9830400 | bytes 30670848 | tf_op jit(solution)/shard_map/convert_element_type | solution.py:189
  219.0 7.4 all-gather.12.cloned.1.call-done
  226.4 4.5 convolution_select_fusion
  230.9 2.9 copy.117
  250.8 6.6 fusion.77
  272.8 14.7 %fusion.234 = (bf16[5,32,16,256]{3,1,2,0:T(8,128)(2,1)S(1)}, f32[5,32,16,256]{3,1,2,0:T(8,128)}) fusion(f32[5,32,16,256]{3,1,2,0:T(8,128)S(1)} %copy-done.32, f32[32,16,256]{2,0,1:T(8,128)S(1)} %bitcast.166, f32[5,32,16,256]{3,1,2,0:T(8,128)} %fusion.164, f32[5,34,18,258]{3,1,2,0:T(8,128)} %copy-done.57, f32[5,32,16,256]{3,1,2,0:T(8,128)} %fusion.169, ...), kind=kLoop, calls=%fused_computation.652 | loop fusion | flops 11796480 | bytes 33292288 | tf_op jit(solution)/shard_map/convert_element_type | solution.py:189
  297.4 4.8 collective-permute-done.10
  318.2 6.4 fusion.61
  340.2 13.7 %collective-permute-done.12 = f32[1,5,8,64,128]{4,3,2,1,0:T(8,128)} collective-permute-done((f32[1,5,8,64,128]{4,3,2,1,0:T(8,128)S(1)}, f32[1,5,8,64,128]{4,3,2,1,0:T(8,128)}, u32[]{:S(2)}, u32[]{:S(2)}) %collective-permute-start.12) | collective-permute-done | bytes 1310752 | tf_op jit(solution)/shard_map/ppermute | solution.py:45
  357.7 38.0 %all-gather.4 = bf16[8,2,10240]{2,1,0:T(2,128)(2,1)S(1)} all-gather(bf16[1,2,10240]{2,1,0:T(2,128)(2,1)S(1)} %reshape.337), channel_id=1, replica_groups=mesh['gx'=4,'gy'=8] {'gy'}, dimensions={0}, use_global_device_ids=true | all-gather | bytes 368640 | tf_op jit(solution)/shard_map/all_gather | solution.py:200
  398.1 5.8 fusion.241
  403.8 13.5 %pad_maximum_fusion = f32[2,5,10,66,130]{4,2,1,0,3:T(8,128)S(1)} fusion(f32[2,5,10,66,1]{4,2,1,0,3:T(8,128)} %get-tuple-element.190, f32[2,5,1,66,128]{4,2,1,0,3:T(1,128)S(1)} %get-tuple-element.202, f32[2,5,8,1,128]{4,2,1,0,3:T(8,128)S(1)} %bitcast.175, f32[2,5,8,64,128]{4,2,1,0,3:T(8,128)S(1)} %get-tuple-element.55, f32[2,5,8,1,128]{4,2,1,0,3:T(8,128)S(1)} %bitcast.187, ...), kind=kLoop, calls=%fused_computation.4 | loop fusion | flops 5148000 | bytes 6864000 | tf_op jit(solution)/shard_map/concatenate | solution.py:136
  417.4 3.1 constant_dynamic-update-slice_fusion.24
  420.4 2.9 constant_dynamic-update-slice_fusion.23
  423.3 5.7 slice_dynamic-update-slice_fusion.8
  429.1 4.6 constant_dynamic-update-slice_fusion.21
  433.7 3.4 multiply_dynamic-update-slice_fusion.29
  437.1 24.9 %fusion.45 = (f32[2,5,8,64,128]{4,2,1,0,3:T(8,128)}, f32[2,5,8,64,128]{4,2,1,0,3:T(8,128)}, f32[2,5,8,64,128]{4,2,1,0,3:T(8,128)}) fusion(f32[2,5,10,66,130]{4,2,1,0,3:T(8,128)} %get-tuple-element.46), kind=kLoop, calls=%fused_computation.82 | loop fusion | flops 4587520 | bytes 26214400 | tf_op jit(solution)/shard_map/sub | solution.py:103
  470.4 7.5 add_dynamic-update-slice_fusion.8
  477.9 2.9 multiply_dynamic-update-slice_fusion.28
  480.8 6.6 multiply_dynamic-update-slice_fusion.27
  487.5 7.5 multiply_dynamic-update-slice_fusion.26
  502.4 22.6 %fusion.231 = (bf16[2,5,8,64,128]{4,2,1,0,3:T(8,128)(2,1)}, f32[2,5,8,64,128]{4,2,1,0,3:T(8,128)}) fusion(f32[2,5,8,64,128]{4,2,1,0,3:T(8,128)S(1)} %get-tuple-element.55, f32[2,64]{0,1:T(8,128)S(1)} %copy-done.85, f32[2,5,10,66,130]{4,2,1,0,3:T(8,128)} %get-tuple-element.100, f32[2,8,64,128]{3,1,0,2:T(8,128)S(1)} %copy-done.44, ...), kind=kLoop, calls=%fused_computation.650 | loop fusion | flops 11796480 | bytes 33292800 | tf_op jit(solution)/shard_map/convert.11
  525.9 32.9 %all-gather.5 = bf16[8,2,10240]{2,1,0:T(2,128)(2,1)} all-gather(bf16[1,2,10240]{2,1,0:T(2,128)(2,1)S(1)} %reshape.339), channel_id=1, replica_groups=mesh['gx'=4,'gy'=8] {'gy'}, dimensions={0}, use_global_device_ids=true | all-gather | bytes 368640 | tf_op jit(solution)/shard_map/all_gather | solution.py:200
  563.0 3.0 maximum_multiply_fusion.1
  567.7 5.8 fusion.240
  573.4 13.5 %pad_maximum_fusion.1 = f32[2,5,10,66,130]{4,2,1,0,3:T(8,128)S(1)} fusion(f32[2,5,10,66,1]{4,2,1,0,3:T(8,128)} %get-tuple-element.188, f32[2,5,1,66,128]{4,2,1,0,3:T(1,128)S(1)} %get-tuple-element.200, f32[2,5,8,1,128]{4,2,1,0,3:T(8,128)S(1)} %bitcast.181, f32[2,5,8,64,128]{4,2,1,0,3:T(8,128)S(1)} %copy-done.6, f32[2,5,8,1,128]{4,2,1,0,3:T(8,128)S(1)} %bitcast.190, ...), kind=kLoop, calls=%fused_computation.5 | loop fusion | flops 5148000 | bytes 6864000 | tf_op jit(solution)/shard_map/concatenate | solution.py:136
  587.0 3.0 constant_dynamic-update-slice_fusion.31
  590.0 2.9 constant_dynamic-update-slice_fusion.30
  592.9 5.8 slice_dynamic-update-slice_fusion.5
  598.6 4.6 constant_dynamic-update-slice_fusion.28
  603.3 3.4 multiply_dynamic-update-slice_fusion.19
  606.7 25.0 %fusion.31 = (f32[2,5,8,64,128]{4,2,1,0,3:T(8,128)}, f32[2,5,8,64,128]{4,2,1,0,3:T(8,128)}, f32[2,5,8,64,128]{4,2,1,0,3:T(8,128)}) fusion(f32[2,5,10,66,130]{4,2,1,0,3:T(8,128)} %get-tuple-element.36), kind=kLoop, calls=%fused_computation.61 | loop fusion | flops 4587520 | bytes 26214400 | tf_op jit(solution)/shard_map/sub | solution.py:103
  640.0 7.5 add_dynamic-update-slice_fusion.5
  647.5 2.9 multiply_dynamic-update-slice_fusion.18
  650.5 6.6 multiply_dynamic-update-slice_fusion.17
  657.1 7.5 multiply_dynamic-update-slice_fusion.16
  672.0 23.7 %fusion.229 = (bf16[2,5,8,64,128]{4,2,1,0,3:T(8,128)(2,1)}, f32[2,5,8,64,128]{4,2,1,0,3:T(8,128)}) fusion(f32[2,5,8,64,128]{4,2,1,0,3:T(8,128)} %get-tuple-element.45, f32[2,64]{0,1:T(8,128)S(1)} %copy-done.85, f32[2,5,10,66,130]{4,2,1,0,3:T(8,128)} %get-tuple-element.89, f32[2,8,64,128]{3,1,0,2:T(8,128)S(1)} %copy-done.44, ...), kind=kLoop, calls=%fused_computation.649 | loop fusion | flops 13762560 | bytes 35914240 | tf_op jit(solution)/shard_map/convert.5
  696.5 32.9 %all-gather.6 = bf16[8,2,10240]{2,1,0:T(2,128)(2,1)} all-gather(bf16[1,2,10240]{2,1,0:T(2,128)(2,1)S(1)} %reshape.341), channel_id=1, replica_groups=mesh['gx'=4,'gy'=8] {'gy'}, dimensions={0}, use_global_device_ids=true | all-gather | bytes 368640 | tf_op jit(solution)/shard_map/all_gather | solution.py:200
  733.6 3.0 maximum_multiply_fusion
  737.9 5.8 fusion.239
  743.7 13.7 %pad_maximum_fusion.2 = f32[2,5,10,66,130]{4,2,1,0,3:T(8,128)S(1)} fusion(f32[2,5,10,66,1]{4,2,1,0,3:T(8,128)} %get-tuple-element.186, f32[2,5,1,66,128]{4,2,1,0,3:T(1,128)S(1)} %get-tuple-element.198, f32[2,5,8,1,128]{4,2,1,0,3:T(8,128)S(1)} %bitcast.178, f32[2,5,8,64,128]{4,2,1,0,3:T(8,128)S(1)} %copy-done.4, f32[2,5,8,1,128]{4,2,1,0,3:T(8,128)S(1)} %bitcast.184, ...), kind=kLoop, calls=%fused_computation.6 | loop fusion | flops 5148000 | bytes 6864000 | tf_op jit(solution)/shard_map/concatenate | solution.py:136
  762.3 5.8 slice_dynamic-update-slice_fusion.2
  768.1 4.7 constant_dynamic-update-slice_fusion.35
  772.8 2.8 multiply_dynamic-update-slice_fusion.9
  775.6 6.5 add_dynamic-update-slice_fusion.2
  782.1 2.9 multiply_dynamic-update-slice_fusion.8
  785.0 6.6 multiply_dynamic-update-slice_fusion.7
  791.6 7.5 multiply_dynamic-update-slice_fusion.6
  801.4 24.5 %fusion.15 = (f32[2,5,8,64,128]{4,2,1,0,3:T(8,128)}, f32[2,5,8,64,128]{4,2,1,0,3:T(8,128)}, f32[2,5,8,64,128]{4,2,1,0,3:T(8,128)S(1)}) fusion(f32[2,5,10,66,130]{4,2,1,0,3:T(8,128)} %get-tuple-element.26), kind=kLoop, calls=%fused_computation.38 | loop fusion | flops 4587520 | bytes 26214400 | tf_op jit(solution)/shard_map/sub | solution.py:103
  838.4 22.5 %fusion.7 = f32[2,5,8,64,128]{4,2,1,0,3:T(8,128)} fusion(f32[2,5,8,64,128]{4,2,1,0,3:T(8,128)S(1)} %copy-done.5, f32[2,5,10,66,130]{4,2,1,0,3:T(8,128)} %get-tuple-element.78, f32[2,5,10,66,130]{4,2,1,0,3:T(8,128)} %multiply_dynamic-update-slice_fusion.3, f32[2,5,10,66,130]{4,2,1,0,3:T(8,128)} %get-tuple-element.77, f32[2,5,8,64,128]{4,2,1,0,3:T(8,128)} %fusion.104, ...), kind=kLoop, calls=%fused_computation.24 | loop fusion | flops 13107200 | bytes 34603520 | tf_op jit(solution)/shard_map/add | solution.py:129
  864.7 14.1 %fusion.53 = f32[5,32,16,256]{3,1,2,0:T(8,128)S(1)} fusion(f32[5,32,16,256]{3,1,2,0:T(8,128)} %get-tuple-element.62, f32[5,32,16,256]{3,1,2,0:T(8,128)} %fusion.149, f32[5,34,18,258]{3,1,2,0:T(8,128)} %copy-done.62, f32[5,32,16,256]{3,1,2,0:T(8,128)} %fusion.154, f32[5,34,18,258]{3,1,2,0:T(8,128)} %multiply_dynamic-update-slice_fusion.33, ...), kind=kLoop, calls=%fused_computation.92 | loop fusion | flops 11141120 | bytes 31981568 | tf_op jit(solution)/shard_map/add | solution.py:129
  878.8 3.0 copy.83
  881.7 12.6 %collective-permute-done.16 = f32[1,5,8,64,128]{4,2,1,0,3:T(8,128)S(1)} collective-permute-done((f32[1,5,8,64,128]{4,2,1,0,3:T(8,128)S(1)}, f32[1,5,8,64,128]{4,2,1,0,3:T(8,128)S(1)}, u32[]{:S(2)}, u32[]{:S(2)}) %collective-permute-start.16) | collective-permute-done | bytes 1310752 | tf_op jit(solution)/shard_map/ppermute | solution.py:45
  (462 shorter events, 239.4 us)
Async XLA Ops:
  7.2 14.4 %copy-start = (bf16[8,128,128]{2,1,0:T(8,128)(2,1)S(1)}, bf16[8,128,128]{2,1,0:T(8,128)(2,1)}, u32[]{:S(2)}) copy-start(bf16[8,128,128]{2,1,0:T(8,128)(2,1)} %param.19) | copy-start | bytes 786436
  7.2 128.1 %all-gather.10.cloned.1.call-start = ((), (), s32[]{:S(2)}) async-start(), calls=%async_computation | async-start | bytes 5898240 | tf_op jit(solution)/shard_map/all_gather | solution.py:239
  21.6 8.5 copy-start.83
  23.3 203.1 %all-gather.12.cloned.1.call-start = ((), (), s32[]{:S(2)}) async-start(), calls=%async_computation.1 | async-start | bytes 5898240 | tf_op jit(solution)/shard_map/all_gather | solution.py:242
  23.9 32.8 %collective-permute-start.14 = (s32[1]{0:T(128)}, s32[1]{0:T(128)}, u32[]{:S(2)}, u32[]{:S(2)}) collective-permute-start(s32[1]{0:T(128)} %slice.958), channel_id=1, source_target_pairs={{0,4},{1,5},{2,6},{3,7},{4,0},{5,1},{6,2},{7,3},{8,12},{9,13},{10,... | collective-permute-start | bytes 20 | tf_op jit(solution)/shard_map/ppermute | solution.py:45
  30.1 116.8 %collective-permute-start.13 = (f32[1,3,8,64,128]{4,3,2,1,0:T(8,128)}, f32[1,3,8,64,128]{4,3,2,1,0:T(8,128)}, u32[]{:S(2)}, u32[]{:S(2)}) collective-permute-start(f32[1,3,8,64,128]{4,3,2,1,0:T(8,128)} %slice.955), channel_id=1, source_target_pairs={{0,4},{1,5},{2,6},{3,7},{4,0},{5,1},{6,2},{7,3},{8,12},{9,13},{10,... | collective-permute-start | bytes 2359304 | tf_op jit(solution)/shard_map/ppermute | solution.py:45
  44.3 8.8 copy-start.94
  44.3 10.1 %copy-start.92 = (s32[3,8]{1,0:T(4,128)S(1)}, s32[3,8]{1,0:T(4,128)}, u32[]{:S(2)}) copy-start(s32[3,8]{1,0:T(4,128)} %param.18) | copy-start | bytes 292
  44.3 11.8 %copy-start.89 = (s32[64,2]{0,1:T(2,128)S(1)}, s32[64,2]{0,1:T(2,128)}, u32[]{:S(2)}) copy-start(s32[64,2]{0,1:T(2,128)} %param.17) | copy-start | bytes 1540
  89.1 4.5 collective-permute-start.15
  139.6 133.2 %copy-start.7 = (f32[5,4,8,2,8,2,128]{6,2,5,1,4,3,0:T(8,128)}, f32[5,4,8,2,8,2,128]{6,2,5,1,4,3,0:T(8,128)S(1)}, u32[]{:S(2)}) copy-start(f32[5,4,8,2,8,2,128]{6,2,5,1,4,3,0:T(8,128)S(1)} %copy.70) | copy-start | bytes 7864324
  139.6 7.3 copy-start.84
  139.9 2.1 collective-permute-start.1
  140.0 4.7 collective-permute-start
  144.8 8.9 collective-permute-start.3
  146.5 9.7 %collective-permute-start.2 = (bf16[5,34,1,256]{3,1,2,0:T(8,128)(2,1)S(1)}, bf16[5,34,1,256]{3,1,2,0:T(8,128)(2,1)S(1)}, u32[]{:S(2)}, u32[]{:S(2)}) collective-permute-start(bf16[5,34,1,256]{3,1,2,0:T(8,128)(2,1)S(1)} %get-tuple-element.216), channel_id=1, source_target_pairs={{0,1},{1,2},{2,3},{3,4},{4,5},{5,6},{6,7},{7,0},{8,9},{9,10},{10,1... | collective-permute-start | bytes 261128 | tf_op jit(solution)/shard_map/ppermute | solution.py:26
  160.4 5.5 copy-start.23
  178.7 8.1 copy-start.40
  184.5 5.7 copy-start.80
  193.3 79.5 %copy-start.54 = (f32[4,8,2,8,2,128]{5,1,4,0,3,2:T(8,128)}, f32[4,8,2,8,2,128]{5,1,4,0,3,2:T(8,128)S(1)}, u32[]{:S(2)}) copy-start(f32[4,8,2,8,2,128]{5,1,4,0,3,2:T(8,128)S(1)} %broadcast_in_dim.191) | copy-start | bytes 1572868
  194.1 15.0 %copy-start.65 = (f32[2,3,8,64,128]{4,3,2,1,0:T(8,128)S(1)}, f32[2,3,8,64,128]{4,3,2,1,0:T(8,128)}, u32[]{:S(2)}) copy-start(f32[2,3,8,64,128]{4,3,2,1,0:T(8,128)} %select_select_fusion) | copy-start | bytes 4718596
  208.0 8.3 copy-start.29
  208.1 8.1 collective-permute-start.5
  208.5 7.7 collective-permute-start.4
  217.0 16.9 %collective-permute-start.7 = (bf16[5,34,1,256]{3,1,2,0:T(8,128)(2,1)}, bf16[5,34,1,256]{3,1,2,0:T(8,128)(2,1)}, u32[]{:S(2)}, u32[]{:S(2)}) collective-permute-start(bf16[5,34,1,256]{3,1,2,0:T(8,128)(2,1)} %get-tuple-element.215), channel_id=1, source_target_pairs={{1,0},{2,1},{3,2},{4,3},{5,4},{6,5},{7,6},{0,7},{9,8},{10,9},{11,1... | collective-permute-start | bytes 261128 | tf_op jit(solution)/shard_map/ppermute | solution.py:29
  217.8 16.0 %collective-permute-start.6 = (bf16[5,34,1,256]{3,1,2,0:T(8,128)(2,1)S(1)}, bf16[5,34,1,256]{3,1,2,0:T(8,128)(2,1)}, u32[]{:S(2)}, u32[]{:S(2)}) collective-permute-start(bf16[5,34,1,256]{3,1,2,0:T(8,128)(2,1)S(1)} %get-tuple-element.214), channel_id=1, source_target_pairs={{0,1},{1,2},{2,3},{3,4},{4,5},{5,6},{6,7},{7,0},{8,9},{9,10},{10,1... | collective-permute-start | bytes 261128 | tf_op jit(solution)/shard_map/ppermute | solution.py:26
  238.9 5.5 copy-start.25
  257.4 8.0 copy-start.41
  272.8 15.4 %copy-start.28 = (f32[3,8,5,8,8,128]{5,4,1,3,2,0:T(8,128)S(1)}, f32[3,8,5,8,8,128]{5,4,1,3,2,0:T(8,128)}, u32[]{:S(2)}) copy-start(f32[3,8,5,8,8,128]{5,4,1,3,2,0:T(8,128)} %copy.117) | copy-start | bytes 11796484
  287.6 2.3 collective-permute-start.9
  287.7 4.8 collective-permute-start.8
  292.5 4.9 collective-permute-start.11
  293.7 8.6 collective-permute-start.10
  294.7 59.2 %collective-permute-start.12 = (f32[1,5,8,64,128]{4,3,2,1,0:T(8,128)S(1)}, f32[1,5,8,64,128]{4,3,2,1,0:T(8,128)}, u32[]{:S(2)}, u32[]{:S(2)}) collective-permute-start(f32[1,5,8,64,128]{4,3,2,1,0:T(8,128)S(1)} %slice_bitcast_fusion.1), channel_id=1, source_target_pairs={{0,4},{1,5},{2,6},{3,7},{4,0},{5,1},{6,2},{7,3},{8,12},{9,13},{10,... | collective-permute-start | bytes 3932168 | tf_op jit(solution)/shard_map/ppermute | solution.py:45
  324.6 13.5 %copy-start.31 = (f32[5,32,16,256]{3,1,2,0:T(8,128)}, f32[5,32,16,256]{3,1,2,0:T(8,128)S(1)}, u32[]{:S(2)}) copy-start(f32[5,32,16,256]{3,1,2,0:T(8,128)S(1)} %get-tuple-element.167) | copy-start | bytes 7864324
  324.6 8.4 copy-start.42
  339.0 17.0 %copy-start.43 = (f32[2,5,8,64,128]{4,3,2,1,0:T(8,128)S(1)}, f32[2,5,8,64,128]{4,3,2,1,0:T(8,128)}, u32[]{:S(2)}) copy-start(f32[2,5,8,64,128]{4,3,2,1,0:T(8,128)} %slice_bitcast_fusion) | copy-start | bytes 7864324
  356.0 40.4 %copy-start.86 = (f32[5]{0:T(128)S(1)}, f32[5]{0:T(128)}, u32[]{:S(2)}) copy-start(f32[5]{0:T(128)} %constant.105.clone) | copy-start | bytes 64
  417.4 16.3 %copy-start.2 = (f32[2,5,10,66,130]{4,2,1,0,3:T(8,128)}, f32[2,5,10,66,130]{4,2,1,0,3:T(8,128)S(1)}, u32[]{:S(2)}) copy-start(f32[2,5,10,66,130]{4,2,1,0,3:T(8,128)S(1)} %pad_maximum_fusion) | copy-start | bytes 10296004
  429.1 4.6 copy-start.18
  462.1 8.3 copy-start.11
  462.1 8.3 copy-start.19
  466.1 11.8 %slice-start = ((s8[10813440]{0:T(1024)(128)(4,1)}), s8[4194304]{0:T(1024)(128)(4,1)S(1)}, s32[]{:S(2)}) async-start(s8[10813440]{0:T(1024)(128)(4,1)} %bitcast.149), calls=%async_computation.2 | async-start | bytes 8388608
  470.4 7.6 slice-start.1
  470.4 7.6 slice-start.2
  487.5 7.5 copy-start.12
  560.5 5.4 copy-start.6
  587.0 16.3 %copy-start.3 = (f32[2,5,10,66,130]{4,2,1,0,3:T(8,128)}, f32[2,5,10,66,130]{4,2,1,0,3:T(8,128)S(1)}, u32[]{:S(2)}) copy-start(f32[2,5,10,66,130]{4,2,1,0,3:T(8,128)S(1)} %pad_maximum_fusion.1) | copy-start | bytes 10296004
  598.6 4.6 copy-start.20
  631.7 8.3 copy-start.13
  631.7 8.3 copy-start.21
  635.7 11.8 %slice-start.3 = ((s8[10813440]{0:T(1024)(128)(4,1)}), s8[4194304]{0:T(1024)(128)(4,1)S(1)}, s32[]{:S(2)}) async-start(s8[10813440]{0:T(1024)(128)(4,1)} %bitcast.151), calls=%async_computation.5 | async-start | bytes 8388608
  640.0 7.6 slice-start.4
  640.0 7.6 slice-start.5
  657.1 7.5 copy-start.14
  731.2 5.4 copy-start.4
  768.1 4.7 copy-start.17
  768.1 4.7 copy-start.22
  775.6 6.5 copy-start.15
  791.6 7.5 copy-start.16
  825.8 8.1 copy-start.68
  862.5 31.9 %collective-permute-start.16 = (f32[1,5,8,64,128]{4,2,1,0,3:T(8,128)S(1)}, f32[1,5,8,64,128]{4,2,1,0,3:T(8,128)S(1)}, u32[]{:S(2)}, u32[]{:S(2)}) collective-permute-start(f32[1,5,8,64,128]{4,2,1,0,3:T(8,128)S(1)} %dynamic-slice_select_fusion), channel_id=1, source_target_pairs={{0,4},{1,5},{2,6},{3,7},{4,0},{5,1},{6,2},{7,3},{8,12},{9,13},{10,... | collective-permute-start | bytes 3932168 | tf_op jit(solution)/shard_map/ppermute | solution.py:45
  878.7 15.6 %copy-start.27 = (f32[2,5,8,64,128]{4,2,1,0,3:T(8,128)S(1)}, f32[2,5,8,64,128]{4,2,1,0,3:T(8,128)}, u32[]{:S(2)}) copy-start(f32[2,5,8,64,128]{4,2,1,0,3:T(8,128)} %fusion.7) | copy-start | bytes 7864324
  878.8 15.6 %copy-start.88 = (pred[3]{0:T(512)(128)(4,1)S(1)}, pred[3]{0:T(512)(128)(4,1)}, u32[]{:S(2)}) copy-start(pred[3]{0:T(512)(128)(4,1)} %copy-done.87) | copy-start | bytes 13
  (56 other events, 172.0 us)
Sparse Core Ops, SparseCore 0:
  23.4 111.8 all-gather.9
  137.5 88.8 all-gather.11
where the time goes:
time: 914 us; the launch traced here: 905 us
  other arithmetic  505 us (55%)
  blocking collectives  134 us (15%)
  local copies, waits for them, and re-layouts  121 us (13%)
  waiting for transfers between devices  98.5 us (11%)
  between operations  17.8 us (2%)
  starting transfers between devices  14.1 us (2%)
  matrix products  13.8 us (2%)
    unnamed x90, other arithmetic  158 us
    all_gather x3, blocking collectives, near_rate(): portion_faces = lax.all_gather(as_sent(face_rows), 'gy', axis=0, tiled=True)  104 us
    sub x6, other arithmetic, residual(): shifted(viscous_contribution, direction, 1)  93.8 us
    unnamed x254, local copies, waits for them, and re-layouts  69.6 us
    another operation x3, other arithmetic  48 us
    all_gather x1, waiting for transfers between devices, local(): values_in = lax.all_gather(sent_in, 'gy', axis=0, tiled=True)  41.5 us
    concatenate x3, other arithmetic, frame_near(): return jnp.concatenate([joined[..., 0:1], joined, joined[..., -1:]], axis=4)  40.8 us
    another operation x12, other arithmetic, residual(): fluxes = jnp.stack(pieces, axis=-4)  37.6 us
  transfers between devices with their start and end apart: 19, of which 12 were waited for; matrix products, arithmetic and copies ran while one was open for 16% of the time, Pallas kernels for 0%

commit v1 on v0

v1 whole, which is shorter than its diff:
```python
import functools

import jax
import jax.numpy as jnp
from jax import lax
from jax.experimental import pallas as pl
from jax.experimental.pallas import tpu as pltpu
from jax.sharding import PartitionSpec as P

TW = 8
TL = 128
DEPTH = 3
RING = 8
META = 16
FIELDS = 5
HEAT_RATIO = 1.4
VISCOSITY = 0.8
CONDUCTION = 1.12
TIME_STEP = 0.1
QUIET_STATE = (1.0, 0.0, 0.0, 0.0, 2.5)
CENTRE = (1.0, 0.0, 0.0, 0.0, 2.5, 0.0)
SECTIONS = ((0.0, 1.0), (0.75, 0.25), (1.0 / 3.0, 2.0 / 3.0))
FACE_LAYERS = FIELDS * DEPTH + 3 * (DEPTH - 1) + 1
FACE_ROWS = FACE_LAYERS * TW
LAG = 2
RINGS = 4
VMEM_MIB = 56
FRONT = 6

VMEM = pltpu.VMEM
SMEM = pltpu.SMEM


def vmem_spec():
    return pl.BlockSpec(memory_space=VMEM)


def smem_spec():
    return pl.BlockSpec(memory_space=SMEM)


def any_spec():
    return pl.BlockSpec(memory_space=pl.ANY)


def params(mebibytes):
    return pltpu.CompilerParams(vmem_limit_bytes=mebibytes * 1024 * 1024)


def cost(flops, moved):
    return pl.CostEstimate(flops=int(flops), bytes_accessed=int(moved), transcendentals=0)


def aligned(value, unit):
    return pl.multiple_of(value * unit, unit)


def off_place(tile, y_tiles, z_tiles):
    a = tile // (y_tiles * z_tiles)
    b = (tile // z_tiles) % y_tiles
    c = tile % z_tiles
    return aligned(a, TW), aligned(b, TW), aligned(c, TL)


def interp_kernel(count, slots, dims, refs):
    (fin, fout, slot_ref, off_ref, near_ref, maps_in, maps_out) = refs[:7]
    outs = refs[7 : 7 + count]
    near_buf, off_buf, in_buf, out_buf, sems = refs[7 + count :]
    rows_here, per_slot, y_tiles, z_tiles = dims
    me = lax.axis_index("gy")
    copies, heads = [], []
    for j in range(count):
        dest = lax.rem(me + j, count)
        k_in, k_out = jnp.int32(0), jnp.int32(0)
        t_in, t_out = jnp.int32(-1), jnp.int32(-1)
        for k in range(rows_here):
            hit = fin[1, k] == dest
            k_in = jnp.where(hit, k, k_in)
            t_in = jnp.where(hit, fin[2, k], t_in)
            hit = fout[1, k] == dest
            k_out = jnp.where(hit, k, k_out)
            t_out = jnp.where(hit, fout[2, k], t_out)
        heads.append((t_in, t_out))
        donor = fin[0, k_in]
        slot, q = donor // per_slot, aligned(donor % per_slot, TW)
        x0, y0, z0 = off_place(fout[0, k_out], y_tiles, z_tiles)
        group = [
            pltpu.make_async_copy(
                near_ref.at[slot, :, :, pl.ds(q, TW), :], near_buf.at[j], sems.at[0, j]
            ),
            pltpu.make_async_copy(maps_in.at[k_in], in_buf.at[j], sems.at[1, j]),
            pltpu.make_async_copy(
                off_ref.at[:, pl.ds(x0, TW), pl.ds(y0, TW), pl.ds(z0, TL)],
                off_buf.at[j],
                sems.at[2, j],
            ),
            pltpu.make_async_copy(maps_out.at[k_out], out_buf.at[j], sems.at[3, j]),
        ]
        for copy in group:
            copy.start()
        copies.append(group)
    lines = FIELDS * TW * TW
    row = lax.broadcasted_iota(jnp.int32, (META, TL), 0)
    for j in range(count):
        for copy in copies[j]:
            copy.wait()
        for side, (tiles, maps) in enumerate(((near_buf, in_buf), (off_buf, out_buf))):
            donors = tiles[j].reshape(lines, TL).astype(jnp.bfloat16)
            mixed = jnp.dot(donors, maps[j], preferred_element_type=jnp.float32)
            outs[j][side * lines : (side + 1) * lines, :] = mixed.astype(jnp.bfloat16)
        head = jnp.where(row == 0, heads[j][0], jnp.where(row == 1, heads[j][1], 0))
        for s in range(slots):
            head = jnp.where(row == 2 + s, slot_ref[s], head)
        outs[j][2 * lines :, :] = head.astype(jnp.float32).astype(jnp.bfloat16)


def base_kernel(slots, dims, refs):
    off_ref, near_ref, metric_ref, layers, faces, edge, medge, sems = refs
    around, nx, ny, nz = dims
    loads = []
    for end, start in enumerate((0, around - TW)):
        for k, (source, target) in enumerate(((near_ref, edge), (metric_ref, medge))):
            loads.append(
                pltpu.make_async_copy(
                    source.at[:, :, :, pl.ds(start, TW), :], target.at[end], sems.at[k, end]
                )
            )
    for copy in loads:
        copy.start()

    def turn(x, _):
        for end, start in enumerate((0, ny - DEPTH)):
            for c in range(FIELDS):
                for d in range(DEPTH):
                    for h in range(nz // TL):
                        layers[end, c * DEPTH + d, h, pl.ds(x, 1), :] = (
                            off_ref[c, x, start + d : start + d + 1, h * TL : (h + 1) * TL]
                            - CENTRE[c]
                        )
        return 0

    lax.fori_loop(0, nx, turn, 0)
    layers[:, FIELDS * DEPTH :] = jnp.ones((2, DEPTH) + layers.shape[2:], jnp.float32)
    for copy in loads:
        copy.wait()
    for s in range(slots):
        for end in range(2):
            number = 0
            for c in range(FIELDS):
                for d in range(DEPTH):
                    layer = d + (0 if end == 0 else TW - DEPTH)
                    slab = face_slab(edge, (end, s, c), layer) - CENTRE[c]
                    faces[s * 2 + end, number * TW : (number + 1) * TW, :] = slab
                    number += 1
            for a in range(3):
                for d in range(DEPTH - 1):
                    layer = d + (0 if end == 0 else TW - DEPTH + 1)
                    slab = face_slab(medge, (end, s, a), layer)
                    faces[s * 2 + end, number * TW : (number + 1) * TW, :] = slab
                    number += 1
            faces[s * 2 + end, number * TW : (number + 1) * TW, :] = jnp.ones(
                (TW, TL), jnp.float32
            )


def patch_kernel(count, dims, refs):
    parcels = refs[:count]
    base_layers, y_low, y_high, table = refs[count : count + 4]
    layers, tiles, wide, head_v, head_s, sems = refs[count + 4 :]
    nx, ny, nz = dims
    y_tiles, z_tiles = ny // TW, nz // TL
    lines = FIELDS * TW * TW
    heads = [
        pltpu.make_async_copy(
            parcels[j].at[pl.ds(2 * lines, META), :],
            tiles.at[j, pl.ds(lines, META), :],
            sems.at[j],
        )
        for j in range(count)
    ]
    bodies = [
        pltpu.make_async_copy(
            parcels[j].at[pl.ds(0, lines), :],
            tiles.at[j, pl.ds(0, lines), :],
            sems.at[count + j],
        )
        for j in range(count)
    ]
    load = pltpu.make_async_copy(base_layers, layers, sems.at[2 * count])
    for copy in heads + bodies + [load]:
        copy.start()
    for j in range(count):
        heads[j].wait()
        head = tiles[j, lines:, :].astype(jnp.float32)
        head_v[j * META : (j + 1) * META, :] = head.astype(jnp.int32)
    head_copy = pltpu.make_async_copy(head_v, head_s, sems.at[2 * count + 1])
    head_copy.start()
    for j in range(count):
        bodies[j].wait()
        wide[j] = tiles[j, :lines, :].astype(jnp.float32)
    load.wait()
    head_copy.wait()
    for j in range(count):
        for r in range(RING):
            table[j * RING + r] = head_s[j * META + r, 0]
    for j in range(count):
        tile = head_s[j * META, 0]
        a = tile // (y_tiles * z_tiles)
        b = (tile // z_tiles) % y_tiles
        h = tile % z_tiles
        x0 = aligned(a, TW)
        for end, edge_tile in enumerate((0, y_tiles - 1)):

            @pl.when((tile >= 0) & (b == edge_tile))
            def _():
                first = 0 if end == 0 else TW - DEPTH
                for c in range(FIELDS):
                    for d in range(DEPTH):
                        slab = wide[j, pl.ds(c * TW * TW + first + d, TW, stride=TW), :]
                        layers[end, c * DEPTH + d, h, pl.ds(x0, TW), :] = slab - CENTRE[c]
                for d in range(DEPTH):
                    layers[end, FIELDS * DEPTH + d, h, pl.ds(x0, TW), :] = jnp.zeros(
                        (TW, TL), jnp.float32
                    )

    for end, out in enumerate((y_low, y_high)):
        out[...] = layers[end].astype(jnp.bfloat16)


def face_slab(ref, lead, layer):
    row = lax.broadcasted_iota(jnp.int32, (TW, TL), 0)
    slab = None
    for i in range(TW):
        line = jnp.broadcast_to(ref[lead + (i, slice(layer, layer + 1), slice(None))], (TW, TL))
        slab = line if slab is None else jnp.where(row == i, line, slab)
    return slab


def fill_kernel(count, per_slot, dims, refs):
    table = refs[0]
    parcels = refs[1 : 1 + count]
    off_ref, base_faces, placed, faces = refs[1 + count : 5 + count]
    tiles, wide, front, sems = refs[5 + count :]
    nx, ny, nz = dims
    y_tiles, z_tiles = ny // TW, nz // TL
    lines = FIELDS * TW * TW
    loads = [pltpu.make_async_copy(parcels[j], tiles.at[j], sems.at[j]) for j in range(count)]
    loads.append(pltpu.make_async_copy(base_faces, front, sems.at[count]))
    for copy in loads:
        copy.start()
    for h in range(z_tiles):
        placed[0:FIELDS, :, h] = off_ref[:, :, :, h * TL : (h + 1) * TL]
    placed[FIELDS] = jnp.full(placed.shape[1:], TIME_STEP, jnp.float32)
    for copy in loads:
        copy.wait()
    for j in range(count):
        tile = table[j * RING + 1]
        s = tile // per_slot
        for end, edge_tile in enumerate((0, per_slot - 1)):

            @pl.when((tile >= 0) & (tile % per_slot == edge_tile))
            def _():
                wide[...] = tiles[j, lines : 2 * lines, :].astype(jnp.float32)
                first = 0 if end == 0 else TW - DEPTH
                for c in range(FIELDS):
                    for d in range(DEPTH):
                        slab = wide[pl.ds(c * TW * TW + first + d, TW, stride=TW), :]
                        number = c * DEPTH + d
                        front[s * 2 + end, number * TW : (number + 1) * TW, :] = slab - CENTRE[c]
                front[s * 2 + end, FACE_ROWS - TW :, :] = jnp.zeros((TW, TL), jnp.float32)

    faces[...] = front[...].astype(jnp.bfloat16)
    for j in range(count):
        tile = table[j * RING]

        @pl.when(tile >= 0)
        def _():
            x0 = (tile // (y_tiles * z_tiles)) * TW
            y0 = aligned((tile // z_tiles) % y_tiles, TW)
            h = tile % z_tiles
            for c in range(FIELDS):
                for i in range(0, TW, 2):
                    start = (c * TW + i) * TW
                    pair = tiles[j, start : start + 2 * TW, :].astype(jnp.float32)
                    for k in range(2):
                        placed[c, x0 + i + k, h, pl.ds(y0, TW), :] = pair[k * TW : (k + 1) * TW]
            for i in range(TW):
                placed[FIELDS, x0 + i, h, pl.ds(y0, TW), :] = jnp.zeros((TW, TL), jnp.float32)


def ghost_rows(low, high, c, h, x, scale):
    row = lax.broadcasted_iota(jnp.int32, (RING, TL), 0)
    tile = jnp.full((RING, TL), QUIET_STATE[c] if c < FIELDS else 1.0, jnp.float32)
    for d in range(DEPTH):
        line = high[c * DEPTH + d, h, pl.ds(x, 1), :] + CENTRE[c]
        tile = jnp.where(row == d, jnp.broadcast_to(line, (RING, TL)), tile)
        line = low[c * DEPTH + d, h, pl.ds(x, 1), :] + CENTRE[c]
        tile = jnp.where(row == RING - DEPTH + d, jnp.broadcast_to(line, (RING, TL)), tile)
    return tile * scale if c == FIELDS else tile


def slab_kernel(dims, refs):
    placed, from_low, from_high, _, x_low, x_high, layers, wide, edge, sems = refs
    nx, ny, nz = dims
    halves = nz // TL
    starts = (0, nx - DEPTH)
    loads = [
        pltpu.make_async_copy(placed.at[:, pl.ds(start, DEPTH)], edge.at[end], sems.at[end])
        for end, start in enumerate(starts)
    ]
    loads += [
        pltpu.make_async_copy(source, layers.at[k], sems.at[2 + k])
        for k, source in enumerate((from_low, from_high))
    ]
    for copy in loads:
        copy.start()
    for copy in loads:
        copy.wait()
    wide[...] = layers[...].astype(jnp.float32)
    low, high = wide.at[0], wide.at[1]
    size = halves * (ny + RING)
    for end, (out, start) in enumerate(((x_low, 0), (x_high, nx - DEPTH))):
        for c in range(FIELDS + 1):
            for d in range(DEPTH):
                parts = []
                for h in range(halves):
                    parts.append(edge[end, c, d, h])
                    parts.append(ghost_rows(low, high, c, h, start + d, TIME_STEP))
                block = jnp.concatenate(parts, axis=0) - CENTRE[c]
                number = c * DEPTH + d
                out[number * size : (number + 1) * size, :] = block.astype(jnp.bfloat16)


def primitives(u):
    density, m0, m1, m2, energy = u
    scaled = VISCOSITY / density
    f = [m0 * scaled, m1 * scaled, m2 * scaled]
    ratio = 0.5 / VISCOSITY
    n0, n1, n2 = ratio * m0, ratio * m1, ratio * m2
    d0, d1, d2 = n0 * f[0], n1 * f[1], n2 * f[2]
    c01, c02, c12 = n0 * f[1], n0 * f[2], n1 * f[2]
    kinetic = (d0 + d1) + d2
    hp = (0.5 * (HEAT_RATIO - 1.0)) * (energy - kinetic)
    f.append(scaled * (kinetic + (2.0 * CONDUCTION / VISCOSITY) * hp))
    enthalpy = ratio * energy + (1.0 / VISCOSITY) * hp
    flux = (
        (0.5 * m0, d0 + hp, c01, c02, enthalpy * f[0]),
        (0.5 * m1, c01, d1 + hp, c12, enthalpy * f[1]),
        (0.5 * m2, c02, c12, d2 + hp, enthalpy * f[2]),
    )
    return f, flux


def off_kernel(dims, refs):
    placed, from_low, from_high, from_left, from_right = refs[:5]
    out, token = refs[5:7]
    layers, slabs, wide, begin, state_one, state_two, sems = refs[7:14]
    flux_x, flux_y, f_s = refs[14:18], refs[18:22], refs[22:26]
    up_z, down_z = refs[26:30], refs[30:34]
    nx, ny, nz = dims
    halves = nz // TL
    rows = ny + RING
    main = FRONT + DEPTH
    load = pltpu.make_async_copy(
        placed, begin.at[:, pl.ds(main, nx), :, pl.ds(0, ny), :], sems.at[0]
    )
    load.start()
    low, high = wide.at[0], wide.at[1]
    received = [
        pltpu.make_async_copy(source, target, sems.at[1 + k])
        for k, (source, target) in enumerate(
            (
                (from_low, layers.at[0]),
                (from_high, layers.at[1]),
                (from_left, slabs.at[0]),
                (from_right, slabs.at[1]),
            )
        )
    ]
    for copy in received:
        copy.start()
    token[...] = jnp.zeros(token.shape, jnp.float32)
    lane = lax.broadcasted_iota(jnp.int32, (TW, TL), 1)
    first_lane, last_lane = lane == 0, lane == TL - 1

    def around_z(parts, distance, mask):
        rolled = [pltpu.roll(part, distance % TL, 1) for part in parts]
        return [jnp.where(mask, rolled[(h - distance) % halves], rolled[h]) for h in range(halves)]

    for copy in received:
        copy.wait()
    wide[...] = layers[...].astype(jnp.float32)
    size = halves * rows
    for side, base in ((slabs.at[0], main - DEPTH), (slabs.at[1], main + nx)):
        for c in range(FIELDS + 1):
            for d in range(DEPTH):
                number = c * DEPTH + d
                block = side[number * size : (number + 1) * size, :].astype(jnp.float32)
                for h in range(halves):
                    begin[c, base + d, h] = block[h * rows : (h + 1) * rows] + CENTRE[c]

    def fill(x, _):
        for c in range(FIELDS + 1):
            for h in range(halves):
                begin[c, x + main, h, ny:rows, :] = ghost_rows(low, high, c, h, x, TIME_STEP)
        return 0

    lax.fori_loop(0, nx, fill, 0)
    load.wait()

    for section, (alpha, beta) in enumerate(SECTIONS):
        last = section == len(SECTIONS) - 1
        source, target = ((begin, state_one), (state_one, state_two), (state_two, out))[section]
        tiles = (ny if last else rows) // TW

        def step(i, turn):
            now, one, two, three = (turn % RINGS, *((turn - k) % RINGS for k in (1, 2, 3)))
            x = i - LAG
            for q in range(rows // TW):
                at = slice(q * TW, (q + 1) * TW)
                base = TW + q * TW
                here, after, before = (slice(base + k, base + k + TW) for k in (0, 1, -1))
                if q < tiles:
                    along_z = []
                    for b in range(FIELDS):
                        up = [up_z[two][b, h, at, :] for h in range(halves)]
                        down = [down_z[two][b, h, at, :] for h in range(halves)]
                        up = around_z(up, -1, last_lane)
                        down = around_z(down, 1, first_lane)
                        along_z.append([up[h] + down[h] for h in range(halves)])
                for h in range(halves):
                    for b in range(FIELDS):
                        if q >= tiles:
                            break
                        k = b - 1
                        rate = along_z[b][h] + (
                            (flux_x[three][b, h, at, :] - flux_x[one][b, h, at, :])
                            + (flux_y[two][b, h, before, :] - flux_y[two][b, h, after, :])
                        )
                        if b > 0:
                            sum_x = f_s[three][k, h, here, :] + f_s[one][k, h, here, :]
                            sum_y = f_s[two][k, h, before, :] + f_s[two][k, h, after, :]
                            rate = rate + ((sum_x + sum_y) - 6.0 * f_s[two][k, h, here, :])
                        moved = source[b, x, h, at, :] + begin[FIELDS, x, h, at, :] * rate
                        if section > 0:
                            moved = alpha * begin[b, x, h, at, :] + beta * moved
                        if last:
                            place = jnp.maximum(x - main, 0)
                            out[b, place, at, h * TL : (h + 1) * TL] = moved
                        else:
                            target[b, x, h, at, :] = moved
                    f, flux = primitives([source[c, i, h, at, :] for c in range(FIELDS)])
                    wrap = None
                    if q == 0:
                        wrap = slice(TW + rows, 2 * TW + rows)
                    if (q + 1) * TW == rows:
                        wrap = slice(0, TW)
                    for b in range(FIELDS):
                        if q < tiles:
                            flux_x[now][b, h, at, :] = flux[0][b]
                        flux_y[now][b, h, here, :] = flux[1][b]
                        if wrap is not None:
                            flux_y[now][b, h, wrap, :] = flux[1][b]
                        if b > 0:
                            f_s[now][b - 1, h, here, :] = f[b - 1]
                            if wrap is not None:
                                f_s[now][b - 1, h, wrap, :] = f[b - 1]
                    if q < tiles:
                        for b in range(FIELDS):
                            part = flux[2][b]
                            up_z[now][b, h, at, :] = f[b - 1] - part if b > 0 else -part
                            down_z[now][b, h, at, :] = f[b - 1] + part if b > 0 else part

        reach = DEPTH - 1 - section
        stop = main + nx + reach + LAG
        turns = -(-(nx + 2 * reach + LAG + 1) // RINGS)

        def body(j, _):
            for turn in range(RINGS):
                step(stop - turns * RINGS + j * RINGS + turn, turn)
            return 0

        lax.fori_loop(0, turns, body, 0)


def find(table, count, slots, block):
    where_j, where_t = jnp.int32(0), jnp.int32(0)
    for j in range(count):
        for t in range(slots):
            hit = table[j * RING + 2 + t] == block
            where_j = jnp.where(hit, j, where_j)
            where_t = jnp.where(hit, t, where_t)
    return where_j, where_t


def pack_kernel(count, slots, refs):
    table, block_faces = refs[:2]
    held = refs[2 : 2 + count // 2]
    packed, sems = refs[4 + count // 2 :]
    me = lax.axis_index("gy")
    offset = jnp.where(lax.rem(me, 2) == 1, 1, count - 1)
    for phase in range(2):
        for s in range(slots):
            block = table[offset * RING + 2 + s]

            @pl.when(block >= 0)
            def _():
                for side in range(2):
                    j, t = find(table, count, slots, block_faces[block, side])
                    for m in range(count // 2):

                        @pl.when(j == 2 * m)
                        def _():
                            number = s * 2 + side
                            copy = pltpu.make_async_copy(
                                held[m].at[t * 2 + 1 - side], packed.at[number], sems.at[number]
                            )
                            if phase == 0:
                                copy.start()
                            else:
                                copy.wait()


def near_kernel(count, slots, dims, edges, refs):
    per_slot, around, normal = dims
    table, block_faces, slot_ref, near_ref, metric_ref = refs[:5]
    parcels = refs[5 : 5 + count]
    refs = refs[5 + count :]
    if edges:
        held, packed, main_ref = refs[: count // 2], refs[count // 2], refs[count // 2 + 1]
        out_ref = refs[count // 2 + 3]
        scratch = refs[count // 2 + 4 :]
        own = 2 * TW
        rows = own + RING
    else:
        out_ref, token = refs[1:3]
        scratch = refs[3:]
        token[...] = jnp.zeros(token.shape, jnp.float32)
        own = rows = around
    begins, metrics, state_one, state_two, square, coeff, hold, out, along = scratch[:9]
    tile_buf, in_sems, out_sems, tile_sems = scratch[9:13]
    rings = scratch[13:37]
    flux_n, flux_a, f_s = rings[:4], rings[4:8], rings[8:12]
    up_s, down_s, own_s = rings[12:16], rings[16:20], rings[20:24]
    if edges:
        ghost, face_buf, main_buf, face_sems, main_sems = scratch[37:]
    lines = FIELDS * TW * TW
    wall = (-1.0, 1.0, 1.0, 1.0, -1.0)
    mirror = (-1.0, -1.0, -1.0, 1.0)
    pieces = ((0, 0), (around - TW, TW)) if edges else ((0, 0),)
    piece = TW if edges else around

    def loads(s):
        side = lax.rem(s, 2)
        return [
            pltpu.make_async_copy(
                ref.at[s, :, :, pl.ds(source, piece), :],
                buf.at[side, :, :, pl.ds(target, piece), :],
                in_sems.at[k, p, side],
            )
            for k, (ref, buf) in enumerate(((near_ref, begins), (metric_ref, metrics)))
            for p, (source, target) in enumerate(pieces)
        ]

    def main_loads(s):
        return [
            pltpu.make_async_copy(
                main_ref.at[s, :, :, pl.ds(source, TW), :],
                main_buf.at[s, :, :, pl.ds(target, TW), :],
                main_sems.at[s, p],
            )
            for p, (source, target) in enumerate(pieces)
        ]

    def stores(s):
        return [
            pltpu.make_async_copy(
                out.at[s, :, :, pl.ds(target, piece), :],
                out_ref.at[s, :, :, pl.ds(source, piece), :],
                out_sems.at[s, p],
            )
            for p, (source, target) in enumerate(pieces)
        ]

    def start_loads(s):
        @pl.when(slot_ref[s] >= 0)
        def _():
            for copy in loads(s):
                copy.start()

    start_loads(0)
    lane = lax.broadcasted_iota(jnp.int32, (rows, TL), 1)
    tile_loads = [
        pltpu.make_async_copy(
            parcels[j].at[pl.ds(lines, lines), :], tile_buf.at[j], tile_sems.at[j]
        )
        for j in range(count)
    ]
    for copy in tile_loads:
        copy.start()

    def face_loads(s):
        for side in range(2):
            j, t = find(table, count, slots, block_faces[slot_ref[s], side])
            target, sem = face_buf.at[s, side], face_sems.at[s, side]
            for m in range(count // 2):

                @pl.when(j == 2 * m)
                def _():
                    pltpu.make_async_copy(held[m].at[t * 2 + 1 - side], target, sem).start()

            @pl.when(lax.rem(j, 2) == 1)
            def _():
                pltpu.make_async_copy(packed.at[s * 2 + side], target, sem).start()

    if edges:
        for s in range(slots):

            @pl.when(slot_ref[s] >= 0)
            def _():
                face_loads(s)
                for copy in main_loads(s):
                    copy.start()

    for copy in tile_loads:
        copy.wait()
    row = lax.broadcasted_iota(jnp.int32, (RING, TL), 0)

    def take_ghosts(s, begin, metric):
        for side in range(2):
            pltpu.make_async_copy(
                packed.at[0], face_buf.at[s, side], face_sems.at[s, side]
            ).wait()
            ghost[side] = face_buf[s, side].astype(jnp.float32)

        def ghost_tile(number, layers, i, fill, centre):
            tile = jnp.full((RING, TL), fill, jnp.float32)
            for d in range(layers):
                at = (number + d) * TW + i
                line = jnp.broadcast_to(ghost[1, at : at + 1, :] + centre, (RING, TL))
                tile = jnp.where(row == d, line, tile)
                line = jnp.broadcast_to(ghost[0, at : at + 1, :] + centre, (RING, TL))
                tile = jnp.where(row == RING - layers + d, line, tile)
            return tile

        step = DEPTH - 1
        for i in range(normal):
            for c in range(FIELDS):
                begin[c, i, own:rows, :] = ghost_tile(
                    c * DEPTH, DEPTH, i, QUIET_STATE[c], CENTRE[c]
                )
            for a in range(3):
                metric[a, i, own:rows, :] = ghost_tile(
                    FIELDS * DEPTH + a * step, step, i, 1.0, 0.0
                )
        last_layer = (FACE_LAYERS - 1) * TW
        hold[own:rows, :] = TIME_STEP * jnp.where(
            row < RING // 2,
            ghost[1, last_layer : last_layer + TW, :],
            ghost[0, last_layer : last_layer + TW, :],
        )

    def slot_work(s, _):
        begin, metric = begins.at[lax.rem(s, 2)], metrics.at[lax.rem(s, 2)]

        @pl.when(s + 1 < slots)
        def _():
            start_loads(jnp.minimum(s + 1, slots - 1))

        if not edges:

            @pl.when(slot_ref[s] < 0)
            def _():
                out[s] = jnp.zeros(out.shape[1:], jnp.float32)

        @pl.when(slot_ref[s] >= 0)
        def _():
            if edges:
                take_ghosts(s, begin, metric)
            hold[0:own, :] = jnp.full((own, TL), TIME_STEP, jnp.float32)
            for copy in loads(s):
                copy.wait()
            if edges:
                for copy in main_loads(s):
                    copy.wait()
            for j in range(count):
                tile = table[j * RING + 1]
                number = tile % per_slot
                mine = (tile >= 0) & (tile // per_slot == s)
                if edges:
                    mine = mine & ((number == 0) | (number == per_slot - 1))
                    number = jnp.where(number == 0, 0, 1)

                @pl.when(mine)
                def _():
                    q = aligned(number, TW)
                    for c in range(FIELDS):
                        for i in range(0, TW, 2):
                            start = (c * TW + i) * TW
                            pair = tile_buf[j, start : start + 2 * TW, :].astype(jnp.float32)
                            begin[c, i, pl.ds(q, TW), :] = pair[:TW]
                            begin[c, i + 1, pl.ds(q, TW), :] = pair[TW:]
                    hold[pl.ds(q, TW), :] = jnp.zeros((TW, TL), jnp.float32)

            def prepare(i, _):
                squares = [metric[a, i] * metric[a, i] for a in range(3)]
                for a in range(2):
                    square[a, i] = squares[a]
                total = -2.0 * ((squares[0] + squares[1]) + squares[2])
                at_end = (lane == 0) | (lane == TL - 1)
                coeff[i] = jnp.where(at_end, total + squares[2], total)
                g = metric[2, i]
                along[0, i] = jnp.where(lane == 0, 0.0, pltpu.roll(g, 1, 1))
                along[1, i] = jnp.where(lane == TL - 1, 0.0, pltpu.roll(g, TL - 1, 1))
                along[2, i] = jnp.where(lane == 0, g, jnp.where(lane == TL - 1, -g, 0.0))
                return 0

            lax.fori_loop(0, normal, prepare, 0)

            for section, (alpha, beta) in enumerate(SECTIONS):
                last = section == len(SECTIONS) - 1
                source = (begin, state_one, state_two)[section]
                target = (state_one, state_two, out)[section]
                tiles = (own if last else rows) // TW

                def advance(x, q):
                    at = slice(q * TW, (q + 1) * TW)
                    base = TW + q * TW
                    here, after, before = (slice(base + k, base + k + TW) for k in (0, 1, -1))
                    mid, low = x % RINGS, (x - 1) % RINGS
                    high = (x + 1) % RINGS
                    g = [metric[a, x, at, :] for a in range(2)]
                    g2 = [square[a, x, at, :] for a in range(2)]
                    center = coeff[x, at, :]
                    for b in range(FIELDS):
                        k = b - 1
                        rate = pltpu.roll(up_s[mid][b, at, :], TL - 1, 1)
                        rate = rate + pltpu.roll(down_s[mid][b, at, :], 1, 1)
                        rate = rate + own_s[mid][b, at, :]
                        rate = rate + g[0] * (flux_n[low][b, at, :] - flux_n[high][b, at, :])
                        rate = rate + g[1] * (
                            flux_a[mid][b, before, :] - flux_a[mid][b, after, :]
                        )
                        if b > 0:
                            rate = rate + g2[0] * (f_s[low][k, here, :] + f_s[high][k, here, :])
                            rate = rate + g2[1] * (
                                f_s[mid][k, before, :] + f_s[mid][k, after, :]
                            )
                            rate = rate + center * f_s[mid][k, here, :]
                        moved = source[b, x, at, :] + hold[at, :] * rate
                        if section > 0:
                            moved = alpha * begin[b, x, at, :] + beta * moved
                        if last and edges:
                            right = row < DEPTH if q == 0 else row >= TW - DEPTH
                            moved = jnp.where(right, moved, main_buf[s, b, x, at, :])
                        if last:
                            out[s, b, x, at, :] = moved
                        else:
                            target[b, x, at, :] = moved

                def work(i, q):
                    at = slice(q * TW, (q + 1) * TW)
                    base = TW + q * TW
                    here = slice(base, base + TW)
                    now = i % RINGS
                    f, flux = primitives([source[c, i, at, :] for c in range(FIELDS)])
                    wrap = None
                    if q == 0:
                        wrap = slice(TW + rows, 2 * TW + rows)
                    if base == rows:
                        wrap = slice(0, TW)
                    for b in range(FIELDS):
                        if q < tiles:
                            flux_n[now][b, at, :] = flux[0][b]
                            if i == 0:
                                flux_n[now - 1][b, at, :] = wall[b] * flux[0][b]
                            if i == normal - 1:
                                flux_n[(now + 1) % RINGS][b, at, :] = flux[0][b]
                        flux_a[now][b, here, :] = flux[1][b]
                        if wrap is not None:
                            flux_a[now][b, wrap, :] = flux[1][b]
                        if b > 0:
                            f_s[now][b - 1, here, :] = f[b - 1]
                            if wrap is not None:
                                f_s[now][b - 1, wrap, :] = f[b - 1]
                            if i == 0:
                                f_s[now - 1][b - 1, here, :] = mirror[b - 1] * f[b - 1]
                            if i == normal - 1:
                                f_s[(now + 1) % RINGS][b - 1, here, :] = f[b - 1]
                    if q < tiles:
                        g_up, g_down = along[0, i, at, :], along[1, i, at, :]
                        g_own = along[2, i, at, :]
                        for b in range(FIELDS):
                            part = flux[2][b]
                            if b > 0:
                                up_s[now][b, at, :] = g_up * (g_up * f[b - 1] - part)
                                down_s[now][b, at, :] = g_down * (g_down * f[b - 1] + part)
                            else:
                                up_s[now][b, at, :] = -(g_up * part)
                                down_s[now][b, at, :] = g_down * part
                            own_s[now][b, at, :] = g_own * part

                for i in range(normal + LAG):
                    for q in range(rows // TW):
                        if i >= LAG and q < tiles:
                            advance(i - LAG, q)
                        if i < normal:
                            work(i, q)

        def send_out():
            for copy in stores(s):
                copy.start()

        if edges:
            pl.when(slot_ref[s] >= 0)(send_out)
        else:
            send_out()
        return 0

    lax.fori_loop(0, slots, slot_work, 0)
    for s in range(slots):

        def end_out():
            for copy in stores(s):
                copy.wait()

        if edges:
            pl.when(slot_ref[s] >= 0)(end_out)
        else:
            end_out()


def packed_refs(kernel, *first):
    def body(*refs):
        kernel(*first, refs)

    return body


def off_call(placed, from_low, from_high, from_left, from_right):
    _, nx, halves, ny, _ = placed.shape
    nz = halves * TL
    f32, shape = jnp.float32, jax.ShapeDtypeStruct
    rows = ny + RING
    slices = FRONT + nx + 2 * DEPTH + 2
    return pl.pallas_call(
        packed_refs(off_kernel, (nx, ny, nz)),
        out_shape=[shape((FIELDS, nx, ny, nz), f32), shape((RING, TL), f32)],
        in_specs=[any_spec()] * 5,
        out_specs=[vmem_spec()] * 2,
        scratch_shapes=[
            VMEM((2,) + from_low.shape, jnp.bfloat16),
            VMEM((2,) + from_left.shape, jnp.bfloat16),
            VMEM((2,) + from_low.shape, f32),
            VMEM((FIELDS + 1, slices, halves, rows, TL), f32),
            VMEM((FIELDS, slices, halves, rows, TL), f32),
            VMEM((FIELDS, slices, halves, rows, TL), f32),
            pltpu.SemaphoreType.DMA((5,)),
        ]
        + [VMEM((FIELDS, halves, rows, TL), f32)] * RINGS
        + [VMEM((FIELDS, halves, rows + 2 * TW, TL), f32)] * RINGS
        + [VMEM((FIELDS - 1, halves, rows + 2 * TW, TL), f32)] * RINGS
        + [VMEM((FIELDS, halves, rows, TL), f32)] * RINGS * 2,
        compiler_params=params(40),
        cost_estimate=cost(1e8, 5e7),
        name="off_sections",
    )(placed, from_low, from_high, from_left, from_right)


def near_call(table, block_faces, slot_block, near_state, near_metric, parcels, edges, after):
    count = len(parcels)
    slots, _, normal, around, _ = near_state.shape
    f32, shape = jnp.float32, jax.ShapeDtypeStruct
    dma = pltpu.SemaphoreType.DMA
    own = 2 * TW if edges else around
    rows = own + RING if edges else own
    pieces = 2 if edges else 1
    out_shape = [shape(near_state.shape, f32)]
    out_specs = [any_spec()]
    extra, aliases = [], {}
    if edges:
        aliases = {5 + count + count // 2 + 1: 0}
        extra = [
            VMEM((2, FACE_ROWS, TL), f32),
            VMEM((slots, 2, FACE_ROWS, TL), jnp.bfloat16),
            VMEM((slots, FIELDS, normal, own, TL), f32),
            dma((slots, 2)),
            dma((slots, 2)),
        ]
    else:
        out_shape.append(shape((RING, TL), f32))
        out_specs.append(vmem_spec())
    return pl.pallas_call(
        packed_refs(near_kernel, count, slots, (around // TW, around, normal), edges),
        out_shape=out_shape,
        in_specs=[smem_spec()] * 3 + [any_spec()] * (2 + count + len(after)),
        out_specs=out_specs,
        input_output_aliases=aliases,
        scratch_shapes=[
            VMEM((2, FIELDS, normal, rows, TL), f32),
            VMEM((2, 3, normal, rows, TL), f32),
            VMEM((FIELDS, normal, rows, TL), f32),
            VMEM((FIELDS, normal, rows, TL), f32),
            VMEM((2, normal, rows, TL), f32),
            VMEM((normal, rows, TL), f32),
            VMEM((rows, TL), f32),
            VMEM((slots, FIELDS, normal, own, TL), f32),
            VMEM((3, normal, rows, TL), f32),
            VMEM((count, FIELDS * TW * TW, TL), jnp.bfloat16),
            dma((2, pieces, 2)),
            dma((slots, pieces)),
            dma((count,)),
        ]
        + [VMEM((FIELDS, rows, TL), f32)] * RINGS
        + [VMEM((FIELDS, rows + 2 * TW, TL), f32)] * RINGS
        + [VMEM((FIELDS - 1, rows + 2 * TW, TL), f32)] * RINGS
        + [VMEM((FIELDS, rows, TL), f32)] * RINGS * 3
        + extra,
        compiler_params=params(VMEM_MIB),
        cost_estimate=cost(1e8, 5e7),
        name="near_edges" if edges else "near_sections",
    )(table, block_faces, slot_block, near_state, near_metric, *parcels, *after)


def ring(axis, distance):
    count = lax.axis_size(axis)
    return [(i, (i + distance) % count) for i in range(count)]


def send(value, axis, distance):
    return lax.ppermute(value, axis, ring(axis, distance))


def local(
    off_state,
    near_state,
    near_metric,
    slot_block,
    block_faces,
    fringe_in,
    fringe_in_maps,
    fringe_out,
    fringe_out_maps,
):
    count = lax.axis_size("gy")
    slots, _, normal, around, span = near_state.shape
    _, nx, ny, nz = off_state.shape
    rows_here = fringe_in.shape[1]
    per_slot = around // TW
    lines = FIELDS * TW * TW
    half, f32 = jnp.bfloat16, jnp.float32
    shape = jax.ShapeDtypeStruct
    tile_buf = VMEM((count, FIELDS, TW, TW, TL), f32)
    map_buf = VMEM((count, TL, TL), half)

    parcels = pl.pallas_call(
        packed_refs(
            interp_kernel, count, slots, (rows_here, per_slot, ny // TW, nz // TL)
        ),
        out_shape=[shape((2 * lines + META, TL), half)] * count,
        in_specs=[smem_spec()] * 3 + [any_spec()] * 4,
        out_specs=[vmem_spec()] * count,
        scratch_shapes=[
            tile_buf,
            tile_buf,
            map_buf,
            map_buf,
            pltpu.SemaphoreType.DMA((4, count)),
        ],
        compiler_params=params(VMEM_MIB),
        cost_estimate=cost(2e8, 6e6),
        name="interp",
    )(fringe_in, fringe_out, slot_block, off_state, near_state, fringe_in_maps, fringe_out_maps)
    dma = pltpu.SemaphoreType.DMA
    planes = (FIELDS + 1) * DEPTH
    halves = nz // TL
    layer_shape = (planes, halves, nx, TL)
    base_layers, base_faces = pl.pallas_call(
        packed_refs(base_kernel, slots, (around, nx, ny, nz)),
        out_shape=[
            shape((2,) + layer_shape, f32),
            shape((2 * slots, FACE_ROWS, TL), f32),
        ],
        in_specs=[vmem_spec()] + [any_spec()] * 2,
        out_specs=[vmem_spec()] * 2,
        scratch_shapes=[
            VMEM((2, slots, FIELDS, normal, TW, TL), f32),
            VMEM((2, slots, 3, normal, TW, TL), f32),
            dma((2, 2)),
        ],
        compiler_params=params(VMEM_MIB),
        cost_estimate=cost(1e7, 2e7),
        name="base",
    )(off_state, near_state, near_metric)

    parcels = [parcels[0]] + [send(parcels[j], "gy", j) for j in range(1, count)]

    y_low, y_high, table = pl.pallas_call(
        packed_refs(patch_kernel, count, (nx, ny, nz)),
        out_shape=[
            shape(layer_shape, half),
            shape(layer_shape, half),
            shape((count * RING,), jnp.int32),
        ],
        in_specs=[any_spec()] * (count + 1),
        out_specs=[vmem_spec()] * 2 + [smem_spec()],
        scratch_shapes=[
            VMEM((2,) + layer_shape, f32),
            VMEM((count, lines + META, TL), half),
            VMEM((count, lines, TL), f32),
            VMEM((count * META, TL), jnp.int32),
            SMEM((count * META, TL), jnp.int32),
            dma((2 * count + 2,)),
        ],
        compiler_params=params(12),
        cost_estimate=cost(1e7, 8e6),
        name="patch",
    )(*parcels, base_layers)

    from_low = send(y_high, "gy", 1)
    from_high = send(y_low, "gy", count - 1)

    placed, faces = pl.pallas_call(
        packed_refs(fill_kernel, count, per_slot, (nx, ny, nz)),
        out_shape=[
            shape((FIELDS + 1, nx, halves, ny, TL), f32),
            shape((2 * slots, FACE_ROWS, TL), half),
        ],
        in_specs=[smem_spec()] + [any_spec()] * count + [vmem_spec()] + [any_spec()],
        out_specs=[vmem_spec()] * 2,
        scratch_shapes=[
            VMEM((count, 2 * lines + META, TL), half),
            VMEM((lines, TL), f32),
            VMEM((2 * slots, FACE_ROWS, TL), f32),
            dma((count + 1,)),
        ],
        compiler_params=params(VMEM_MIB),
        cost_estimate=cost(1e7, 1e7),
        name="fill",
    )(table, *parcels, off_state, base_faces)
    held = [faces] + [send(faces, "gy", 2 * m) for m in range(1, count // 2)]

    near_main, near_token = near_call(
        table, block_faces, slot_block, near_state, near_metric, parcels, False, [faces]
    )

    x_low, x_high = pl.pallas_call(
        packed_refs(slab_kernel, (nx, ny, nz)),
        out_shape=[shape((planes * halves * (ny + RING), TL), half)] * 2,
        in_specs=[any_spec()] * 4,
        out_specs=[vmem_spec()] * 2,
        scratch_shapes=[
            VMEM((2,) + layer_shape, half),
            VMEM((2,) + layer_shape, f32),
            VMEM((2, FIELDS + 1, DEPTH, halves, ny, TL), f32),
            dma((4,)),
        ],
        compiler_params=params(8),
        cost_estimate=cost(1e6, 4e6),
        name="slabs",
    )(placed, from_low, from_high, near_token)
    from_left = send(x_high, "gx", 1)
    from_right = send(x_low, "gx", lax.axis_size("gx") - 1)

    packed = pl.pallas_call(
        packed_refs(pack_kernel, count, slots),
        out_shape=shape((2 * slots, FACE_ROWS, TL), half),
        in_specs=[smem_spec()] * 2 + [any_spec()] * (count // 2 + 2),
        out_specs=any_spec(),
        scratch_shapes=[dma((2 * slots,))],
        compiler_params=params(4),
        cost_estimate=cost(1e5, 2e6),
        name="pack",
    )(table, block_faces, *held, from_left, from_right)
    packed = lax.ppermute(packed, "gy", [(i, i ^ 1) for i in range(count)])

    off_next, off_token = off_call(placed, from_low, from_high, from_left, from_right)
    after = [*held, packed, near_main, off_token]
    (near_next,) = near_call(
        table, block_faces, slot_block, near_state, near_metric, parcels, True, after
    )
    return off_next, near_next


def solution(mesh):
    in_specs = (
        P(None, "gx", "gy", None),
        P(("gx", "gy"), None, None, None, None),
        P(("gx", "gy"), None, None, None, None),
        P(("gx", "gy")),
        P(),
        P(None, ("gx", "gy")),
        P(("gx", "gy"), None, None),
        P(None, ("gx", "gy")),
        P(("gx", "gy"), None, None),
    )
    out_specs = (P(None, "gx", "gy", None), P(("gx", "gy"), None, None, None, None))
    return jax.shard_map(local, mesh=mesh, in_specs=in_specs, out_specs=out_specs, check_vma=False)
```

time: 914 us -> 121 us (0.13); the launches traced: 905 us -> 121 us
  other arithmetic: 505 us -> 0 us
  blocking collectives: 134 us -> 0 us
  local copies, waits for them, and re-layouts: 121 us -> 4.09 us
  waiting for transfers between devices: 98.5 us -> 10.9 us
  Pallas kernels: 0 us -> 71.8 us
  starting transfers between devices: 14.1 us -> 33 us
  between operations: 17.8 us -> 1.04 us
  matrix products: 13.8 us -> 0 us
    unnamed x90 -> x0, other arithmetic: 158 us -> none
    another operation x36 -> x0, other arithmetic: 114 us -> none
    all_gather x3 -> x0, blocking collectives: 104 us -> none  [near_rate(): portion_faces = lax.all_gather(as_sent(face_rows), 'gy', axis=0, tiled=True)]
    sub x8 -> x0, other arithmetic: 93.9 us -> none  [the longest x6 93.8 us: residual(): shifted(viscous_contribution, direction, 1)]
    pallas_call x0 -> x9, Pallas kernels: none -> 71.8 us  [the longest x2 33 us: near_call(): pl.pallas_call(packed_refs(near_kernel, count, slots, (around // TW, arou...]
    unnamed x254 -> x43, local copies, waits for them, and re-layouts: 69.6 us -> 4.09 us
    concatenate x12 -> x0, other arithmetic: 51 us -> none  [the longest x3 40.8 us: frame_near(): return jnp.concatenate([joined[..., 0:1], joined, joined[..., -1:]], axis=4)]
    all_gather x2 -> x0, waiting for transfers between devices: 48.9 us -> none  [the longest x1 41.5 us: local(): values_in = lax.all_gather(sent_in, 'gy', axis=0, tiled=True)]
  transfers between devices with their start and end apart: 19 -> 15, of which waited for: 12 -> 6; matrix products, arithmetic and copies ran while one was open for 16% -> 1% of each run, Pallas kernels for 0% -> 41%
where the time goes in v1:
time: 121 us
  Pallas kernels  71.8 us (59%)
  starting transfers between devices  33 us (27%)
  waiting for transfers between devices  10.9 us (9%)
  local copies, waits for them, and re-layouts  4.09 us (3%)
    pallas_call x2, Pallas kernels, near_call(): pl.pallas_call(packed_refs(near_kernel, count, slots, (around // TW, arou...  33 us
    ppermute x14, starting transfers between devices, send(): return lax.ppermute(value, axis, ring(axis, distance))  32.9 us
    pallas_call x1, Pallas kernels, off_call(): pl.pallas_call(packed_refs(off_kernel, (nx, ny, nz)), out_shape=[shape((F...  17.8 us
    ppermute x14, waiting for transfers between devices, send(): return lax.ppermute(value, axis, ring(axis, distance))  10.9 us
    pallas_call x1, Pallas kernels, local(): pl.pallas_call(packed_refs(fill_kernel, count, per_slot, (nx, ny, nz)), o...  5.51 us
    pallas_call x1, Pallas kernels, local(): pl.pallas_call(packed_refs(base_kernel, slots, (around, nx, ny, nz)), out...  4.56 us
    pallas_call x1, Pallas kernels, local(): pl.pallas_call(packed_refs(interp_kernel, count, slots, (rows_here, per_s...  4.51 us
    unnamed x43, local copies, waits for them, and re-layouts  4.09 us
  transfers between devices with their start and end apart: 15, of which 6 were waited for; matrix products, arithmetic and copies ran while one was open for 1% of the time, Pallas kernels for 41%

profile of v1, /device:TPU:0, one launch (start us, length us, event | category | flops | bytes accessed | tf_op | source)
XLA Modules:
  0.0 120.8 jit_solution(402840373963860936)
XLA Ops:
  0.6 4.5 %interp.1 = (bf16[656,128]{1,0:T(8,128)(2,1)}, bf16[656,128]{1,0:T(8,128)(2,1)}, bf16[656,128]{1,0:T(8,128)(2,1)}, bf16[656,128]{1,0:T(8,128)(2,1)}, bf16[656,12...) custom-call(s32[3,8]{1,0:T(4,128)} %refs_0_.2, ...), custom_call_target="tpu_custom_call" | custom-call | flops 200000000 | bytes 6000000 | tf_op jit(solution)/shard_map/interp/pallas_call | solution.py:956
  5.2 3.0 %collective-permute-start = (bf16[656,128]{1,0:T(8,128)(2,1)}, bf16[656,128]{1,0:T(8,128)(2,1)S(1)}, u32[]{:S(2)}, u32[]{:S(2)}) collective-permute-start(bf16[656,128]{1,0:T(8,128)(2,1)} %get-tuple-element.24), channel_id=1, source_target_pairs={{0,1},{1,2},{2,3},{3,4},{4,5},{5,6},{6,7},{7,0},{8,9},{9,10},{10,1... | collective-permute-start | bytes 503816 | tf_op jit(solution)/shard_map/ppermute | solution.py:931
  8.2 1.6 %collective-permute-start.1 = (bf16[656,128]{1,0:T(8,128)(2,1)}, bf16[656,128]{1,0:T(8,128)(2,1)S(1)}, u32[]{:S(2)}, u32[]{:S(2)}) collective-permute-start(bf16[656,128]{1,0:T(8,128)(2,1)} %get-tuple-element.25), channel_id=1, source_target_pairs={{0,2},{1,3},{2,4},{3,5},{4,6},{5,7},{6,0},{7,1},{8,10},{9,11},{10,... | collective-permute-start | bytes 503816 | tf_op jit(solution)/shard_map/ppermute | solution.py:931
  9.8 2.5 %collective-permute-start.2 = (bf16[656,128]{1,0:T(8,128)(2,1)}, bf16[656,128]{1,0:T(8,128)(2,1)S(1)}, u32[]{:S(2)}, u32[]{:S(2)}) collective-permute-start(bf16[656,128]{1,0:T(8,128)(2,1)} %get-tuple-element.26), channel_id=1, source_target_pairs={{0,3},{1,4},{2,5},{3,6},{4,7},{5,0},{6,1},{7,2},{8,11},{9,12},{10,... | collective-permute-start | bytes 503816 | tf_op jit(solution)/shard_map/ppermute | solution.py:931
  12.3 1.2 %collective-permute-start.3 = (bf16[656,128]{1,0:T(8,128)(2,1)}, bf16[656,128]{1,0:T(8,128)(2,1)S(1)}, u32[]{:S(2)}, u32[]{:S(2)}) collective-permute-start(bf16[656,128]{1,0:T(8,128)(2,1)} %get-tuple-element.27), channel_id=1, source_target_pairs={{0,4},{1,5},{2,6},{3,7},{4,0},{5,1},{6,2},{7,3},{8,12},{9,13},{10,... | collective-permute-start | bytes 503816 | tf_op jit(solution)/shard_map/ppermute | solution.py:931
  13.5 2.6 %collective-permute-start.4 = (bf16[656,128]{1,0:T(8,128)(2,1)}, bf16[656,128]{1,0:T(8,128)(2,1)S(1)}, u32[]{:S(2)}, u32[]{:S(2)}) collective-permute-start(bf16[656,128]{1,0:T(8,128)(2,1)} %get-tuple-element.28), channel_id=1, source_target_pairs={{0,5},{1,6},{2,7},{3,0},{4,1},{5,2},{6,3},{7,4},{8,13},{9,14},{10,... | collective-permute-start | bytes 503816 | tf_op jit(solution)/shard_map/ppermute | solution.py:931
  16.2 0.5 collective-permute-done.refs_1_.refs_2_.refs_6_
  16.7 1.8 %collective-permute-start.5 = (bf16[656,128]{1,0:T(8,128)(2,1)}, bf16[656,128]{1,0:T(8,128)(2,1)S(1)}, u32[]{:S(2)}, u32[]{:S(2)}) collective-permute-start(bf16[656,128]{1,0:T(8,128)(2,1)} %get-tuple-element.29), channel_id=1, source_target_pairs={{0,6},{1,7},{2,0},{3,1},{4,2},{5,3},{6,4},{7,5},{8,14},{9,15},{10,... | collective-permute-start | bytes 503816 | tf_op jit(solution)/shard_map/ppermute | solution.py:931
  18.6 0.0 collective-permute-done.1.refs_2_.refs_3_.refs_7_
  18.6 2.8 %collective-permute-start.6 = (bf16[656,128]{1,0:T(8,128)(2,1)}, bf16[656,128]{1,0:T(8,128)(2,1)S(1)}, u32[]{:S(2)}, u32[]{:S(2)}) collective-permute-start(bf16[656,128]{1,0:T(8,128)(2,1)} %get-tuple-element.30), channel_id=1, source_target_pairs={{0,7},{1,0},{2,1},{3,2},{4,3},{5,4},{6,5},{7,6},{8,15},{9,8},{10,9... | collective-permute-start | bytes 503816 | tf_op jit(solution)/shard_map/ppermute | solution.py:931
  21.4 4.6 %base.1 = (f32[2,18,2,32,128]{4,3,2,1,0:T(8,128)}, f32[6,176,128]{2,1,0:T(8,128)}) custom-call(f32[5,32,16,256]{3,2,1,0:T(8,128)} %refs_9_.1, f32[3,5,8,64,128]{4,3,2,1,0:T(8,128)} %refs_3_.5, f32[3,3,8,64,128]{4,3,2,1,0:T(8,128)} %refs_4_.5), custom_call_target="tpu_custom_call" | custom-call | flops 10000000 | bytes 20000000 | tf_op jit(solution)/shard_map/base/pallas_call | solution.py:978
  25.9 4.3 %collective-permute-done.2.refs_3_.refs_4_.refs_8_ = bf16[656,128]{1,0:T(8,128)(2,1)S(1)} collective-permute-done((bf16[656,128]{1,0:T(8,128)(2,1)}, bf16[656,128]{1,0:T(8,128)(2,1)S(1)}, u32[]{:S(2)}, u32[]{:S(2)}) %collective-permute-start.2) | collective-permute-done | bytes 167968 | tf_op jit(solution)/shard_map/ppermute | solution.py:931
  30.3 0.2 collective-permute-done.3.refs_4_.refs_5_.refs_9_
  30.5 0.0 collective-permute-done.4.refs_5_.refs_6_.refs_10_
  30.5 0.0 collective-permute-done.5.refs_6_.refs_7_.refs_11_
  30.5 0.0 copy-start.7
  30.5 0.9 collective-permute-done.6.refs_7_.refs_8_.refs_12_
  31.4 0.0 copy-done.2
  31.4 0.0 copy-done.3
  31.4 0.0 copy-done.1
  31.4 0.0 copy-start.10
  31.4 1.3 %copy-done.10 = f32[2,18,2,32,128]{4,3,2,1,0:T(8,128)S(1)} copy-done((f32[2,18,2,32,128]{4,3,2,1,0:T(8,128)S(1)}, f32[2,18,2,32,128]{4,3,2,1,0:T(8,128)}, u32[]{:S(2)}) %copy-start.10) | copy-done | bytes 1179672
  32.7 3.9 %patch.1 = (bf16[18,2,32,128]{3,2,1,0:T(8,128)(2,1)S(1)}, bf16[18,2,32,128]{3,2,1,0:T(8,128)(2,1)S(1)}, s32[64]{0:T(128)S(1)}) custom-call(bf16[656,128]{1,0:T(8,128)(2,1)S(1)} %copy-done.1, bf16[656,128]{1,0:T(8,128)(2,1)S(1)} %collective-permute-done.refs_1_.refs_2_.refs_6_, bf16[656,128]{1,0:T(8,128)(2,1)S(1)} %collective-permute-done.1.refs_2_.refs_3_.refs_7_, ...), custom_call_target="tpu_custom_call" | custom-call | flops 10000000 | bytes 8000000 | tf_op jit(solution)/shard_map/patch/pallas_call | solution.py:998
  36.6 0.0 copy-start.15
  36.6 4.3 %collective-permute-start.7 = (bf16[18,2,32,128]{3,2,1,0:T(8,128)(2,1)S(1)}, bf16[18,2,32,128]{3,2,1,0:T(8,128)(2,1)S(1)}, u32[]{:S(2)}, u32[]{:S(2)}) collective-permute-start(bf16[18,2,32,128]{3,2,1,0:T(8,128)(2,1)S(1)} %get-tuple-element.35), channel_id=1, source_target_pairs={{0,1},{1,2},{2,3},{3,4},{4,5},{5,6},{6,7},{7,0},{8,9},{9,10},{10,1... | collective-permute-start | bytes 884744 | tf_op jit(solution)/shard_map/ppermute | solution.py:931
  40.9 0.0 copy-done.15
  40.9 8.7 %collective-permute-start.8 = (bf16[18,2,32,128]{3,2,1,0:T(8,128)(2,1)S(1)}, bf16[18,2,32,128]{3,2,1,0:T(8,128)(2,1)S(1)}, u32[]{:S(2)}, u32[]{:S(2)}) collective-permute-start(bf16[18,2,32,128]{3,2,1,0:T(8,128)(2,1)S(1)} %get-tuple-element.36), channel_id=1, source_target_pairs={{0,7},{1,0},{2,1},{3,2},{4,3},{5,4},{6,5},{7,6},{8,15},{9,8},{10,9... | collective-permute-start | bytes 884744 | tf_op jit(solution)/shard_map/ppermute | solution.py:931
  49.6 0.0 copy-done.4
  49.6 0.0 copy-done.5
  49.6 0.0 copy-done.6
  49.6 0.0 copy-done.7
  49.6 0.0 copy-done.8
  49.6 5.5 %fill.1 = (f32[6,32,2,16,128]{4,3,2,1,0:T(8,128)}, bf16[6,176,128]{2,1,0:T(8,128)(2,1)}) custom-call(s32[64]{0:T(128)} %copy-done.15, bf16[656,128]{1,0:T(8,128)(2,1)} %get-tuple-element.23.refs_0_.refs_1_.refs_5_, bf16[656,128]{1,0:T(8,128)(2,1)} %copy-done.2, bf16[656,128]{1,0:T(8,128)(2,1)} %copy-done.3, bf16[656,128]{1,0:T(8,128)(2,1)} %copy-done.4, ...), custom_call_target="tpu_custom_call" | custom-call | flops 10000000 | bytes 10000000 | tf_op jit(solution)/shard_map/fill/pallas_call | solution.py:1023
  55.2 0.5 collective-permute-start.13
  55.7 0.0 collective-permute-start.12
  55.7 1.9 %collective-permute-start.11 = (bf16[6,176,128]{2,1,0:T(8,128)(2,1)}, bf16[6,176,128]{2,1,0:T(8,128)(2,1)S(1)}, u32[]{:S(2)}, u32[]{:S(2)}) collective-permute-start(bf16[6,176,128]{2,1,0:T(8,128)(2,1)} %get-tuple-element.37.refs_13_.refs_2_), channel_id=1, source_target_pairs={{0,2},{1,3},{2,4},{3,5},{4,6},{5,7},{6,0},{7,1},{8,10},{9,11},{10,... | collective-permute-start | bytes 811016 | tf_op jit(solution)/shard_map/ppermute | solution.py:931
  57.6 0.0 copy-done.20
  57.6 0.7 copy.12.refs_1_
  58.3 21.5 %near_sections.1 = (f32[3,5,8,64,128]{4,3,2,1,0:T(8,128)}, f32[8,128]{1,0:T(8,128)}) custom-call(s32[64]{0:T(128)} %copy-done.15, s32[64,2]{1,0:T(8,128)} %copy.12.refs_1_, s32[3]{0:T(128)} %refs_2_.7, f32[3,5,8,64,128]{4,3,2,1,0:T(8,128)} %refs_3_.5, f32[3,3,8,64,128]{4,3,2,1,0:T(8,128)} %refs_4_.5, ...), custom_call_target="tpu_custom_call" | custom-call | flops 100000000 | bytes 50000000 | tf_op jit(solution)/shard_map/near_sections/pallas_call | solution.py:893
  79.8 0.0 copy-start.9
  79.8 0.0 copy-start.14
  79.8 0.0 collective-permute-done.7.refs_1_
  79.8 0.0 collective-permute-done.8.refs_2_
  79.9 0.0 copy-start.18
  79.9 0.7 copy-done.18
  80.6 0.4 slabs.1
  81.0 0.1 collective-permute-start.9
  81.1 1.7 %collective-permute-start.10 = (bf16[864,128]{1,0:T(8,128)(2,1)S(1)}, bf16[864,128]{1,0:T(8,128)(2,1)S(1)}, u32[]{:S(2)}, u32[]{:S(2)}) collective-permute-start(bf16[864,128]{1,0:T(8,128)(2,1)S(1)} %get-tuple-element.40), channel_id=1, source_target_pairs={{0,24},{8,0},{16,8},{24,16},{1,25},{9,1},{17,9},{25,17},{2,26},{10... | collective-permute-start | bytes 663560 | tf_op jit(solution)/shard_map/ppermute | solution.py:931
  82.8 0.0 collective-permute-done.13.refs_5_.refs_16_
  82.8 0.0 collective-permute-done.12.refs_4_.refs_15_
  82.8 0.0 collective-permute-done.11.refs_3_.refs_14_
  82.8 4.1 %collective-permute-done.9.refs_3_.refs_6_ = bf16[864,128]{1,0:T(8,128)(2,1)S(1)} collective-permute-done((bf16[864,128]{1,0:T(8,128)(2,1)S(1)}, bf16[864,128]{1,0:T(8,128)(2,1)S(1)}, u32[]{:S(2)}, u32[]{:S(2)}) %collective-permute-start.9) | collective-permute-done | bytes 221216 | tf_op jit(solution)/shard_map/ppermute | solution.py:931
  86.9 0.9 collective-permute-done.10.refs_4_.refs_7_
  87.8 0.0 copy-done.9
  87.8 2.1 %pack.1 = bf16[6,176,128]{2,1,0:T(8,128)(2,1)S(1)} custom-call(s32[64]{0:T(128)S(1)} %copy-done.16, s32[64,2]{1,0:T(8,128)S(1)} %copy-done.14, bf16[6,176,128]{2,1,0:T(8,128)(2,1)S(1)} %copy-done.9, bf16[6,176,128]{2,1,0:T(8,128)(2,1)S(1)} %collective-permute-done.11.refs_3_.refs_14_, bf16[6,176,128]{2,1,0:T(8,128)(2,1)S(1)} %collective-permute-done.12.refs_4_.refs_15_, ...), custom_call_target="tpu_custom_call" | custom-call | flops 100000 | bytes 2000000 | tf_op jit(solution)/shard_map/pack/pallas_call | solution.py:1065
  89.9 0.1 collective-permute-start.14
  90.0 17.8 %off_sections.1 = (f32[5,32,16,256]{3,2,1,0:T(8,128)}, f32[8,128]{1,0:T(8,128)S(1)}) custom-call(f32[6,32,2,16,128]{4,3,2,1,0:T(8,128)S(1)} %copy-done, bf16[18,2,32,128]{3,2,1,0:T(8,128)(2,1)S(1)} %collective-permute-done.7.refs_1_, bf16[18,2,32,128]{3,2,1,0:T(8,128)(2,1)S(1)} %collective-permute-done.8.refs_2_, ...), custom_call_target="tpu_custom_call" | custom-call | flops 100000000 | bytes 50000000 | tf_op jit(solution)/shard_map/off_sections/pallas_call | solution.py:846
  107.8 0.0 copy-start.17
  107.9 0.6 copy-done.17
  108.4 0.0 collective-permute-done.14.refs_17_
  108.4 0.0 copy-done.12
  108.5 0.0 copy-done.13
  108.5 0.7 copy-done.19
  109.2 11.5 %near_edges.1 = f32[3,5,8,64,128]{4,3,2,1,0:T(8,128)} custom-call(s32[64]{0:T(128)} %copy-done.15, s32[64,2]{1,0:T(8,128)} %copy.12.refs_1_, s32[3]{0:T(128)} %refs_2_.7, f32[3,5,8,64,128]{4,3,2,1,0:T(8,128)} %refs_3_.5, f32[3,3,8,64,128]{4,3,2,1,0:T(8,128)} %refs_4_.5, ...), custom_call_target="tpu_custom_call", output_to_operand_aliasing={{}: (18, {})} | custom-call | flops 100000000 | bytes 50000000 | tf_op jit(solution)/shard_map/near_edges/pallas_call | solution.py:893
  (18 shorter events, 0.0 us)
Async XLA Ops:
  5.2 11.6 %collective-permute-start = (bf16[656,128]{1,0:T(8,128)(2,1)}, bf16[656,128]{1,0:T(8,128)(2,1)S(1)}, u32[]{:S(2)}, u32[]{:S(2)}) collective-permute-start(bf16[656,128]{1,0:T(8,128)(2,1)} %get-tuple-element.24), channel_id=1, source_target_pairs={{0,1},{1,2},{2,3},{3,4},{4,5},{5,6},{6,7},{7,0},{8,9},{9,10},{10,1... | collective-permute-start | bytes 503816 | tf_op jit(solution)/shard_map/ppermute | solution.py:931
  8.2 10.4 %collective-permute-start.1 = (bf16[656,128]{1,0:T(8,128)(2,1)}, bf16[656,128]{1,0:T(8,128)(2,1)S(1)}, u32[]{:S(2)}, u32[]{:S(2)}) collective-permute-start(bf16[656,128]{1,0:T(8,128)(2,1)} %get-tuple-element.25), channel_id=1, source_target_pairs={{0,2},{1,3},{2,4},{3,5},{4,6},{5,7},{6,0},{7,1},{8,10},{9,11},{10,... | collective-permute-start | bytes 503816 | tf_op jit(solution)/shard_map/ppermute | solution.py:931
  9.8 20.5 %collective-permute-start.2 = (bf16[656,128]{1,0:T(8,128)(2,1)}, bf16[656,128]{1,0:T(8,128)(2,1)S(1)}, u32[]{:S(2)}, u32[]{:S(2)}) collective-permute-start(bf16[656,128]{1,0:T(8,128)(2,1)} %get-tuple-element.26), channel_id=1, source_target_pairs={{0,3},{1,4},{2,5},{3,6},{4,7},{5,0},{6,1},{7,2},{8,11},{9,12},{10,... | collective-permute-start | bytes 503816 | tf_op jit(solution)/shard_map/ppermute | solution.py:931
  12.3 18.2 %collective-permute-start.3 = (bf16[656,128]{1,0:T(8,128)(2,1)}, bf16[656,128]{1,0:T(8,128)(2,1)S(1)}, u32[]{:S(2)}, u32[]{:S(2)}) collective-permute-start(bf16[656,128]{1,0:T(8,128)(2,1)} %get-tuple-element.27), channel_id=1, source_target_pairs={{0,4},{1,5},{2,6},{3,7},{4,0},{5,1},{6,2},{7,3},{8,12},{9,13},{10,... | collective-permute-start | bytes 503816 | tf_op jit(solution)/shard_map/ppermute | solution.py:931
  13.5 17.0 %collective-permute-start.4 = (bf16[656,128]{1,0:T(8,128)(2,1)}, bf16[656,128]{1,0:T(8,128)(2,1)S(1)}, u32[]{:S(2)}, u32[]{:S(2)}) collective-permute-start(bf16[656,128]{1,0:T(8,128)(2,1)} %get-tuple-element.28), channel_id=1, source_target_pairs={{0,5},{1,6},{2,7},{3,0},{4,1},{5,2},{6,3},{7,4},{8,13},{9,14},{10,... | collective-permute-start | bytes 503816 | tf_op jit(solution)/shard_map/ppermute | solution.py:931
  16.7 14.7 %copy-start.2 = (bf16[656,128]{1,0:T(8,128)(2,1)}, bf16[656,128]{1,0:T(8,128)(2,1)S(1)}, u32[]{:S(2)}) copy-start(bf16[656,128]{1,0:T(8,128)(2,1)S(1)} %collective-permute-done.refs_1_.refs_2_.refs_6_) | copy-start | bytes 503812
  16.7 13.8 %collective-permute-start.5 = (bf16[656,128]{1,0:T(8,128)(2,1)}, bf16[656,128]{1,0:T(8,128)(2,1)S(1)}, u32[]{:S(2)}, u32[]{:S(2)}) collective-permute-start(bf16[656,128]{1,0:T(8,128)(2,1)} %get-tuple-element.29), channel_id=1, source_target_pairs={{0,6},{1,7},{2,0},{3,1},{4,2},{5,3},{6,4},{7,5},{8,14},{9,15},{10,... | collective-permute-start | bytes 503816 | tf_op jit(solution)/shard_map/ppermute | solution.py:931
  18.6 12.8 %copy-start.3 = (bf16[656,128]{1,0:T(8,128)(2,1)}, bf16[656,128]{1,0:T(8,128)(2,1)S(1)}, u32[]{:S(2)}) copy-start(bf16[656,128]{1,0:T(8,128)(2,1)S(1)} %collective-permute-done.1.refs_2_.refs_3_.refs_7_) | copy-start | bytes 503812
  18.6 12.8 %copy-start.1 = (bf16[656,128]{1,0:T(8,128)(2,1)S(1)}, bf16[656,128]{1,0:T(8,128)(2,1)}, u32[]{:S(2)}) copy-start(bf16[656,128]{1,0:T(8,128)(2,1)} %get-tuple-element.23.refs_0_.refs_1_.refs_5_) | copy-start | bytes 503812
  18.6 12.8 %collective-permute-start.6 = (bf16[656,128]{1,0:T(8,128)(2,1)}, bf16[656,128]{1,0:T(8,128)(2,1)S(1)}, u32[]{:S(2)}, u32[]{:S(2)}) collective-permute-start(bf16[656,128]{1,0:T(8,128)(2,1)} %get-tuple-element.30), channel_id=1, source_target_pairs={{0,7},{1,0},{2,1},{3,2},{4,3},{5,4},{6,5},{7,6},{8,15},{9,8},{10,9... | collective-permute-start | bytes 503816 | tf_op jit(solution)/shard_map/ppermute | solution.py:931
  30.2 19.4 %copy-start.4 = (bf16[656,128]{1,0:T(8,128)(2,1)}, bf16[656,128]{1,0:T(8,128)(2,1)S(1)}, u32[]{:S(2)}) copy-start(bf16[656,128]{1,0:T(8,128)(2,1)S(1)} %collective-permute-done.2.refs_3_.refs_4_.refs_8_) | copy-start | bytes 503812
  30.5 19.1 %copy-start.5 = (bf16[656,128]{1,0:T(8,128)(2,1)}, bf16[656,128]{1,0:T(8,128)(2,1)S(1)}, u32[]{:S(2)}) copy-start(bf16[656,128]{1,0:T(8,128)(2,1)S(1)} %collective-permute-done.3.refs_4_.refs_5_.refs_9_) | copy-start | bytes 503812
  30.5 19.1 %copy-start.6 = (bf16[656,128]{1,0:T(8,128)(2,1)}, bf16[656,128]{1,0:T(8,128)(2,1)S(1)}, u32[]{:S(2)}) copy-start(bf16[656,128]{1,0:T(8,128)(2,1)S(1)} %collective-permute-done.4.refs_5_.refs_6_.refs_10_) | copy-start | bytes 503812
  30.5 19.1 %copy-start.7 = (bf16[656,128]{1,0:T(8,128)(2,1)}, bf16[656,128]{1,0:T(8,128)(2,1)S(1)}, u32[]{:S(2)}) copy-start(bf16[656,128]{1,0:T(8,128)(2,1)S(1)} %collective-permute-done.5.refs_6_.refs_7_.refs_11_) | copy-start | bytes 503812
  31.4 18.3 %copy-start.8 = (bf16[656,128]{1,0:T(8,128)(2,1)}, bf16[656,128]{1,0:T(8,128)(2,1)S(1)}, u32[]{:S(2)}) copy-start(bf16[656,128]{1,0:T(8,128)(2,1)S(1)} %collective-permute-done.6.refs_7_.refs_8_.refs_12_) | copy-start | bytes 503812
  31.4 1.3 %copy-start.10 = (f32[2,18,2,32,128]{4,3,2,1,0:T(8,128)S(1)}, f32[2,18,2,32,128]{4,3,2,1,0:T(8,128)}, u32[]{:S(2)}) copy-start(f32[2,18,2,32,128]{4,3,2,1,0:T(8,128)} %get-tuple-element.31.refs_8_) | copy-start | bytes 3538948
  32.7 24.8 %copy-start.20 = (s32[64,2]{0,1:T(2,128)S(1)}, s32[64,2]{0,1:T(2,128)}, u32[]{:S(2)}) copy-start(s32[64,2]{0,1:T(2,128)} %param.13) | copy-start | bytes 1540
  36.6 4.4 %copy-start.15 = (s32[64]{0:T(128)}, s32[64]{0:T(128)S(1)}, u32[]{:S(2)}) copy-start(s32[64]{0:T(128)S(1)} %get-tuple-element.32.refs_0_) | copy-start | bytes 772
  36.6 43.2 %collective-permute-start.7 = (bf16[18,2,32,128]{3,2,1,0:T(8,128)(2,1)S(1)}, bf16[18,2,32,128]{3,2,1,0:T(8,128)(2,1)S(1)}, u32[]{:S(2)}, u32[]{:S(2)}) collective-permute-start(bf16[18,2,32,128]{3,2,1,0:T(8,128)(2,1)S(1)} %get-tuple-element.35), channel_id=1, source_target_pairs={{0,1},{1,2},{2,3},{3,4},{4,5},{5,6},{6,7},{7,0},{8,9},{9,10},{10,1... | collective-permute-start | bytes 884744 | tf_op jit(solution)/shard_map/ppermute | solution.py:931
  40.9 38.9 %collective-permute-start.8 = (bf16[18,2,32,128]{3,2,1,0:T(8,128)(2,1)S(1)}, bf16[18,2,32,128]{3,2,1,0:T(8,128)(2,1)S(1)}, u32[]{:S(2)}, u32[]{:S(2)}) collective-permute-start(bf16[18,2,32,128]{3,2,1,0:T(8,128)(2,1)S(1)} %get-tuple-element.36), channel_id=1, source_target_pairs={{0,7},{1,0},{2,1},{3,2},{4,3},{5,4},{6,5},{7,6},{8,15},{9,8},{10,9... | collective-permute-start | bytes 884744 | tf_op jit(solution)/shard_map/ppermute | solution.py:931
  55.2 27.7 %collective-permute-start.13 = (bf16[6,176,128]{2,1,0:T(8,128)(2,1)}, bf16[6,176,128]{2,1,0:T(8,128)(2,1)S(1)}, u32[]{:S(2)}, u32[]{:S(2)}) collective-permute-start(bf16[6,176,128]{2,1,0:T(8,128)(2,1)} %get-tuple-element.37.refs_13_.refs_2_), channel_id=1, source_target_pairs={{0,6},{1,7},{2,0},{3,1},{4,2},{5,3},{6,4},{7,5},{8,14},{9,15},{10,... | collective-permute-start | bytes 811016 | tf_op jit(solution)/shard_map/ppermute | solution.py:931
  55.7 27.1 %collective-permute-start.12 = (bf16[6,176,128]{2,1,0:T(8,128)(2,1)}, bf16[6,176,128]{2,1,0:T(8,128)(2,1)S(1)}, u32[]{:S(2)}, u32[]{:S(2)}) collective-permute-start(bf16[6,176,128]{2,1,0:T(8,128)(2,1)} %get-tuple-element.37.refs_13_.refs_2_), channel_id=1, source_target_pairs={{0,4},{1,5},{2,6},{3,7},{4,0},{5,1},{6,2},{7,3},{8,12},{9,13},{10,... | collective-permute-start | bytes 811016 | tf_op jit(solution)/shard_map/ppermute | solution.py:931
  55.7 27.1 %collective-permute-start.11 = (bf16[6,176,128]{2,1,0:T(8,128)(2,1)}, bf16[6,176,128]{2,1,0:T(8,128)(2,1)S(1)}, u32[]{:S(2)}, u32[]{:S(2)}) collective-permute-start(bf16[6,176,128]{2,1,0:T(8,128)(2,1)} %get-tuple-element.37.refs_13_.refs_2_), channel_id=1, source_target_pairs={{0,2},{1,3},{2,4},{3,5},{4,6},{5,7},{6,0},{7,1},{8,10},{9,11},{10,... | collective-permute-start | bytes 811016 | tf_op jit(solution)/shard_map/ppermute | solution.py:931
  58.3 21.6 %copy-start = (f32[6,32,2,16,128]{4,3,2,1,0:T(8,128)S(1)}, f32[6,32,2,16,128]{4,3,2,1,0:T(8,128)}, u32[]{:S(2)}) copy-start(f32[6,32,2,16,128]{4,3,2,1,0:T(8,128)} %get-tuple-element.34.refs_0_) | copy-start | bytes 9437188
  79.8 8.0 %copy-start.9 = (bf16[6,176,128]{2,1,0:T(8,128)(2,1)S(1)}, bf16[6,176,128]{2,1,0:T(8,128)(2,1)}, u32[]{:S(2)}) copy-start(bf16[6,176,128]{2,1,0:T(8,128)(2,1)} %get-tuple-element.37.refs_13_.refs_2_) | copy-start | bytes 811012
  79.8 8.0 %copy-start.14 = (s32[64,2]{1,0:T(8,128)S(1)}, s32[64,2]{1,0:T(8,128)}, u32[]{:S(2)}) copy-start(s32[64,2]{1,0:T(8,128)} %copy.12.refs_1_) | copy-start | bytes 1540
  79.8 8.0 %copy-start.16 = (s32[64]{0:T(128)S(1)}, s32[64]{0:T(128)}, u32[]{:S(2)}) copy-start(s32[64]{0:T(128)} %copy-done.15) | copy-start | bytes 772
  79.9 0.7 copy-start.18
  81.0 5.9 %collective-permute-start.9 = (bf16[864,128]{1,0:T(8,128)(2,1)S(1)}, bf16[864,128]{1,0:T(8,128)(2,1)S(1)}, u32[]{:S(2)}, u32[]{:S(2)}) collective-permute-start(bf16[864,128]{1,0:T(8,128)(2,1)S(1)} %get-tuple-element.39), channel_id=1, source_target_pairs={{0,8},{8,16},{16,24},{24,0},{1,9},{9,17},{17,25},{25,1},{2,10},{10... | collective-permute-start | bytes 663560 | tf_op jit(solution)/shard_map/ppermute | solution.py:931
  81.1 6.7 %collective-permute-start.10 = (bf16[864,128]{1,0:T(8,128)(2,1)S(1)}, bf16[864,128]{1,0:T(8,128)(2,1)S(1)}, u32[]{:S(2)}, u32[]{:S(2)}) collective-permute-start(bf16[864,128]{1,0:T(8,128)(2,1)S(1)} %get-tuple-element.40), channel_id=1, source_target_pairs={{0,24},{8,0},{16,8},{24,16},{1,25},{9,1},{17,9},{25,17},{2,26},{10... | collective-permute-start | bytes 663560 | tf_op jit(solution)/shard_map/ppermute | solution.py:931
  82.8 25.6 %copy-start.11 = (bf16[6,176,128]{2,1,0:T(8,128)(2,1)}, bf16[6,176,128]{2,1,0:T(8,128)(2,1)S(1)}, u32[]{:S(2)}) copy-start(bf16[6,176,128]{2,1,0:T(8,128)(2,1)S(1)} %collective-permute-done.13.refs_5_.refs_16_) | copy-start | bytes 811012
  82.8 25.6 %copy-start.12 = (bf16[6,176,128]{2,1,0:T(8,128)(2,1)}, bf16[6,176,128]{2,1,0:T(8,128)(2,1)S(1)}, u32[]{:S(2)}) copy-start(bf16[6,176,128]{2,1,0:T(8,128)(2,1)S(1)} %collective-permute-done.12.refs_4_.refs_15_) | copy-start | bytes 811012
  82.8 25.6 %copy-start.13 = (bf16[6,176,128]{2,1,0:T(8,128)(2,1)}, bf16[6,176,128]{2,1,0:T(8,128)(2,1)S(1)}, u32[]{:S(2)}) copy-start(bf16[6,176,128]{2,1,0:T(8,128)(2,1)S(1)} %collective-permute-done.11.refs_3_.refs_14_) | copy-start | bytes 811012
  89.9 18.5 %collective-permute-start.14 = (bf16[6,176,128]{2,1,0:T(8,128)(2,1)S(1)}, bf16[6,176,128]{2,1,0:T(8,128)(2,1)S(1)}, u32[]{:S(2)}, u32[]{:S(2)}) collective-permute-start(bf16[6,176,128]{2,1,0:T(8,128)(2,1)S(1)} %pack.1), channel_id=1, source_target_pairs={{0,1},{1,0},{2,3},{3,2},{4,5},{5,4},{6,7},{7,6},{8,9},{9,8},{10,11... | collective-permute-start | bytes 811016 | tf_op jit(solution)/shard_map/ppermute | solution.py:1075
  107.8 0.6 copy-start.17
  108.4 0.7 copy-start.19

commit v2 on v1

--- a/solution.py
+++ b/solution.py
@@ -24,7 +24,7 @@
 FACE_ROWS = FACE_LAYERS * TW
 LAG = 2
 RINGS = 4
-VMEM_MIB = 56
+VMEM_MIB = 61
 FRONT = 6
 
 VMEM = pltpu.VMEM
@@ -115,7 +115,7 @@
 
 
 def base_kernel(slots, dims, refs):
-    off_ref, near_ref, metric_ref, layers, faces, edge, medge, sems = refs
+    off_ref, near_ref, metric_ref, layers, faces, placed, edge, medge, sems = refs
     around, nx, ny, nz = dims
     loads = []
     for end, start in enumerate((0, around - TW)):
@@ -127,6 +127,10 @@
             )
     for copy in loads:
         copy.start()
+
+    for h in range(nz // TL):
+        placed[0:FIELDS, :, h] = off_ref[:, :, :, h * TL : (h + 1) * TL]
+    placed[FIELDS] = jnp.full(placed.shape[1:], TIME_STEP, jnp.float32)
 
     def turn(x, _):
         for end, start in enumerate((0, ny - DEPTH)):
@@ -163,52 +167,78 @@
             )
 
 
-def patch_kernel(count, dims, refs):
+def patch_kernel(count, per_slot, dims, refs):
     parcels = refs[:count]
-    base_layers, y_low, y_high, table = refs[count : count + 4]
-    layers, tiles, wide, head_v, head_s, sems = refs[count + 4 :]
+    base_layers, base_faces, _, y_low, y_high, faces, table, placed = refs[count : count + 8]
+    layers, front, tiles, wide, near_wide, nothing, head_v, head_s, sems, out_sems = refs[count + 8 :]
     nx, ny, nz = dims
     y_tiles, z_tiles = ny // TW, nz // TL
     lines = FIELDS * TW * TW
     heads = [
         pltpu.make_async_copy(
             parcels[j].at[pl.ds(2 * lines, META), :],
-            tiles.at[j, pl.ds(lines, META), :],
+            tiles.at[j, pl.ds(2 * lines, META), :],
             sems.at[j],
         )
         for j in range(count)
     ]
     bodies = [
         pltpu.make_async_copy(
-            parcels[j].at[pl.ds(0, lines), :],
-            tiles.at[j, pl.ds(0, lines), :],
+            parcels[j].at[pl.ds(0, 2 * lines), :],
+            tiles.at[j, pl.ds(0, 2 * lines), :],
             sems.at[count + j],
         )
         for j in range(count)
     ]
-    load = pltpu.make_async_copy(base_layers, layers, sems.at[2 * count])
-    for copy in heads + bodies + [load]:
+    rest = [
+        pltpu.make_async_copy(base_layers, layers, sems.at[2 * count]),
+        pltpu.make_async_copy(base_faces, front, sems.at[2 * count + 1]),
+    ]
+    for copy in heads + bodies + rest:
         copy.start()
+    nothing[...] = jnp.zeros(nothing.shape, jnp.float32)
     for j in range(count):
         heads[j].wait()
-        head = tiles[j, lines:, :].astype(jnp.float32)
+        head = tiles[j, 2 * lines :, :].astype(jnp.float32)
         head_v[j * META : (j + 1) * META, :] = head.astype(jnp.int32)
-    head_copy = pltpu.make_async_copy(head_v, head_s, sems.at[2 * count + 1])
+    head_copy = pltpu.make_async_copy(head_v, head_s, sems.at[2 * count + 2])
     head_copy.start()
     for j in range(count):
         bodies[j].wait()
         wide[j] = tiles[j, :lines, :].astype(jnp.float32)
-    load.wait()
+    for copy in rest:
+        copy.wait()
     head_copy.wait()
     for j in range(count):
         for r in range(RING):
             table[j * RING + r] = head_s[j * META + r, 0]
-    for j in range(count):
+
+    def tile_place(j):
         tile = head_s[j * META, 0]
         a = tile // (y_tiles * z_tiles)
         b = (tile // z_tiles) % y_tiles
-        h = tile % z_tiles
-        x0 = aligned(a, TW)
+        return tile, aligned(a, TW), b, tile % z_tiles
+
+    def tile_copies(j):
+        tile, x0, b, h = tile_place(j)
+        at = (pl.ds(x0, TW), h, pl.ds(aligned(b, TW), TW), slice(None))
+        return [
+            pltpu.make_async_copy(
+                wide.at[j].reshape(FIELDS, TW, TW, TL),
+                placed.at[(pl.ds(0, FIELDS),) + at],
+                out_sems.at[0, j],
+            ),
+            pltpu.make_async_copy(nothing, placed.at[(FIELDS,) + at], out_sems.at[1, j]),
+        ]
+
+    for j in range(count):
+        tile, x0, b, h = tile_place(j)
+
+        @pl.when(tile >= 0)
+        def _():
+            for copy in tile_copies(j):
+                copy.start()
+
         for end, edge_tile in enumerate((0, y_tiles - 1)):
 
             @pl.when((tile >= 0) & (b == edge_tile))
@@ -223,8 +253,30 @@
                         (TW, TL), jnp.float32
                     )
 
+        tile = head_s[j * META + 1, 0]
+        s = tile // per_slot
+        for end, edge_tile in enumerate((0, per_slot - 1)):
+
+            @pl.when((tile >= 0) & (tile % per_slot == edge_tile))
+            def _():
+                near_wide[...] = tiles[j, lines : 2 * lines, :].astype(jnp.float32)
+                first = 0 if end == 0 else TW - DEPTH
+                for c in range(FIELDS):
+                    for d in range(DEPTH):
+                        slab = near_wide[pl.ds(c * TW * TW + first + d, TW, stride=TW), :]
+                        number = c * DEPTH + d
+                        front[s * 2 + end, number * TW : (number + 1) * TW, :] = slab - CENTRE[c]
+                front[s * 2 + end, FACE_ROWS - TW :, :] = jnp.zeros((TW, TL), jnp.float32)
+
     for end, out in enumerate((y_low, y_high)):
         out[...] = layers[end].astype(jnp.bfloat16)
+    faces[...] = front[...].astype(jnp.bfloat16)
+    for j in range(count):
+
+        @pl.when(head_s[j * META, 0] >= 0)
+        def _():
+            for copy in tile_copies(j):
+                copy.wait()
 
 
 def face_slab(ref, lead, layer):
@@ -234,58 +286,6 @@
         line = jnp.broadcast_to(ref[lead + (i, slice(layer, layer + 1), slice(None))], (TW, TL))
         slab = line if slab is None else jnp.where(row == i, line, slab)
     return slab
-
-
-def fill_kernel(count, per_slot, dims, refs):
-    table = refs[0]
-    parcels = refs[1 : 1 + count]
-    off_ref, base_faces, placed, faces = refs[1 + count : 5 + count]
-    tiles, wide, front, sems = refs[5 + count :]
-    nx, ny, nz = dims
-    y_tiles, z_tiles = ny // TW, nz // TL
-    lines = FIELDS * TW * TW
-    loads = [pltpu.make_async_copy(parcels[j], tiles.at[j], sems.at[j]) for j in range(count)]
-    loads.append(pltpu.make_async_copy(base_faces, front, sems.at[count]))
-    for copy in loads:
-        copy.start()
-    for h in range(z_tiles):
-        placed[0:FIELDS, :, h] = off_ref[:, :, :, h * TL : (h + 1) * TL]
-    placed[FIELDS] = jnp.full(placed.shape[1:], TIME_STEP, jnp.float32)
-    for copy in loads:
-        copy.wait()
-    for j in range(count):
-        tile = table[j * RING + 1]
-        s = tile // per_slot
-        for end, edge_tile in enumerate((0, per_slot - 1)):
-
-            @pl.when((tile >= 0) & (tile % per_slot == edge_tile))
-            def _():
-                wide[...] = tiles[j, lines : 2 * lines, :].astype(jnp.float32)
-                first = 0 if end == 0 else TW - DEPTH
-                for c in range(FIELDS):
-                    for d in range(DEPTH):
-                        slab = wide[pl.ds(c * TW * TW + first + d, TW, stride=TW), :]
-                        number = c * DEPTH + d
-                        front[s * 2 + end, number * TW : (number + 1) * TW, :] = slab - CENTRE[c]
-                front[s * 2 + end, FACE_ROWS - TW :, :] = jnp.zeros((TW, TL), jnp.float32)
-
-    faces[...] = front[...].astype(jnp.bfloat16)
-    for j in range(count):
-        tile = table[j * RING]
-
-        @pl.when(tile >= 0)
-        def _():
-            x0 = (tile // (y_tiles * z_tiles)) * TW
-            y0 = aligned((tile // z_tiles) % y_tiles, TW)
-            h = tile % z_tiles
-            for c in range(FIELDS):
-                for i in range(0, TW, 2):
-                    start = (c * TW + i) * TW
-                    pair = tiles[j, start : start + 2 * TW, :].astype(jnp.float32)
-                    for k in range(2):
-                        placed[c, x0 + i + k, h, pl.ds(y0, TW), :] = pair[k * TW : (k + 1) * TW]
-            for i in range(TW):
-                placed[FIELDS, x0 + i, h, pl.ds(y0, TW), :] = jnp.zeros((TW, TL), jnp.float32)
 
 
 def ghost_rows(low, high, c, h, x, scale):
@@ -351,12 +351,12 @@
     return f, flux
 
 
-def off_kernel(dims, refs):
-    placed, from_low, from_high, from_left, from_right = refs[:5]
-    out, token = refs[5:7]
-    layers, slabs, wide, begin, state_one, state_two, sems = refs[7:14]
-    flux_x, flux_y, f_s = refs[14:18], refs[18:22], refs[22:26]
-    up_z, down_z = refs[26:30], refs[30:34]
+def off_sections(dims, inputs, out_ref, scratch):
+    placed, from_low, from_high, from_left, from_right = inputs
+    out, layers, slabs, wide, begin, state_one, state_two, sems = scratch[:8]
+    rings = scratch[8:]
+    flux_x, flux_y, f_s = rings[:4], rings[4:8], rings[8:12]
+    up_z, down_z = rings[12:16], rings[16:20]
     nx, ny, nz = dims
     halves = nz // TL
     rows = ny + RING
@@ -364,7 +364,6 @@
     load = pltpu.make_async_copy(
         placed, begin.at[:, pl.ds(main, nx), :, pl.ds(0, ny), :], sems.at[0]
     )
-    load.start()
     low, high = wide.at[0], wide.at[1]
     received = [
         pltpu.make_async_copy(source, target, sems.at[1 + k])
@@ -377,9 +376,6 @@
             )
         )
     ]
-    for copy in received:
-        copy.start()
-    token[...] = jnp.zeros(token.shape, jnp.float32)
     lane = lax.broadcasted_iota(jnp.int32, (TW, TL), 1)
     first_lane, last_lane = lane == 0, lane == TL - 1
 
@@ -387,6 +383,10 @@
         rolled = [pltpu.roll(part, distance % TL, 1) for part in parts]
         return [jnp.where(mask, rolled[(h - distance) % halves], rolled[h]) for h in range(halves)]
 
+    store = pltpu.make_async_copy(out, out_ref, sems.at[5])
+    for copy in received + [load]:
+        copy.start()
+    yield
     for copy in received:
         copy.wait()
     wide[...] = layers[...].astype(jnp.float32)
@@ -482,6 +482,11 @@
 
         lax.fori_loop(0, turns, body, 0)
 
+    store.start()
+    yield
+    store.wait()
+    yield
+
 
 def find(table, count, slots, block):
     where_j, where_t = jnp.int32(0), jnp.int32(0)
@@ -497,46 +502,42 @@
     table, block_faces = refs[:2]
     held = refs[2 : 2 + count // 2]
     packed, sems = refs[4 + count // 2 :]
+    for finish in (False, True):
+        pack(count, slots, table, block_faces, held, packed, sems, finish)
+
+
+def pack(count, slots, table, block_faces, held, packed, sems, finish):
     me = lax.axis_index("gy")
     offset = jnp.where(lax.rem(me, 2) == 1, 1, count - 1)
-    for phase in range(2):
-        for s in range(slots):
-            block = table[offset * RING + 2 + s]
-
-            @pl.when(block >= 0)
-            def _():
-                for side in range(2):
-                    j, t = find(table, count, slots, block_faces[block, side])
-                    for m in range(count // 2):
-
-                        @pl.when(j == 2 * m)
-                        def _():
-                            number = s * 2 + side
-                            copy = pltpu.make_async_copy(
-                                held[m].at[t * 2 + 1 - side], packed.at[number], sems.at[number]
-                            )
-                            if phase == 0:
-                                copy.start()
-                            else:
-                                copy.wait()
-
-
-def near_kernel(count, slots, dims, edges, refs):
+    for s in range(slots):
+        block = table[offset * RING + 2 + s]
+
+        @pl.when(block >= 0)
+        def _():
+            for side in range(2):
+                j, t = find(table, count, slots, block_faces[side, block])
+                number = s * 2 + side
+                for m in range(count // 2):
+
+                    @pl.when(j == 2 * m)
+                    def _():
+                        copy = pltpu.make_async_copy(
+                            held[m].at[t * 2 + 1 - side], packed.at[number], sems.at[number]
+                        )
+                        if finish:
+                            copy.wait()
+                        else:
+                            copy.start()
+
+
+def near_sections(count, slots, dims, edges, inputs, out_ref, scratch):
     per_slot, around, normal = dims
-    table, block_faces, slot_ref, near_ref, metric_ref = refs[:5]
-    parcels = refs[5 : 5 + count]
-    refs = refs[5 + count :]
+    table, block_faces, slot_ref, near_ref, metric_ref = inputs[:5]
+    parcels, rest = inputs[5 : 5 + count], inputs[5 + count :]
     if edges:
-        held, packed, main_ref = refs[: count // 2], refs[count // 2], refs[count // 2 + 1]
-        out_ref = refs[count // 2 + 3]
-        scratch = refs[count // 2 + 4 :]
-        own = 2 * TW
-        rows = own + RING
-    else:
-        out_ref, token = refs[1:3]
-        scratch = refs[3:]
-        token[...] = jnp.zeros(token.shape, jnp.float32)
-        own = rows = around
+        held, packed, main_ref = rest[: count // 2], rest[count // 2], rest[count // 2 + 1]
+    own = 2 * TW if edges else around
+    rows = own + RING if edges else own
     begins, metrics, state_one, state_two, square, coeff, hold, out, along = scratch[:9]
     tile_buf, in_sems, out_sems, tile_sems = scratch[9:13]
     rings = scratch[13:37]
@@ -601,7 +602,7 @@
 
     def face_loads(s):
         for side in range(2):
-            j, t = find(table, count, slots, block_faces[slot_ref[s], side])
+            j, t = find(table, count, slots, block_faces[side, slot_ref[s]])
             target, sem = face_buf.at[s, side], face_sems.at[s, side]
             for m in range(count // 2):
 
@@ -622,8 +623,7 @@
                 for copy in main_loads(s):
                     copy.start()
 
-    for copy in tile_loads:
-        copy.wait()
+    yield
     row = lax.broadcasted_iota(jnp.int32, (RING, TL), 0)
 
     def take_ghosts(s, begin, metric):
@@ -683,6 +683,7 @@
             if edges:
                 for copy in main_loads(s):
                     copy.wait()
+
             for j in range(count):
                 tile = table[j * RING + 1]
                 number = tile % per_slot
@@ -817,7 +818,10 @@
             send_out()
         return 0
 
+    for copy in tile_loads:
+        copy.wait()
     lax.fori_loop(0, slots, slot_work, 0)
+    yield
     for s in range(slots):
 
         def end_out():
@@ -828,6 +832,28 @@
             pl.when(slot_ref[s] >= 0)(end_out)
         else:
             end_out()
+    yield
+
+
+def near_kernel(count, slots, dims, refs):
+    inputs, (out_ref, token) = refs[: 5 + count], refs[6 + count : 8 + count]
+    token[...] = jnp.zeros(token.shape, jnp.float32)
+    for _ in near_sections(count, slots, dims, False, inputs, out_ref, refs[8 + count :]):
+        pass
+
+
+def edge_kernel(count, slots, dims, refs):
+    size = 5 + count + count // 2 + 2
+    out_ref, scratch = refs[size + 1], refs[size + 2 :]
+    for _ in near_sections(count, slots, dims, True, refs[:size], out_ref, scratch):
+        pass
+
+
+def off_kernel(dims, refs):
+    out_ref, token = refs[6:8]
+    token[...] = jnp.zeros(token.shape, jnp.float32)
+    for _ in off_sections(dims, refs[:5], out_ref, refs[8:]):
+        pass
 
 
 def packed_refs(kernel, *first):
@@ -837,49 +863,37 @@
     return body
 
 
-def off_call(placed, from_low, from_high, from_left, from_right):
-    _, nx, halves, ny, _ = placed.shape
-    nz = halves * TL
-    f32, shape = jnp.float32, jax.ShapeDtypeStruct
-    rows = ny + RING
+def off_buffers(dims, layer_shape, slab_shape):
+    nx, ny, nz = dims
+    halves, rows = nz // TL, ny + RING
+    f32, half = jnp.float32, jnp.bfloat16
     slices = FRONT + nx + 2 * DEPTH + 2
-    return pl.pallas_call(
-        packed_refs(off_kernel, (nx, ny, nz)),
-        out_shape=[shape((FIELDS, nx, ny, nz), f32), shape((RING, TL), f32)],
-        in_specs=[any_spec()] * 5,
-        out_specs=[vmem_spec()] * 2,
-        scratch_shapes=[
-            VMEM((2,) + from_low.shape, jnp.bfloat16),
-            VMEM((2,) + from_left.shape, jnp.bfloat16),
-            VMEM((2,) + from_low.shape, f32),
+    return (
+        [
+            VMEM((FIELDS, nx, ny, nz), f32),
+            VMEM((2,) + layer_shape, half),
+            VMEM((2,) + slab_shape, half),
+            VMEM((2,) + layer_shape, f32),
             VMEM((FIELDS + 1, slices, halves, rows, TL), f32),
             VMEM((FIELDS, slices, halves, rows, TL), f32),
             VMEM((FIELDS, slices, halves, rows, TL), f32),
-            pltpu.SemaphoreType.DMA((5,)),
+            pltpu.SemaphoreType.DMA((6,)),
         ]
         + [VMEM((FIELDS, halves, rows, TL), f32)] * RINGS
         + [VMEM((FIELDS, halves, rows + 2 * TW, TL), f32)] * RINGS
         + [VMEM((FIELDS - 1, halves, rows + 2 * TW, TL), f32)] * RINGS
-        + [VMEM((FIELDS, halves, rows, TL), f32)] * RINGS * 2,
-        compiler_params=params(40),
-        cost_estimate=cost(1e8, 5e7),
-        name="off_sections",
-    )(placed, from_low, from_high, from_left, from_right)
-
-
-def near_call(table, block_faces, slot_block, near_state, near_metric, parcels, edges, after):
-    count = len(parcels)
-    slots, _, normal, around, _ = near_state.shape
-    f32, shape = jnp.float32, jax.ShapeDtypeStruct
-    dma = pltpu.SemaphoreType.DMA
+        + [VMEM((FIELDS, halves, rows, TL), f32)] * RINGS * 2
+    )
+
+
+def near_buffers(count, slots, dims, edges):
+    _, around, normal = dims
+    f32, dma = jnp.float32, pltpu.SemaphoreType.DMA
     own = 2 * TW if edges else around
     rows = own + RING if edges else own
     pieces = 2 if edges else 1
-    out_shape = [shape(near_state.shape, f32)]
-    out_specs = [any_spec()]
-    extra, aliases = [], {}
+    extra = []
     if edges:
-        aliases = {5 + count + count // 2 + 1: 0}
         extra = [
             VMEM((2, FACE_ROWS, TL), f32),
             VMEM((slots, 2, FACE_ROWS, TL), jnp.bfloat16),
@@ -887,16 +901,8 @@
             dma((slots, 2)),
             dma((slots, 2)),
         ]
-    else:
-        out_shape.append(shape((RING, TL), f32))
-        out_specs.append(vmem_spec())
-    return pl.pallas_call(
-        packed_refs(near_kernel, count, slots, (around // TW, around, normal), edges),
-        out_shape=out_shape,
-        in_specs=[smem_spec()] * 3 + [any_spec()] * (2 + count + len(after)),
-        out_specs=out_specs,
-        input_output_aliases=aliases,
-        scratch_shapes=[
+    return (
+        [
             VMEM((2, FIELDS, normal, rows, TL), f32),
             VMEM((2, 3, normal, rows, TL), f32),
             VMEM((FIELDS, normal, rows, TL), f32),
@@ -915,11 +921,8 @@
         + [VMEM((FIELDS, rows + 2 * TW, TL), f32)] * RINGS
         + [VMEM((FIELDS - 1, rows + 2 * TW, TL), f32)] * RINGS
         + [VMEM((FIELDS, rows, TL), f32)] * RINGS * 3
-        + extra,
-        compiler_params=params(VMEM_MIB),
-        cost_estimate=cost(1e8, 5e7),
-        name="near_edges" if edges else "near_sections",
-    )(table, block_faces, slot_block, near_state, near_metric, *parcels, *after)
+        + extra
+    )
 
 
 def ring(axis, distance):
@@ -950,6 +953,7 @@
     lines = FIELDS * TW * TW
     half, f32 = jnp.bfloat16, jnp.float32
     shape = jax.ShapeDtypeStruct
+    block_faces = block_faces.T
     tile_buf = VMEM((count, FIELDS, TW, TW, TL), f32)
     map_buf = VMEM((count, TL, TL), half)
 
@@ -975,14 +979,15 @@
     planes = (FIELDS + 1) * DEPTH
     halves = nz // TL
     layer_shape = (planes, halves, nx, TL)
-    base_layers, base_faces = pl.pallas_call(
+    base_layers, base_faces, base_placed = pl.pallas_call(
         packed_refs(base_kernel, slots, (around, nx, ny, nz)),
         out_shape=[
             shape((2,) + layer_shape, f32),
             shape((2 * slots, FACE_ROWS, TL), f32),
+            shape((FIELDS + 1, nx, halves, ny, TL), f32),
         ],
         in_specs=[vmem_spec()] + [any_spec()] * 2,
-        out_specs=[vmem_spec()] * 2,
+        out_specs=[vmem_spec()] * 3,
         scratch_shapes=[
             VMEM((2, slots, FIELDS, normal, TW, TL), f32),
             VMEM((2, slots, 3, normal, TW, TL), f32),
@@ -995,57 +1000,56 @@
 
     parcels = [parcels[0]] + [send(parcels[j], "gy", j) for j in range(1, count)]
 
-    y_low, y_high, table = pl.pallas_call(
-        packed_refs(patch_kernel, count, (nx, ny, nz)),
+    y_low, y_high, faces, table, placed = pl.pallas_call(
+        packed_refs(patch_kernel, count, per_slot, (nx, ny, nz)),
         out_shape=[
             shape(layer_shape, half),
             shape(layer_shape, half),
+            shape((2 * slots, FACE_ROWS, TL), half),
             shape((count * RING,), jnp.int32),
+            shape(base_placed.shape, f32),
         ],
-        in_specs=[any_spec()] * (count + 1),
-        out_specs=[vmem_spec()] * 2 + [smem_spec()],
+        in_specs=[any_spec()] * (count + 3),
+        out_specs=[vmem_spec()] * 3 + [smem_spec(), any_spec()],
+        input_output_aliases={count + 2: 4},
         scratch_shapes=[
             VMEM((2,) + layer_shape, f32),
-            VMEM((count, lines + META, TL), half),
+            VMEM((2 * slots, FACE_ROWS, TL), f32),
+            VMEM((count, 2 * lines + META, TL), half),
             VMEM((count, lines, TL), f32),
+            VMEM((lines, TL), f32),
+            VMEM((TW, TW, TL), f32),
             VMEM((count * META, TL), jnp.int32),
             SMEM((count * META, TL), jnp.int32),
-            dma((2 * count + 2,)),
+            dma((2 * count + 3,)),
+            dma((2, count)),
         ],
-        compiler_params=params(12),
+        compiler_params=params(VMEM_MIB),
         cost_estimate=cost(1e7, 8e6),
         name="patch",
-    )(*parcels, base_layers)
-
+    )(*parcels, base_layers, base_faces, base_placed)
+
+    held = [faces] + [send(faces, "gy", 2 * m) for m in range(1, count // 2)]
     from_low = send(y_high, "gy", 1)
     from_high = send(y_low, "gy", count - 1)
 
-    placed, faces = pl.pallas_call(
-        packed_refs(fill_kernel, count, per_slot, (nx, ny, nz)),
-        out_shape=[
-            shape((FIELDS + 1, nx, halves, ny, TL), f32),
-            shape((2 * slots, FACE_ROWS, TL), half),
-        ],
-        in_specs=[smem_spec()] + [any_spec()] * count + [vmem_spec()] + [any_spec()],
-        out_specs=[vmem_spec()] * 2,
-        scratch_shapes=[
-            VMEM((count, 2 * lines + META, TL), half),
-            VMEM((lines, TL), f32),
-            VMEM((2 * slots, FACE_ROWS, TL), f32),
-            dma((count + 1,)),
-        ],
+    near_dims, off_dims = (per_slot, around, normal), (nx, ny, nz)
+    near_inputs = (table, block_faces, slot_block, near_state, near_metric, *parcels)
+    token_shape = shape((RING, TL), f32)
+
+    near_main, token = pl.pallas_call(
+        packed_refs(near_kernel, count, slots, near_dims),
+        out_shape=[shape(near_state.shape, f32), token_shape],
+        in_specs=[smem_spec()] * 3 + [any_spec()] * (2 + count + 1),
+        out_specs=[any_spec(), vmem_spec()],
+        scratch_shapes=near_buffers(count, slots, near_dims, False),
         compiler_params=params(VMEM_MIB),
-        cost_estimate=cost(1e7, 1e7),
-        name="fill",
-    )(table, *parcels, off_state, base_faces)
-    held = [faces] + [send(faces, "gy", 2 * m) for m in range(1, count // 2)]
-
-    near_main, near_token = near_call(
-        table, block_faces, slot_block, near_state, near_metric, parcels, False, [faces]
-    )
+        cost_estimate=cost(1e8, 5e7),
+        name="near_sections",
+    )(*near_inputs, faces)
 
     x_low, x_high = pl.pallas_call(
-        packed_refs(slab_kernel, (nx, ny, nz)),
+        packed_refs(slab_kernel, off_dims),
         out_shape=[shape((planes * halves * (ny + RING), TL), half)] * 2,
         in_specs=[any_spec()] * 4,
         out_specs=[vmem_spec()] * 2,
@@ -1055,30 +1059,48 @@
             VMEM((2, FIELDS + 1, DEPTH, halves, ny, TL), f32),
             dma((4,)),
         ],
-        compiler_params=params(8),
+        compiler_params=params(VMEM_MIB),
         cost_estimate=cost(1e6, 4e6),
         name="slabs",
-    )(placed, from_low, from_high, near_token)
+    )(placed, from_low, from_high, token)
     from_left = send(x_high, "gx", 1)
     from_right = send(x_low, "gx", lax.axis_size("gx") - 1)
 
-    packed = pl.pallas_call(
+    packed_here = pl.pallas_call(
         packed_refs(pack_kernel, count, slots),
         out_shape=shape((2 * slots, FACE_ROWS, TL), half),
         in_specs=[smem_spec()] * 2 + [any_spec()] * (count // 2 + 2),
-        out_specs=any_spec(),
+        out_specs=vmem_spec(),
         scratch_shapes=[dma((2 * slots,))],
-        compiler_params=params(4),
+        compiler_params=params(VMEM_MIB),
         cost_estimate=cost(1e5, 2e6),
         name="pack",
     )(table, block_faces, *held, from_left, from_right)
-    packed = lax.ppermute(packed, "gy", [(i, i ^ 1) for i in range(count)])
-
-    off_next, off_token = off_call(placed, from_low, from_high, from_left, from_right)
-    after = [*held, packed, near_main, off_token]
-    (near_next,) = near_call(
-        table, block_faces, slot_block, near_state, near_metric, parcels, True, after
-    )
+    packed = lax.ppermute(packed_here, "gy", [(i, i ^ 1) for i in range(count)])
+
+    off_next, token = pl.pallas_call(
+        packed_refs(off_kernel, off_dims),
+        out_shape=[shape(off_state.shape, f32), token_shape],
+        in_specs=[any_spec()] * 6,
+        out_specs=[any_spec(), vmem_spec()],
+        scratch_shapes=off_buffers(off_dims, layer_shape, x_low.shape),
+        compiler_params=params(VMEM_MIB),
+        cost_estimate=cost(1e8, 5e7),
+        name="off_sections",
+    )(placed, from_low, from_high, from_left, from_right, packed_here)
+
+    number = len(near_inputs) + count // 2 + 1
+    near_next = pl.pallas_call(
+        packed_refs(edge_kernel, count, slots, near_dims),
+        out_shape=shape(near_state.shape, f32),
+        in_specs=[smem_spec()] * 3 + [any_spec()] * (number - 2 + 1),
+        out_specs=any_spec(),
+        input_output_aliases={number: 0},
+        scratch_shapes=near_buffers(count, slots, near_dims, True),
+        compiler_params=params(VMEM_MIB),
+        cost_estimate=cost(1e8, 5e7),
+        name="near_edges",
+    )(*near_inputs, *held, packed, near_main, token)
     return off_next, near_next
 
 

time: 121 us -> 117 us (0.967); the launches traced: 121 us -> 115 us
  Pallas kernels: 71.8 us -> 62.4 us
  starting transfers between devices: 33 us -> 35.5 us
  waiting for transfers between devices: 10.9 us -> 12.5 us
    pallas_call x6 -> x5, Pallas kernels: 60.6 us -> 49.9 us  [the longest x1 18.7 us: local(): pl.pallas_call(packed_refs(off_kernel, off_dims), out_shape=[shape(off_st...]
    ppermute x1, starting transfers between devices: 0.07 us -> 3.02 us  [local(): packed = lax.ppermute(packed_here, 'gy', [(i, i ^ 1) for i in range(count)])]
    ppermute x14, waiting for transfers between devices: 10.9 us -> 12.5 us  [send(): return lax.ppermute(value, axis, ring(axis, distance))]
    unnamed x43 -> x30, local copies, waits for them, and re-layouts: 4.09 us -> 3.66 us
  transfers between devices with their start and end apart: 15 -> 15, of which waited for: 6 -> 5; matrix products, arithmetic and copies ran while one was open for 1% -> 0% of each run, Pallas kernels for 41% -> 37%
where the time goes in v2:
time: 117 us; the launch traced here: 115 us
  Pallas kernels  62.4 us (53%)
  starting transfers between devices  35.5 us (30%)
  waiting for transfers between devices  12.5 us (11%)
  local copies, waits for them, and re-layouts  3.66 us (3%)
    ppermute x14, starting transfers between devices, send(): return lax.ppermute(value, axis, ring(axis, distance))  32.5 us
    pallas_call x1, Pallas kernels, local(): pl.pallas_call(packed_refs(off_kernel, off_dims), out_shape=[shape(off_st...  18.7 us
    pallas_call x1, Pallas kernels, local(): pl.pallas_call(packed_refs(near_kernel, count, slots, near_dims), out_sha...  15.8 us
    ppermute x14, waiting for transfers between devices, send(): return lax.ppermute(value, axis, ring(axis, distance))  12.5 us
    pallas_call x1, Pallas kernels, local(): pl.pallas_call(packed_refs(edge_kernel, count, slots, near_dims), out_sha...  8.31 us
    pallas_call x1, Pallas kernels, local(): pl.pallas_call(packed_refs(base_kernel, slots, (around, nx, ny, nz)), out...  5.54 us
    pallas_call x1, Pallas kernels, local(): pl.pallas_call(packed_refs(patch_kernel, count, per_slot, (nx, ny, nz)),...  4.9 us
    pallas_call x1, Pallas kernels, local(): pl.pallas_call(packed_refs(interp_kernel, count, slots, (rows_here, per_s...  4.53 us
  transfers between devices with their start and end apart: 15, of which 5 were waited for; matrix products, arithmetic and copies ran while one was open for 0% of the time, Pallas kernels for 37%

profile of v2, /device:TPU:0, one launch (start us, length us, event | category | flops | bytes accessed | tf_op | source)
XLA Modules:
  0.0 115.1 jit_solution(745688506011467327)
XLA Ops:
  0.6 4.5 %interp.1 = (bf16[656,128]{1,0:T(8,128)(2,1)}, bf16[656,128]{1,0:T(8,128)(2,1)}, bf16[656,128]{1,0:T(8,128)(2,1)}, bf16[656,128]{1,0:T(8,128)(2,1)}, bf16[656,12...) custom-call(s32[3,8]{1,0:T(4,128)} %refs_0_.2, ...), custom_call_target="tpu_custom_call" | custom-call | flops 200000000 | bytes 6000000 | tf_op jit(solution)/shard_map/interp/pallas_call | solution.py:960
  5.2 3.0 %collective-permute-start = (bf16[656,128]{1,0:T(8,128)(2,1)}, bf16[656,128]{1,0:T(8,128)(2,1)S(1)}, u32[]{:S(2)}, u32[]{:S(2)}) collective-permute-start(bf16[656,128]{1,0:T(8,128)(2,1)} %get-tuple-element.25), channel_id=1, source_target_pairs={{0,1},{1,2},{2,3},{3,4},{4,5},{5,6},{6,7},{7,0},{8,9},{9,10},{10,1... | collective-permute-start | bytes 503816 | tf_op jit(solution)/shard_map/ppermute | solution.py:934
  8.2 1.6 %collective-permute-start.1 = (bf16[656,128]{1,0:T(8,128)(2,1)}, bf16[656,128]{1,0:T(8,128)(2,1)S(1)}, u32[]{:S(2)}, u32[]{:S(2)}) collective-permute-start(bf16[656,128]{1,0:T(8,128)(2,1)} %get-tuple-element.26), channel_id=1, source_target_pairs={{0,2},{1,3},{2,4},{3,5},{4,6},{5,7},{6,0},{7,1},{8,10},{9,11},{10,... | collective-permute-start | bytes 503816 | tf_op jit(solution)/shard_map/ppermute | solution.py:934
  9.8 2.5 %collective-permute-start.2 = (bf16[656,128]{1,0:T(8,128)(2,1)}, bf16[656,128]{1,0:T(8,128)(2,1)S(1)}, u32[]{:S(2)}, u32[]{:S(2)}) collective-permute-start(bf16[656,128]{1,0:T(8,128)(2,1)} %get-tuple-element.27), channel_id=1, source_target_pairs={{0,3},{1,4},{2,5},{3,6},{4,7},{5,0},{6,1},{7,2},{8,11},{9,12},{10,... | collective-permute-start | bytes 503816 | tf_op jit(solution)/shard_map/ppermute | solution.py:934
  12.3 1.2 %collective-permute-start.3 = (bf16[656,128]{1,0:T(8,128)(2,1)}, bf16[656,128]{1,0:T(8,128)(2,1)S(1)}, u32[]{:S(2)}, u32[]{:S(2)}) collective-permute-start(bf16[656,128]{1,0:T(8,128)(2,1)} %get-tuple-element.28), channel_id=1, source_target_pairs={{0,4},{1,5},{2,6},{3,7},{4,0},{5,1},{6,2},{7,3},{8,12},{9,13},{10,... | collective-permute-start | bytes 503816 | tf_op jit(solution)/shard_map/ppermute | solution.py:934
  13.5 2.6 %collective-permute-start.4 = (bf16[656,128]{1,0:T(8,128)(2,1)}, bf16[656,128]{1,0:T(8,128)(2,1)S(1)}, u32[]{:S(2)}, u32[]{:S(2)}) collective-permute-start(bf16[656,128]{1,0:T(8,128)(2,1)} %get-tuple-element.29), channel_id=1, source_target_pairs={{0,5},{1,6},{2,7},{3,0},{4,1},{5,2},{6,3},{7,4},{8,13},{9,14},{10,... | collective-permute-start | bytes 503816 | tf_op jit(solution)/shard_map/ppermute | solution.py:934
  16.2 0.5 collective-permute-done.refs_1_.refs_6_
  16.7 0.0 copy-start
  16.7 1.8 %collective-permute-start.5 = (bf16[656,128]{1,0:T(8,128)(2,1)}, bf16[656,128]{1,0:T(8,128)(2,1)S(1)}, u32[]{:S(2)}, u32[]{:S(2)}) collective-permute-start(bf16[656,128]{1,0:T(8,128)(2,1)} %get-tuple-element.30), channel_id=1, source_target_pairs={{0,6},{1,7},{2,0},{3,1},{4,2},{5,3},{6,4},{7,5},{8,14},{9,15},{10,... | collective-permute-start | bytes 503816 | tf_op jit(solution)/shard_map/ppermute | solution.py:934
  18.6 0.0 collective-permute-done.1.refs_2_.refs_7_
  18.6 2.8 %collective-permute-start.6 = (bf16[656,128]{1,0:T(8,128)(2,1)}, bf16[656,128]{1,0:T(8,128)(2,1)S(1)}, u32[]{:S(2)}, u32[]{:S(2)}) collective-permute-start(bf16[656,128]{1,0:T(8,128)(2,1)} %get-tuple-element.31), channel_id=1, source_target_pairs={{0,7},{1,0},{2,1},{3,2},{4,3},{5,4},{6,5},{7,6},{8,15},{9,8},{10,9... | collective-permute-start | bytes 503816 | tf_op jit(solution)/shard_map/ppermute | solution.py:934
  21.4 5.5 %base.1 = (f32[2,18,2,32,128]{4,3,2,1,0:T(8,128)}, f32[6,176,128]{2,1,0:T(8,128)}, f32[6,32,2,16,128]{4,3,2,1,0:T(8,128)}) custom-call(f32[5,32,16,256]{3,2,1,0:T(8,128)} %refs_0_.3, f32[3,5,8,64,128]{4,3,2,1,0:T(8,128)} %refs_3_.5, f32[3,3,8,64,128]{4,3,2,1,0:T(8,128)} %refs_4_.5), custom_call_target="tpu_custom_call" | custom-call | flops 10000000 | bytes 20000000 | tf_op jit(solution)/shard_map/base/pallas_call | solution.py:982
  26.9 0.0 copy-done
  26.9 0.0 copy-done.1
  27.0 3.3 %collective-permute-done.2.refs_3_.refs_8_ = bf16[656,128]{1,0:T(8,128)(2,1)S(1)} collective-permute-done((bf16[656,128]{1,0:T(8,128)(2,1)}, bf16[656,128]{1,0:T(8,128)(2,1)S(1)}, u32[]{:S(2)}, u32[]{:S(2)}) %collective-permute-start.2) | collective-permute-done | bytes 167968 | tf_op jit(solution)/shard_map/ppermute | solution.py:934
  30.3 0.0 copy-start.2
  30.3 0.2 collective-permute-done.3.refs_4_.refs_9_
  30.5 0.0 copy-start.3
  30.5 0.0 collective-permute-done.4.refs_5_.refs_10_
  30.5 0.0 copy-start.4
  30.5 0.0 collective-permute-done.5.refs_6_.refs_11_
  30.5 0.0 copy-start.5
  30.5 0.9 collective-permute-done.6.refs_7_.refs_12_
  31.4 0.0 copy-start.6
  31.4 0.0 copy-done.2
  31.4 0.0 copy-done.3
  31.4 0.0 copy-done.4
  31.4 0.0 copy-done.5
  31.4 0.6 copy-done.6
  32.0 4.9 %patch.1 = (bf16[18,2,32,128]{3,2,1,0:T(8,128)(2,1)}, bf16[18,2,32,128]{3,2,1,0:T(8,128)(2,1)}, bf16[6,176,128]{2,1,0:T(8,128)(2,1)}, s32[64]{0:T(128)}, f32[6,32,2,16,128]{4,3,2,1,0:T(8,128)}) custom-call(bf16[656,128]{1,0:T(8,128)(2,1)} %get-tuple-element.24.refs_0_.refs_5_, bf16[656,128]{1,0:T(8,128)(2,1)} %copy-done, ...), custom_call_target="tpu_custom_call", output_to_operand_aliasing={{4}: (10, {})} | custom-call | flops 10000000 | bytes 8000000 | tf_op jit(solution)/shard_map/patch/pallas_call | solution.py:1003
  36.9 4.3 %collective-permute-start.7 = (bf16[18,2,32,128]{3,2,1,0:T(8,128)(2,1)}, bf16[18,2,32,128]{3,2,1,0:T(8,128)(2,1)S(1)}, u32[]{:S(2)}, u32[]{:S(2)}) collective-permute-start(bf16[18,2,32,128]{3,2,1,0:T(8,128)(2,1)} %get-tuple-element.36), channel_id=1, source_target_pairs={{0,1},{1,2},{2,3},{3,4},{4,5},{5,6},{6,7},{7,0},{8,9},{9,10},{10,1... | collective-permute-start | bytes 884744 | tf_op jit(solution)/shard_map/ppermute | solution.py:934
  41.3 8.3 %collective-permute-start.8 = (bf16[18,2,32,128]{3,2,1,0:T(8,128)(2,1)}, bf16[18,2,32,128]{3,2,1,0:T(8,128)(2,1)S(1)}, u32[]{:S(2)}, u32[]{:S(2)}) collective-permute-start(bf16[18,2,32,128]{3,2,1,0:T(8,128)(2,1)} %get-tuple-element.37), channel_id=1, source_target_pairs={{0,7},{1,0},{2,1},{3,2},{4,3},{5,4},{6,5},{7,6},{8,15},{9,8},{10,9... | collective-permute-start | bytes 884744 | tf_op jit(solution)/shard_map/ppermute | solution.py:934
  49.6 1.8 %collective-permute-start.13 = (bf16[6,176,128]{2,1,0:T(8,128)(2,1)}, bf16[6,176,128]{2,1,0:T(8,128)(2,1)S(1)}, u32[]{:S(2)}, u32[]{:S(2)}) collective-permute-start(bf16[6,176,128]{2,1,0:T(8,128)(2,1)} %get-tuple-element.39.refs_13_.refs_2_), channel_id=1, source_target_pairs={{0,6},{1,7},{2,0},{3,1},{4,2},{5,3},{6,4},{7,5},{8,14},{9,15},{10,... | collective-permute-start | bytes 811016 | tf_op jit(solution)/shard_map/ppermute | solution.py:934
  51.4 0.0 collective-permute-start.12
  51.4 0.6 collective-permute-start.11
  52.0 15.8 %near_sections.1 = (f32[3,5,8,64,128]{4,3,2,1,0:T(8,128)}, f32[8,128]{1,0:T(8,128)}) custom-call(s32[64]{0:T(128)} %get-tuple-element.38.refs_0_, s32[2,64]{1,0:T(2,128)} %bitcast.1, s32[3]{0:T(128)} %refs_2_.7, f32[3,5,8,64,128]{4,3,2,1,0:T(8,128)} %refs_3_.5, f32[3,3,8,64,128]{4,3,2,1,0:T(8,128)} %refs_4_.5, ...), custom_call_target="tpu_custom_call" | custom-call | flops 100000000 | bytes 50000000 | tf_op jit(solution)/shard_map/near_sections/pallas_call | solution.py:1040
  67.8 0.0 collective-permute-done.7.refs_1_
  67.8 0.0 copy-start.7
  67.8 0.0 collective-permute-done.8.refs_2_
  67.8 0.0 copy-start.8
  67.8 0.7 copy-done.7
  68.5 0.1 copy-done.8
  68.6 2.2 %slabs.1 = (bf16[864,128]{1,0:T(8,128)(2,1)}, bf16[864,128]{1,0:T(8,128)(2,1)}) custom-call(f32[6,32,2,16,128]{4,3,2,1,0:T(8,128)} %get-tuple-element.35.refs_0_, bf16[18,2,32,128]{3,2,1,0:T(8,128)(2,1)} %copy-done.7, bf16[18,2,32,128]{3,2,1,0:T(8,128)(2,1)} %copy-done.8, f32[8,128]{1,0:T(8,128)} %get-tuple-element.40.refs_3_), custom_call_target="tpu_custom_call" | custom-call | flops 1000000 | bytes 4000000 | tf_op jit(solution)/shard_map/slabs/pallas_call | solution.py:1051
  70.8 0.1 collective-permute-start.9
  70.8 1.7 %collective-permute-start.10 = (bf16[864,128]{1,0:T(8,128)(2,1)}, bf16[864,128]{1,0:T(8,128)(2,1)S(1)}, u32[]{:S(2)}, u32[]{:S(2)}) collective-permute-start(bf16[864,128]{1,0:T(8,128)(2,1)} %get-tuple-element.42), channel_id=1, source_target_pairs={{0,24},{8,0},{16,8},{24,16},{1,25},{9,1},{17,9},{25,17},{2,26},{10... | collective-permute-start | bytes 663560 | tf_op jit(solution)/shard_map/ppermute | solution.py:934
  72.6 0.0 collective-permute-done.13.refs_5_.refs_16_
  72.6 0.0 copy-start.9
  72.6 7.6 %collective-permute-done.12.refs_4_.refs_15_ = bf16[6,176,128]{2,1,0:T(8,128)(2,1)S(1)} collective-permute-done((bf16[6,176,128]{2,1,0:T(8,128)(2,1)}, bf16[6,176,128]{2,1,0:T(8,128)(2,1)S(1)}, u32[]{:S(2)}, u32[]{:S(2)}) %collective-permute-start.12) | collective-permute-done | bytes 270368 | tf_op jit(solution)/shard_map/ppermute | solution.py:934
  80.2 0.0 collective-permute-done.11.refs_3_.refs_14_
  80.2 0.0 collective-permute-done.9.refs_6_.refs_3_
  80.2 0.0 copy-start.12
  80.2 0.0 collective-permute-done.10.refs_7_.refs_4_
  80.2 0.0 copy-done.9
  80.2 0.7 copy-done.10
  80.9 0.1 copy-done.11
  81.0 0.1 copy-done.12
  81.1 0.7 copy-done.13
  81.7 2.5 %pack.1.refs_5_ = bf16[6,176,128]{2,1,0:T(8,128)(2,1)} custom-call(s32[64]{0:T(128)} %get-tuple-element.38.refs_0_, s32[2,64]{1,0:T(2,128)} %bitcast.2, bf16[6,176,128]{2,1,0:T(8,128)(2,1)} %get-tuple-element.39.refs_13_.refs_2_, bf16[6,176,128]{2,1,0:T(8,128)(2,1)} %copy-done.11, bf16[6,176,128]{2,1,0:T(8,128)(2,1)} %copy-done.10, ...), custom_call_target="tpu_custom_call" | custom-call | flops 100000 | bytes 2000000 | tf_op jit(solution)/shard_map/pack/pallas_call | solution.py:1069
  84.2 3.0 %collective-permute-start.14 = (bf16[6,176,128]{2,1,0:T(8,128)(2,1)}, bf16[6,176,128]{2,1,0:T(8,128)(2,1)S(1)}, u32[]{:S(2)}, u32[]{:S(2)}) collective-permute-start(bf16[6,176,128]{2,1,0:T(8,128)(2,1)} %pack.1.refs_5_), channel_id=1, source_target_pairs={{0,1},{1,0},{2,3},{3,2},{4,5},{5,4},{6,7},{7,6},{8,9},{9,8},{10,11... | collective-permute-start | bytes 811016 | tf_op jit(solution)/shard_map/ppermute | solution.py:1079
  87.2 18.7 %off_sections.1 = (f32[5,32,16,256]{3,2,1,0:T(8,128)}, f32[8,128]{1,0:T(8,128)}) custom-call(f32[6,32,2,16,128]{4,3,2,1,0:T(8,128)} %get-tuple-element.35.refs_0_, bf16[18,2,32,128]{3,2,1,0:T(8,128)(2,1)} %copy-done.7, bf16[18,2,32,128]{3,2,1,0:T(8,128)(2,1)} %copy-done.8, bf16[864,128]{1,0:T(8,128)(2,1)} %copy-done.12, bf16[864,128]{1,0:T(8,128)(2,1)} %copy-done.13, ...), custom_call_target="tpu_custom_call" | custom-call | flops 100000000 | bytes 50000000 | tf_op jit(solution)/shard_map/off_sections/pallas_call | solution.py:1081
  106.0 0.0 collective-permute-done.14.refs_17_
  106.0 0.0 copy-start.14
  106.0 0.7 copy-done.14
  106.7 8.3 %near_edges.1 = f32[3,5,8,64,128]{4,3,2,1,0:T(8,128)} custom-call(s32[64]{0:T(128)} %get-tuple-element.38.refs_0_, s32[2,64]{1,0:T(2,128)} %bitcast.3, s32[3]{0:T(128)} %refs_2_.7, f32[3,5,8,64,128]{4,3,2,1,0:T(8,128)} %refs_3_.5, f32[3,3,8,64,128]{4,3,2,1,0:T(8,128)} %refs_4_.5, ...), custom_call_target="tpu_custom_call", output_to_operand_aliasing={{}: (18, {})} | custom-call | flops 100000000 | bytes 50000000 | tf_op jit(solution)/shard_map/near_edges/pallas_call | solution.py:1093
  (4 shorter events, 0.0 us)
Async XLA Ops:
  5.2 11.5 %collective-permute-start = (bf16[656,128]{1,0:T(8,128)(2,1)}, bf16[656,128]{1,0:T(8,128)(2,1)S(1)}, u32[]{:S(2)}, u32[]{:S(2)}) collective-permute-start(bf16[656,128]{1,0:T(8,128)(2,1)} %get-tuple-element.25), channel_id=1, source_target_pairs={{0,1},{1,2},{2,3},{3,4},{4,5},{5,6},{6,7},{7,0},{8,9},{9,10},{10,1... | collective-permute-start | bytes 503816 | tf_op jit(solution)/shard_map/ppermute | solution.py:934
  8.2 10.4 %collective-permute-start.1 = (bf16[656,128]{1,0:T(8,128)(2,1)}, bf16[656,128]{1,0:T(8,128)(2,1)S(1)}, u32[]{:S(2)}, u32[]{:S(2)}) collective-permute-start(bf16[656,128]{1,0:T(8,128)(2,1)} %get-tuple-element.26), channel_id=1, source_target_pairs={{0,2},{1,3},{2,4},{3,5},{4,6},{5,7},{6,0},{7,1},{8,10},{9,11},{10,... | collective-permute-start | bytes 503816 | tf_op jit(solution)/shard_map/ppermute | solution.py:934
  9.8 20.5 %collective-permute-start.2 = (bf16[656,128]{1,0:T(8,128)(2,1)}, bf16[656,128]{1,0:T(8,128)(2,1)S(1)}, u32[]{:S(2)}, u32[]{:S(2)}) collective-permute-start(bf16[656,128]{1,0:T(8,128)(2,1)} %get-tuple-element.27), channel_id=1, source_target_pairs={{0,3},{1,4},{2,5},{3,6},{4,7},{5,0},{6,1},{7,2},{8,11},{9,12},{10,... | collective-permute-start | bytes 503816 | tf_op jit(solution)/shard_map/ppermute | solution.py:934
  12.3 18.2 %collective-permute-start.3 = (bf16[656,128]{1,0:T(8,128)(2,1)}, bf16[656,128]{1,0:T(8,128)(2,1)S(1)}, u32[]{:S(2)}, u32[]{:S(2)}) collective-permute-start(bf16[656,128]{1,0:T(8,128)(2,1)} %get-tuple-element.28), channel_id=1, source_target_pairs={{0,4},{1,5},{2,6},{3,7},{4,0},{5,1},{6,2},{7,3},{8,12},{9,13},{10,... | collective-permute-start | bytes 503816 | tf_op jit(solution)/shard_map/ppermute | solution.py:934
  13.5 17.0 %collective-permute-start.4 = (bf16[656,128]{1,0:T(8,128)(2,1)}, bf16[656,128]{1,0:T(8,128)(2,1)S(1)}, u32[]{:S(2)}, u32[]{:S(2)}) collective-permute-start(bf16[656,128]{1,0:T(8,128)(2,1)} %get-tuple-element.29), channel_id=1, source_target_pairs={{0,5},{1,6},{2,7},{3,0},{4,1},{5,2},{6,3},{7,4},{8,13},{9,14},{10,... | collective-permute-start | bytes 503816 | tf_op jit(solution)/shard_map/ppermute | solution.py:934
  16.7 10.2 %copy-start = (bf16[656,128]{1,0:T(8,128)(2,1)}, bf16[656,128]{1,0:T(8,128)(2,1)S(1)}, u32[]{:S(2)}) copy-start(bf16[656,128]{1,0:T(8,128)(2,1)S(1)} %collective-permute-done.refs_1_.refs_6_) | copy-start | bytes 503812
  16.7 13.8 %collective-permute-start.5 = (bf16[656,128]{1,0:T(8,128)(2,1)}, bf16[656,128]{1,0:T(8,128)(2,1)S(1)}, u32[]{:S(2)}, u32[]{:S(2)}) collective-permute-start(bf16[656,128]{1,0:T(8,128)(2,1)} %get-tuple-element.30), channel_id=1, source_target_pairs={{0,6},{1,7},{2,0},{3,1},{4,2},{5,3},{6,4},{7,5},{8,14},{9,15},{10,... | collective-permute-start | bytes 503816 | tf_op jit(solution)/shard_map/ppermute | solution.py:934
  18.6 8.4 %copy-start.1 = (bf16[656,128]{1,0:T(8,128)(2,1)}, bf16[656,128]{1,0:T(8,128)(2,1)S(1)}, u32[]{:S(2)}) copy-start(bf16[656,128]{1,0:T(8,128)(2,1)S(1)} %collective-permute-done.1.refs_2_.refs_7_) | copy-start | bytes 503812
  18.6 12.8 %collective-permute-start.6 = (bf16[656,128]{1,0:T(8,128)(2,1)}, bf16[656,128]{1,0:T(8,128)(2,1)S(1)}, u32[]{:S(2)}, u32[]{:S(2)}) collective-permute-start(bf16[656,128]{1,0:T(8,128)(2,1)} %get-tuple-element.31), channel_id=1, source_target_pairs={{0,7},{1,0},{2,1},{3,2},{4,3},{5,4},{6,5},{7,6},{8,15},{9,8},{10,9... | collective-permute-start | bytes 503816 | tf_op jit(solution)/shard_map/ppermute | solution.py:934
  30.3 1.1 copy-start.2
  30.5 0.9 copy-start.3
  30.5 0.9 copy-start.4
  30.5 0.9 copy-start.5
  31.4 0.7 copy-start.6
  36.9 30.8 %collective-permute-start.7 = (bf16[18,2,32,128]{3,2,1,0:T(8,128)(2,1)}, bf16[18,2,32,128]{3,2,1,0:T(8,128)(2,1)S(1)}, u32[]{:S(2)}, u32[]{:S(2)}) collective-permute-start(bf16[18,2,32,128]{3,2,1,0:T(8,128)(2,1)} %get-tuple-element.36), channel_id=1, source_target_pairs={{0,1},{1,2},{2,3},{3,4},{4,5},{5,6},{6,7},{7,0},{8,9},{9,10},{10,1... | collective-permute-start | bytes 884744 | tf_op jit(solution)/shard_map/ppermute | solution.py:934
  41.3 26.5 %collective-permute-start.8 = (bf16[18,2,32,128]{3,2,1,0:T(8,128)(2,1)}, bf16[18,2,32,128]{3,2,1,0:T(8,128)(2,1)S(1)}, u32[]{:S(2)}, u32[]{:S(2)}) collective-permute-start(bf16[18,2,32,128]{3,2,1,0:T(8,128)(2,1)} %get-tuple-element.37), channel_id=1, source_target_pairs={{0,7},{1,0},{2,1},{3,2},{4,3},{5,4},{6,5},{7,6},{8,15},{9,8},{10,9... | collective-permute-start | bytes 884744 | tf_op jit(solution)/shard_map/ppermute | solution.py:934
  49.6 23.0 %collective-permute-start.13 = (bf16[6,176,128]{2,1,0:T(8,128)(2,1)}, bf16[6,176,128]{2,1,0:T(8,128)(2,1)S(1)}, u32[]{:S(2)}, u32[]{:S(2)}) collective-permute-start(bf16[6,176,128]{2,1,0:T(8,128)(2,1)} %get-tuple-element.39.refs_13_.refs_2_), channel_id=1, source_target_pairs={{0,6},{1,7},{2,0},{3,1},{4,2},{5,3},{6,4},{7,5},{8,14},{9,15},{10,... | collective-permute-start | bytes 811016 | tf_op jit(solution)/shard_map/ppermute | solution.py:934
  51.4 28.7 %collective-permute-start.12 = (bf16[6,176,128]{2,1,0:T(8,128)(2,1)}, bf16[6,176,128]{2,1,0:T(8,128)(2,1)S(1)}, u32[]{:S(2)}, u32[]{:S(2)}) collective-permute-start(bf16[6,176,128]{2,1,0:T(8,128)(2,1)} %get-tuple-element.39.refs_13_.refs_2_), channel_id=1, source_target_pairs={{0,4},{1,5},{2,6},{3,7},{4,0},{5,1},{6,2},{7,3},{8,12},{9,13},{10,... | collective-permute-start | bytes 811016 | tf_op jit(solution)/shard_map/ppermute | solution.py:934
  51.4 28.8 %collective-permute-start.11 = (bf16[6,176,128]{2,1,0:T(8,128)(2,1)}, bf16[6,176,128]{2,1,0:T(8,128)(2,1)S(1)}, u32[]{:S(2)}, u32[]{:S(2)}) collective-permute-start(bf16[6,176,128]{2,1,0:T(8,128)(2,1)} %get-tuple-element.39.refs_13_.refs_2_), channel_id=1, source_target_pairs={{0,2},{1,3},{2,4},{3,5},{4,6},{5,7},{6,0},{7,1},{8,10},{9,11},{10,... | collective-permute-start | bytes 811016 | tf_op jit(solution)/shard_map/ppermute | solution.py:934
  67.8 0.7 copy-start.7
  67.8 0.8 copy-start.8
  70.8 9.4 %collective-permute-start.9 = (bf16[864,128]{1,0:T(8,128)(2,1)}, bf16[864,128]{1,0:T(8,128)(2,1)S(1)}, u32[]{:S(2)}, u32[]{:S(2)}) collective-permute-start(bf16[864,128]{1,0:T(8,128)(2,1)} %get-tuple-element.41), channel_id=1, source_target_pairs={{0,8},{8,16},{16,24},{24,0},{1,9},{9,17},{17,25},{25,1},{2,10},{10... | collective-permute-start | bytes 663560 | tf_op jit(solution)/shard_map/ppermute | solution.py:934
  70.8 9.3 %collective-permute-start.10 = (bf16[864,128]{1,0:T(8,128)(2,1)}, bf16[864,128]{1,0:T(8,128)(2,1)S(1)}, u32[]{:S(2)}, u32[]{:S(2)}) collective-permute-start(bf16[864,128]{1,0:T(8,128)(2,1)} %get-tuple-element.42), channel_id=1, source_target_pairs={{0,24},{8,0},{16,8},{24,16},{1,25},{9,1},{17,9},{25,17},{2,26},{10... | collective-permute-start | bytes 663560 | tf_op jit(solution)/shard_map/ppermute | solution.py:934
  72.6 7.6 %copy-start.9 = (bf16[6,176,128]{2,1,0:T(8,128)(2,1)}, bf16[6,176,128]{2,1,0:T(8,128)(2,1)S(1)}, u32[]{:S(2)}) copy-start(bf16[6,176,128]{2,1,0:T(8,128)(2,1)S(1)} %collective-permute-done.13.refs_5_.refs_16_) | copy-start | bytes 811012
  80.2 0.7 copy-start.10
  80.2 0.8 copy-start.11
  80.2 0.9 copy-start.12
  81.1 0.7 copy-start.13
  84.2 21.8 %collective-permute-start.14 = (bf16[6,176,128]{2,1,0:T(8,128)(2,1)}, bf16[6,176,128]{2,1,0:T(8,128)(2,1)S(1)}, u32[]{:S(2)}, u32[]{:S(2)}) collective-permute-start(bf16[6,176,128]{2,1,0:T(8,128)(2,1)} %pack.1.refs_5_), channel_id=1, source_target_pairs={{0,1},{1,0},{2,3},{3,2},{4,5},{5,4},{6,7},{7,6},{8,9},{9,8},{10,11... | collective-permute-start | bytes 811016 | tf_op jit(solution)/shard_map/ppermute | solution.py:1079
  106.0 0.7 copy-start.14

commit v3 on v2

--- a/solution.py
+++ b/solution.py
@@ -1043,7 +1043,7 @@
         in_specs=[smem_spec()] * 3 + [any_spec()] * (2 + count + 1),
         out_specs=[any_spec(), vmem_spec()],
         scratch_shapes=near_buffers(count, slots, near_dims, False),
-        compiler_params=params(VMEM_MIB),
+        compiler_params=params(56),
         cost_estimate=cost(1e8, 5e7),
         name="near_sections",
     )(*near_inputs, faces)
@@ -1059,7 +1059,7 @@
             VMEM((2, FIELDS + 1, DEPTH, halves, ny, TL), f32),
             dma((4,)),
         ],
-        compiler_params=params(VMEM_MIB),
+        compiler_params=params(8),
         cost_estimate=cost(1e6, 4e6),
         name="slabs",
     )(placed, from_low, from_high, token)
@@ -1072,7 +1072,7 @@
         in_specs=[smem_spec()] * 2 + [any_spec()] * (count // 2 + 2),
         out_specs=vmem_spec(),
         scratch_shapes=[dma((2 * slots,))],
-        compiler_params=params(VMEM_MIB),
+        compiler_params=params(4),
         cost_estimate=cost(1e5, 2e6),
         name="pack",
     )(table, block_faces, *held, from_left, from_right)

time: 117 us -> 114 us (0.974)
  the two profiles are of different devices: /device:TPU:0 before, /device:TPU:1 now
where the time goes in v3:
time: 114 us
  Pallas kernels  67.5 us (59%)
  starting transfers between devices  31.6 us (28%)
  waiting for transfers between devices  10.9 us (10%)
  local copies, waits for them, and re-layouts  2.48 us (2%)
    ppermute x14, starting transfers between devices, send(): return lax.ppermute(value, axis, ring(axis, distance))  31 us
    pallas_call x1, Pallas kernels, local(): pl.pallas_call(packed_refs(near_kernel, count, slots, near_dims), out_sha...  21.1 us
    pallas_call x1, Pallas kernels, local(): pl.pallas_call(packed_refs(off_kernel, off_dims), out_shape=[shape(off_st...  18.7 us
    pallas_call x1, Pallas kernels, local(): pl.pallas_call(packed_refs(edge_kernel, count, slots, near_dims), out_sha...  10.9 us
    ppermute x14, waiting for transfers between devices, send(): return lax.ppermute(value, axis, ring(axis, distance))  10.9 us
    pallas_call x1, Pallas kernels, local(): pl.pallas_call(packed_refs(base_kernel, slots, (around, nx, ny, nz)), out...  5.55 us
    pallas_call x1, Pallas kernels, local(): pl.pallas_call(packed_refs(patch_kernel, count, per_slot, (nx, ny, nz)),...  4.92 us
    pallas_call x1, Pallas kernels, local(): pl.pallas_call(packed_refs(interp_kernel, count, slots, (rows_here, per_s...  4.52 us
  transfers between devices with their start and end apart: 15, of which 5 were waited for; matrix products, arithmetic and copies ran while one was open for 0% of the time, Pallas kernels for 40%

profile of v3, /device:TPU:1, one launch (start us, length us, event | category | flops | bytes accessed | tf_op | source)
XLA Modules:
  0.0 113.6 jit_solution(12684202045624543011)
XLA Ops:
  0.6 4.5 %interp.1 = (bf16[656,128]{1,0:T(8,128)(2,1)}, bf16[656,128]{1,0:T(8,128)(2,1)}, bf16[656,128]{1,0:T(8,128)(2,1)}, bf16[656,128]{1,0:T(8,128)(2,1)}, bf16[656,12...) custom-call(s32[3,8]{1,0:T(4,128)} %refs_0_.2, ...), custom_call_target="tpu_custom_call" | custom-call | flops 200000000 | bytes 6000000 | tf_op jit(solution)/shard_map/interp/pallas_call | solution.py:960
  5.2 2.1 %collective-permute-start = (bf16[656,128]{1,0:T(8,128)(2,1)}, bf16[656,128]{1,0:T(8,128)(2,1)S(1)}, u32[]{:S(2)}, u32[]{:S(2)}) collective-permute-start(bf16[656,128]{1,0:T(8,128)(2,1)} %get-tuple-element.25), channel_id=1, source_target_pairs={{0,1},{1,2},{2,3},{3,4},{4,5},{5,6},{6,7},{7,0},{8,9},{9,10},{10,1... | collective-permute-start | bytes 503816 | tf_op jit(solution)/shard_map/ppermute | solution.py:934
  7.3 1.3 %collective-permute-start.1 = (bf16[656,128]{1,0:T(8,128)(2,1)}, bf16[656,128]{1,0:T(8,128)(2,1)S(1)}, u32[]{:S(2)}, u32[]{:S(2)}) collective-permute-start(bf16[656,128]{1,0:T(8,128)(2,1)} %get-tuple-element.26), channel_id=1, source_target_pairs={{0,2},{1,3},{2,4},{3,5},{4,6},{5,7},{6,0},{7,1},{8,10},{9,11},{10,... | collective-permute-start | bytes 503816 | tf_op jit(solution)/shard_map/ppermute | solution.py:934
  8.6 2.3 %collective-permute-start.2 = (bf16[656,128]{1,0:T(8,128)(2,1)}, bf16[656,128]{1,0:T(8,128)(2,1)S(1)}, u32[]{:S(2)}, u32[]{:S(2)}) collective-permute-start(bf16[656,128]{1,0:T(8,128)(2,1)} %get-tuple-element.27), channel_id=1, source_target_pairs={{0,3},{1,4},{2,5},{3,6},{4,7},{5,0},{6,1},{7,2},{8,11},{9,12},{10,... | collective-permute-start | bytes 503816 | tf_op jit(solution)/shard_map/ppermute | solution.py:934
  10.8 1.0 collective-permute-start.3
  11.8 2.4 %collective-permute-start.4 = (bf16[656,128]{1,0:T(8,128)(2,1)}, bf16[656,128]{1,0:T(8,128)(2,1)S(1)}, u32[]{:S(2)}, u32[]{:S(2)}) collective-permute-start(bf16[656,128]{1,0:T(8,128)(2,1)} %get-tuple-element.29), channel_id=1, source_target_pairs={{0,5},{1,6},{2,7},{3,0},{4,1},{5,2},{6,3},{7,4},{8,13},{9,14},{10,... | collective-permute-start | bytes 503816 | tf_op jit(solution)/shard_map/ppermute | solution.py:934
  14.2 0.4 collective-permute-done.refs_1_.refs_6_
  14.6 1.1 collective-permute-start.5
  15.6 0.0 collective-permute-done.1.refs_2_.refs_7_
  15.6 3.6 %collective-permute-start.6 = (bf16[656,128]{1,0:T(8,128)(2,1)}, bf16[656,128]{1,0:T(8,128)(2,1)S(1)}, u32[]{:S(2)}, u32[]{:S(2)}) collective-permute-start(bf16[656,128]{1,0:T(8,128)(2,1)} %get-tuple-element.31), channel_id=1, source_target_pairs={{0,7},{1,0},{2,1},{3,2},{4,3},{5,4},{6,5},{7,6},{8,15},{9,8},{10,9... | collective-permute-start | bytes 503816 | tf_op jit(solution)/shard_map/ppermute | solution.py:934
  19.2 5.6 %base.1 = (f32[2,18,2,32,128]{4,3,2,1,0:T(8,128)}, f32[6,176,128]{2,1,0:T(8,128)}, f32[6,32,2,16,128]{4,3,2,1,0:T(8,128)}) custom-call(f32[5,32,16,256]{3,2,1,0:T(8,128)} %refs_0_.3, f32[3,5,8,64,128]{4,3,2,1,0:T(8,128)} %refs_3_.5, f32[3,3,8,64,128]{4,3,2,1,0:T(8,128)} %refs_4_.5), custom_call_target="tpu_custom_call" | custom-call | flops 10000000 | bytes 20000000 | tf_op jit(solution)/shard_map/base/pallas_call | solution.py:982
  24.8 0.0 copy-done.13
  24.8 0.0 copy-done.14
  24.8 4.9 %collective-permute-done.2.refs_3_.refs_8_ = bf16[656,128]{1,0:T(8,128)(2,1)S(1)} collective-permute-done((bf16[656,128]{1,0:T(8,128)(2,1)}, bf16[656,128]{1,0:T(8,128)(2,1)S(1)}, u32[]{:S(2)}, u32[]{:S(2)}) %collective-permute-start.2) | collective-permute-done | bytes 167968 | tf_op jit(solution)/shard_map/ppermute | solution.py:934
  29.7 0.2 collective-permute-done.3.refs_4_.refs_9_
  30.0 0.0 collective-permute-done.4.refs_5_.refs_10_
  30.0 0.0 collective-permute-done.5.refs_6_.refs_11_
  30.0 0.0 copy-start.18
  30.0 0.0 collective-permute-done.6.refs_7_.refs_12_
  30.0 0.0 copy-start.19
  30.0 0.4 copy-done.15
  30.4 0.2 copy-done.16
  30.6 0.1 copy-done.17
  30.7 0.1 copy-done.18
  30.8 0.1 copy-done.19
  30.8 4.9 %patch.1 = (bf16[18,2,32,128]{3,2,1,0:T(8,128)(2,1)}, bf16[18,2,32,128]{3,2,1,0:T(8,128)(2,1)}, bf16[6,176,128]{2,1,0:T(8,128)(2,1)}, s32[64]{0:T(128)}, f32[6,32,2,16,128]{4,3,2,1,0:T(8,128)}) custom-call(bf16[656,128]{1,0:T(8,128)(2,1)} %get-tuple-element.24.refs_0_.refs_5_, bf16[656,128]{1,0:T(8,128)(2,1)} %copy-done.13, ...), custom_call_target="tpu_custom_call", output_to_operand_aliasing={{4}: (10, {})} | custom-call | flops 10000000 | bytes 8000000 | tf_op jit(solution)/shard_map/patch/pallas_call | solution.py:1003
  35.7 4.8 %collective-permute-start.7 = (bf16[18,2,32,128]{3,2,1,0:T(8,128)(2,1)}, bf16[18,2,32,128]{3,2,1,0:T(8,128)(2,1)S(1)}, u32[]{:S(2)}, u32[]{:S(2)}) collective-permute-start(bf16[18,2,32,128]{3,2,1,0:T(8,128)(2,1)} %get-tuple-element.36), channel_id=1, source_target_pairs={{0,1},{1,2},{2,3},{3,4},{4,5},{5,6},{6,7},{7,0},{8,9},{9,10},{10,1... | collective-permute-start | bytes 884744 | tf_op jit(solution)/shard_map/ppermute | solution.py:934
  40.5 7.0 %collective-permute-start.8 = (bf16[18,2,32,128]{3,2,1,0:T(8,128)(2,1)}, bf16[18,2,32,128]{3,2,1,0:T(8,128)(2,1)S(1)}, u32[]{:S(2)}, u32[]{:S(2)}) collective-permute-start(bf16[18,2,32,128]{3,2,1,0:T(8,128)(2,1)} %get-tuple-element.37), channel_id=1, source_target_pairs={{0,7},{1,0},{2,1},{3,2},{4,3},{5,4},{6,5},{7,6},{8,15},{9,8},{10,9... | collective-permute-start | bytes 884744 | tf_op jit(solution)/shard_map/ppermute | solution.py:934
  47.5 0.2 collective-permute-start.13
  47.7 1.3 %collective-permute-start.12 = (bf16[6,176,128]{2,1,0:T(8,128)(2,1)}, bf16[6,176,128]{2,1,0:T(8,128)(2,1)S(1)}, u32[]{:S(2)}, u32[]{:S(2)}) collective-permute-start(bf16[6,176,128]{2,1,0:T(8,128)(2,1)} %get-tuple-element.39.refs_13_.refs_2_), channel_id=1, source_target_pairs={{0,4},{1,5},{2,6},{3,7},{4,0},{5,1},{6,2},{7,3},{8,12},{9,13},{10,... | collective-permute-start | bytes 811016 | tf_op jit(solution)/shard_map/ppermute | solution.py:934
  49.0 1.2 %collective-permute-start.11 = (bf16[6,176,128]{2,1,0:T(8,128)(2,1)}, bf16[6,176,128]{2,1,0:T(8,128)(2,1)S(1)}, u32[]{:S(2)}, u32[]{:S(2)}) collective-permute-start(bf16[6,176,128]{2,1,0:T(8,128)(2,1)} %get-tuple-element.39.refs_13_.refs_2_), channel_id=1, source_target_pairs={{0,2},{1,3},{2,4},{3,5},{4,6},{5,7},{6,0},{7,1},{8,10},{9,11},{10,... | collective-permute-start | bytes 811016 | tf_op jit(solution)/shard_map/ppermute | solution.py:934
  50.2 21.1 %near_sections.1 = (f32[3,5,8,64,128]{4,3,2,1,0:T(8,128)}, f32[8,128]{1,0:T(8,128)}) custom-call(s32[64]{0:T(128)} %get-tuple-element.38.refs_0_, s32[2,64]{1,0:T(2,128)} %bitcast.1, s32[3]{0:T(128)} %refs_2_.7, f32[3,5,8,64,128]{4,3,2,1,0:T(8,128)} %refs_3_.5, f32[3,3,8,64,128]{4,3,2,1,0:T(8,128)} %refs_4_.5, ...), custom_call_target="tpu_custom_call" | custom-call | flops 100000000 | bytes 50000000 | tf_op jit(solution)/shard_map/near_sections/pallas_call | solution.py:1040
  71.3 0.0 copy-start.1
  71.3 0.0 copy-start.10
  71.3 0.0 copy-start.11
  71.4 0.0 collective-permute-done.7.refs_1_
  71.4 0.0 copy-start.2
  71.4 0.0 collective-permute-done.8.refs_2_
  71.4 0.0 copy-start.3
  71.4 0.0 copy-done
  71.4 0.0 copy-start.12
  71.4 0.8 copy-done.12
  72.3 0.4 slabs.1
  72.7 2.9 %collective-permute-start.9 = (bf16[864,128]{1,0:T(8,128)(2,1)S(1)}, bf16[864,128]{1,0:T(8,128)(2,1)S(1)}, u32[]{:S(2)}, u32[]{:S(2)}) collective-permute-start(bf16[864,128]{1,0:T(8,128)(2,1)S(1)} %get-tuple-element.41), channel_id=1, source_target_pairs={{0,8},{8,16},{16,24},{24,0},{1,9},{9,17},{17,25},{25,1},{2,10},{10... | collective-permute-start | bytes 663560 | tf_op jit(solution)/shard_map/ppermute | solution.py:934
  75.5 0.0 collective-permute-start.10
  75.5 0.0 collective-permute-done.13.refs_5_.refs_16_
  75.5 3.3 %collective-permute-done.12.refs_4_.refs_15_ = bf16[6,176,128]{2,1,0:T(8,128)(2,1)S(1)} collective-permute-done((bf16[6,176,128]{2,1,0:T(8,128)(2,1)}, bf16[6,176,128]{2,1,0:T(8,128)(2,1)S(1)}, u32[]{:S(2)}, u32[]{:S(2)}) %collective-permute-start.12) | collective-permute-done | bytes 270368 | tf_op jit(solution)/shard_map/ppermute | solution.py:934
  78.8 0.0 collective-permute-done.11.refs_3_.refs_14_
  78.8 0.0 collective-permute-done.9.refs_6_.refs_3_
  78.8 0.0 copy-start.8
  78.8 2.1 %collective-permute-done.10.refs_7_.refs_4_ = bf16[864,128]{1,0:T(8,128)(2,1)S(1)} collective-permute-done((bf16[864,128]{1,0:T(8,128)(2,1)S(1)}, bf16[864,128]{1,0:T(8,128)(2,1)S(1)}, u32[]{:S(2)}, u32[]{:S(2)}) %collective-permute-start.10) | collective-permute-done | bytes 221216 | tf_op jit(solution)/shard_map/ppermute | solution.py:934
  80.9 0.0 copy-done.1
  80.9 0.0 copy-done.10
  80.9 0.0 copy-done.11
  80.9 0.0 copy-start.9
  80.9 1.4 %pack.1.refs_5_ = bf16[6,176,128]{2,1,0:T(8,128)(2,1)S(1)} custom-call(s32[64]{0:T(128)S(1)} %copy-done.11, s32[2,64]{1,0:T(2,128)S(1)} %bitcast.3, bf16[6,176,128]{2,1,0:T(8,128)(2,1)S(1)} %copy-done.1, bf16[6,176,128]{2,1,0:T(8,128)(2,1)S(1)} %collective-permute-done.11.refs_3_.refs_14_, bf16[6,176,128]{2,1,0:T(8,128)(2,1)S(1)} %collective-permute-done.12.refs_4_.refs_15_, ...), custom_call_target="tpu_custom_call" | custom-call | flops 100000 | bytes 2000000 | tf_op jit(solution)/shard_map/pack/pallas_call | solution.py:1069
  82.4 0.0 copy-start.4
  82.4 0.6 collective-permute-start.14
  83.0 0.0 copy-done.8
  83.0 0.1 copy-done.4
  83.1 18.7 %off_sections.1 = (f32[5,32,16,256]{3,2,1,0:T(8,128)}, f32[8,128]{1,0:T(8,128)}) custom-call(f32[6,32,2,16,128]{4,3,2,1,0:T(8,128)} %get-tuple-element.35.refs_0_, bf16[18,2,32,128]{3,2,1,0:T(8,128)(2,1)} %copy-done.2, bf16[18,2,32,128]{3,2,1,0:T(8,128)(2,1)} %copy-done.3, bf16[864,128]{1,0:T(8,128)(2,1)} %copy-done.8, bf16[864,128]{1,0:T(8,128)(2,1)} %copy-done.9, ...), custom_call_target="tpu_custom_call" | custom-call | flops 100000000 | bytes 50000000 | tf_op jit(solution)/shard_map/off_sections/pallas_call | solution.py:1081
  101.8 0.0 collective-permute-done.14.refs_17_
  101.9 0.7 copy-done.20
  102.5 10.9 %near_edges.1 = f32[3,5,8,64,128]{4,3,2,1,0:T(8,128)} custom-call(s32[64]{0:T(128)} %get-tuple-element.38.refs_0_, s32[2,64]{1,0:T(2,128)} %bitcast.2, s32[3]{0:T(128)} %refs_2_.7, f32[3,5,8,64,128]{4,3,2,1,0:T(8,128)} %refs_3_.5, f32[3,3,8,64,128]{4,3,2,1,0:T(8,128)} %refs_4_.5, ...), custom_call_target="tpu_custom_call", output_to_operand_aliasing={{}: (18, {})} | custom-call | flops 100000000 | bytes 50000000 | tf_op jit(solution)/shard_map/near_edges/pallas_call | solution.py:1093
  (16 shorter events, 0.0 us)
Async XLA Ops:
  5.2 9.4 %collective-permute-start = (bf16[656,128]{1,0:T(8,128)(2,1)}, bf16[656,128]{1,0:T(8,128)(2,1)S(1)}, u32[]{:S(2)}, u32[]{:S(2)}) collective-permute-start(bf16[656,128]{1,0:T(8,128)(2,1)} %get-tuple-element.25), channel_id=1, source_target_pairs={{0,1},{1,2},{2,3},{3,4},{4,5},{5,6},{6,7},{7,0},{8,9},{9,10},{10,1... | collective-permute-start | bytes 503816 | tf_op jit(solution)/shard_map/ppermute | solution.py:934
  7.3 8.4 %collective-permute-start.1 = (bf16[656,128]{1,0:T(8,128)(2,1)}, bf16[656,128]{1,0:T(8,128)(2,1)S(1)}, u32[]{:S(2)}, u32[]{:S(2)}) collective-permute-start(bf16[656,128]{1,0:T(8,128)(2,1)} %get-tuple-element.26), channel_id=1, source_target_pairs={{0,2},{1,3},{2,4},{3,5},{4,6},{5,7},{6,0},{7,1},{8,10},{9,11},{10,... | collective-permute-start | bytes 503816 | tf_op jit(solution)/shard_map/ppermute | solution.py:934
  8.6 21.1 %collective-permute-start.2 = (bf16[656,128]{1,0:T(8,128)(2,1)}, bf16[656,128]{1,0:T(8,128)(2,1)S(1)}, u32[]{:S(2)}, u32[]{:S(2)}) collective-permute-start(bf16[656,128]{1,0:T(8,128)(2,1)} %get-tuple-element.27), channel_id=1, source_target_pairs={{0,3},{1,4},{2,5},{3,6},{4,7},{5,0},{6,1},{7,2},{8,11},{9,12},{10,... | collective-permute-start | bytes 503816 | tf_op jit(solution)/shard_map/ppermute | solution.py:934
  10.8 19.1 %collective-permute-start.3 = (bf16[656,128]{1,0:T(8,128)(2,1)}, bf16[656,128]{1,0:T(8,128)(2,1)S(1)}, u32[]{:S(2)}, u32[]{:S(2)}) collective-permute-start(bf16[656,128]{1,0:T(8,128)(2,1)} %get-tuple-element.28), channel_id=1, source_target_pairs={{0,4},{1,5},{2,6},{3,7},{4,0},{5,1},{6,2},{7,3},{8,12},{9,13},{10,... | collective-permute-start | bytes 503816 | tf_op jit(solution)/shard_map/ppermute | solution.py:934
  11.8 18.2 %collective-permute-start.4 = (bf16[656,128]{1,0:T(8,128)(2,1)}, bf16[656,128]{1,0:T(8,128)(2,1)S(1)}, u32[]{:S(2)}, u32[]{:S(2)}) collective-permute-start(bf16[656,128]{1,0:T(8,128)(2,1)} %get-tuple-element.29), channel_id=1, source_target_pairs={{0,5},{1,6},{2,7},{3,0},{4,1},{5,2},{6,3},{7,4},{8,13},{9,14},{10,... | collective-permute-start | bytes 503816 | tf_op jit(solution)/shard_map/ppermute | solution.py:934
  14.6 10.2 %copy-start.13 = (bf16[656,128]{1,0:T(8,128)(2,1)}, bf16[656,128]{1,0:T(8,128)(2,1)S(1)}, u32[]{:S(2)}) copy-start(bf16[656,128]{1,0:T(8,128)(2,1)S(1)} %collective-permute-done.refs_1_.refs_6_) | copy-start | bytes 503812
  14.6 15.4 %collective-permute-start.5 = (bf16[656,128]{1,0:T(8,128)(2,1)}, bf16[656,128]{1,0:T(8,128)(2,1)S(1)}, u32[]{:S(2)}, u32[]{:S(2)}) collective-permute-start(bf16[656,128]{1,0:T(8,128)(2,1)} %get-tuple-element.30), channel_id=1, source_target_pairs={{0,6},{1,7},{2,0},{3,1},{4,2},{5,3},{6,4},{7,5},{8,14},{9,15},{10,... | collective-permute-start | bytes 503816 | tf_op jit(solution)/shard_map/ppermute | solution.py:934
  15.6 9.2 %copy-start.14 = (bf16[656,128]{1,0:T(8,128)(2,1)}, bf16[656,128]{1,0:T(8,128)(2,1)S(1)}, u32[]{:S(2)}) copy-start(bf16[656,128]{1,0:T(8,128)(2,1)S(1)} %collective-permute-done.1.refs_2_.refs_7_) | copy-start | bytes 503812
  15.6 14.3 %collective-permute-start.6 = (bf16[656,128]{1,0:T(8,128)(2,1)}, bf16[656,128]{1,0:T(8,128)(2,1)S(1)}, u32[]{:S(2)}, u32[]{:S(2)}) collective-permute-start(bf16[656,128]{1,0:T(8,128)(2,1)} %get-tuple-element.31), channel_id=1, source_target_pairs={{0,7},{1,0},{2,1},{3,2},{4,3},{5,4},{6,5},{7,6},{8,15},{9,8},{10,9... | collective-permute-start | bytes 503816 | tf_op jit(solution)/shard_map/ppermute | solution.py:934
  29.7 0.7 copy-start.15
  30.0 0.7 copy-start.16
  30.0 0.7 copy-start.17
  30.0 0.8 copy-start.18
  30.0 0.8 copy-start.19
  35.7 35.6 %collective-permute-start.7 = (bf16[18,2,32,128]{3,2,1,0:T(8,128)(2,1)}, bf16[18,2,32,128]{3,2,1,0:T(8,128)(2,1)S(1)}, u32[]{:S(2)}, u32[]{:S(2)}) collective-permute-start(bf16[18,2,32,128]{3,2,1,0:T(8,128)(2,1)} %get-tuple-element.36), channel_id=1, source_target_pairs={{0,1},{1,2},{2,3},{3,4},{4,5},{5,6},{6,7},{7,0},{8,9},{9,10},{10,1... | collective-permute-start | bytes 884744 | tf_op jit(solution)/shard_map/ppermute | solution.py:934
  40.5 30.9 %collective-permute-start.8 = (bf16[18,2,32,128]{3,2,1,0:T(8,128)(2,1)}, bf16[18,2,32,128]{3,2,1,0:T(8,128)(2,1)S(1)}, u32[]{:S(2)}, u32[]{:S(2)}) collective-permute-start(bf16[18,2,32,128]{3,2,1,0:T(8,128)(2,1)} %get-tuple-element.37), channel_id=1, source_target_pairs={{0,7},{1,0},{2,1},{3,2},{4,3},{5,4},{6,5},{7,6},{8,15},{9,8},{10,9... | collective-permute-start | bytes 884744 | tf_op jit(solution)/shard_map/ppermute | solution.py:934
  47.5 28.1 %collective-permute-start.13 = (bf16[6,176,128]{2,1,0:T(8,128)(2,1)}, bf16[6,176,128]{2,1,0:T(8,128)(2,1)S(1)}, u32[]{:S(2)}, u32[]{:S(2)}) collective-permute-start(bf16[6,176,128]{2,1,0:T(8,128)(2,1)} %get-tuple-element.39.refs_13_.refs_2_), channel_id=1, source_target_pairs={{0,6},{1,7},{2,0},{3,1},{4,2},{5,3},{6,4},{7,5},{8,14},{9,15},{10,... | collective-permute-start | bytes 811016 | tf_op jit(solution)/shard_map/ppermute | solution.py:934
  47.7 31.1 %collective-permute-start.12 = (bf16[6,176,128]{2,1,0:T(8,128)(2,1)}, bf16[6,176,128]{2,1,0:T(8,128)(2,1)S(1)}, u32[]{:S(2)}, u32[]{:S(2)}) collective-permute-start(bf16[6,176,128]{2,1,0:T(8,128)(2,1)} %get-tuple-element.39.refs_13_.refs_2_), channel_id=1, source_target_pairs={{0,4},{1,5},{2,6},{3,7},{4,0},{5,1},{6,2},{7,3},{8,12},{9,13},{10,... | collective-permute-start | bytes 811016 | tf_op jit(solution)/shard_map/ppermute | solution.py:934
  49.0 29.8 %collective-permute-start.11 = (bf16[6,176,128]{2,1,0:T(8,128)(2,1)}, bf16[6,176,128]{2,1,0:T(8,128)(2,1)S(1)}, u32[]{:S(2)}, u32[]{:S(2)}) collective-permute-start(bf16[6,176,128]{2,1,0:T(8,128)(2,1)} %get-tuple-element.39.refs_13_.refs_2_), channel_id=1, source_target_pairs={{0,2},{1,3},{2,4},{3,5},{4,6},{5,7},{6,0},{7,1},{8,10},{9,11},{10,... | collective-permute-start | bytes 811016 | tf_op jit(solution)/shard_map/ppermute | solution.py:934
  50.2 21.2 %copy-start = (f32[6,32,2,16,128]{4,3,2,1,0:T(8,128)S(1)}, f32[6,32,2,16,128]{4,3,2,1,0:T(8,128)}, u32[]{:S(2)}) copy-start(f32[6,32,2,16,128]{4,3,2,1,0:T(8,128)} %get-tuple-element.35.refs_0_) | copy-start | bytes 9437188
  71.3 9.6 %copy-start.1 = (bf16[6,176,128]{2,1,0:T(8,128)(2,1)S(1)}, bf16[6,176,128]{2,1,0:T(8,128)(2,1)}, u32[]{:S(2)}) copy-start(bf16[6,176,128]{2,1,0:T(8,128)(2,1)} %get-tuple-element.39.refs_13_.refs_2_) | copy-start | bytes 811012
  71.3 9.6 %copy-start.10 = (s32[64,2]{0,1:T(2,128)S(1)}, s32[64,2]{0,1:T(2,128)}, u32[]{:S(2)}) copy-start(s32[64,2]{0,1:T(2,128)} %param.13) | copy-start | bytes 1540
  71.3 9.6 %copy-start.11 = (s32[64]{0:T(128)S(1)}, s32[64]{0:T(128)}, u32[]{:S(2)}) copy-start(s32[64]{0:T(128)} %get-tuple-element.38.refs_0_) | copy-start | bytes 772
  71.4 11.6 %copy-start.2 = (bf16[18,2,32,128]{3,2,1,0:T(8,128)(2,1)}, bf16[18,2,32,128]{3,2,1,0:T(8,128)(2,1)S(1)}, u32[]{:S(2)}) copy-start(bf16[18,2,32,128]{3,2,1,0:T(8,128)(2,1)S(1)} %collective-permute-done.7.refs_1_) | copy-start | bytes 884740
  71.4 11.6 %copy-start.3 = (bf16[18,2,32,128]{3,2,1,0:T(8,128)(2,1)}, bf16[18,2,32,128]{3,2,1,0:T(8,128)(2,1)S(1)}, u32[]{:S(2)}) copy-start(bf16[18,2,32,128]{3,2,1,0:T(8,128)(2,1)S(1)} %collective-permute-done.8.refs_2_) | copy-start | bytes 884740
  71.4 0.8 copy-start.12
  72.7 6.1 %collective-permute-start.9 = (bf16[864,128]{1,0:T(8,128)(2,1)S(1)}, bf16[864,128]{1,0:T(8,128)(2,1)S(1)}, u32[]{:S(2)}, u32[]{:S(2)}) collective-permute-start(bf16[864,128]{1,0:T(8,128)(2,1)S(1)} %get-tuple-element.41), channel_id=1, source_target_pairs={{0,8},{8,16},{16,24},{24,0},{1,9},{9,17},{17,25},{25,1},{2,10},{10... | collective-permute-start | bytes 663560 | tf_op jit(solution)/shard_map/ppermute | solution.py:934
  75.5 5.4 %collective-permute-start.10 = (bf16[864,128]{1,0:T(8,128)(2,1)S(1)}, bf16[864,128]{1,0:T(8,128)(2,1)S(1)}, u32[]{:S(2)}, u32[]{:S(2)}) collective-permute-start(bf16[864,128]{1,0:T(8,128)(2,1)S(1)} %get-tuple-element.42), channel_id=1, source_target_pairs={{0,24},{8,0},{16,8},{24,16},{1,25},{9,1},{17,9},{25,17},{2,26},{10... | collective-permute-start | bytes 663560 | tf_op jit(solution)/shard_map/ppermute | solution.py:934
  75.5 26.3 %copy-start.5 = (bf16[6,176,128]{2,1,0:T(8,128)(2,1)}, bf16[6,176,128]{2,1,0:T(8,128)(2,1)S(1)}, u32[]{:S(2)}) copy-start(bf16[6,176,128]{2,1,0:T(8,128)(2,1)S(1)} %collective-permute-done.13.refs_5_.refs_16_) | copy-start | bytes 811012
  78.8 23.0 %copy-start.6 = (bf16[6,176,128]{2,1,0:T(8,128)(2,1)}, bf16[6,176,128]{2,1,0:T(8,128)(2,1)S(1)}, u32[]{:S(2)}) copy-start(bf16[6,176,128]{2,1,0:T(8,128)(2,1)S(1)} %collective-permute-done.12.refs_4_.refs_15_) | copy-start | bytes 811012
  78.8 23.1 %copy-start.7 = (bf16[6,176,128]{2,1,0:T(8,128)(2,1)}, bf16[6,176,128]{2,1,0:T(8,128)(2,1)S(1)}, u32[]{:S(2)}) copy-start(bf16[6,176,128]{2,1,0:T(8,128)(2,1)S(1)} %collective-permute-done.11.refs_3_.refs_14_) | copy-start | bytes 811012
  78.8 4.2 %copy-start.8 = (bf16[864,128]{1,0:T(8,128)(2,1)}, bf16[864,128]{1,0:T(8,128)(2,1)S(1)}, u32[]{:S(2)}) copy-start(bf16[864,128]{1,0:T(8,128)(2,1)S(1)} %collective-permute-done.9.refs_6_.refs_3_) | copy-start | bytes 663556
  80.9 2.1 %copy-start.9 = (bf16[864,128]{1,0:T(8,128)(2,1)}, bf16[864,128]{1,0:T(8,128)(2,1)S(1)}, u32[]{:S(2)}) copy-start(bf16[864,128]{1,0:T(8,128)(2,1)S(1)} %collective-permute-done.10.refs_7_.refs_4_) | copy-start | bytes 663556
  82.4 0.7 copy-start.4
  82.4 19.5 %collective-permute-start.14 = (bf16[6,176,128]{2,1,0:T(8,128)(2,1)S(1)}, bf16[6,176,128]{2,1,0:T(8,128)(2,1)S(1)}, u32[]{:S(2)}, u32[]{:S(2)}) collective-permute-start(bf16[6,176,128]{2,1,0:T(8,128)(2,1)S(1)} %pack.1.refs_5_), channel_id=1, source_target_pairs={{0,1},{1,0},{2,3},{3,2},{4,5},{5,4},{6,7},{7,6},{8,9},{9,8},{10,11... | collective-permute-start | bytes 811016 | tf_op jit(solution)/shard_map/ppermute | solution.py:1079
  101.8 0.7 copy-start.20
